TPU v7x, 256 devices: a whole 4x4x8 slice. The times are simulated.
256 devices in a mesh: ctx: 64 (over y, z, core), head: 4 (over x).
Axes of the slice: x: 4, y: 4, z: 8, core: 2. Of those that a mesh axis runs over, the one named last changes fastest.
Arguments:
- tokens: bfloat16 [32768, 2560], P('ctx', 'head'), may hold values from -6 to 6
- dt_decay: bfloat16 [32768, 2, 80], P('ctx', None, 'head'), may hold values from -0.8 to 0.06, as said below
- dest: int32 [32768], P('ctx'), may hold values from 0 to 32767, as said below
- lengths: int32 [128], replicated, may hold values from 1 to 16384, 32768 in all
- w_x: bfloat16 [2560, 5120], P(None, 'head'), may hold values from -0.125 to 0.125
- w_bc: bfloat16 [2560, 256], replicated, may hold values from -0.125 to 0.125
- conv_x: float32 [4, 5120], P(None, 'head'), may hold values from -3 to 3
- conv_bc: float32 [4, 256], replicated, may hold values from -3 to 3
- bias_x: float32 [5120], P('head'), may hold values from -0.5 to 0.5
- bias_bc: float32 [256], replicated, may hold values from -0.5 to 0.5
- skip: float32 [80], P('head'), may hold values from 0.5 to 1.5
Outputs:
- ssm_output: bfloat16 [32768, 5120], P('ctx', 'head')
Inputs may be any that keep to these rules, and one draw needn't show every extreme that they name: dest is a permutation of the packed positions; loader row r lands on context shard dest[r] // 512. Of the 512 rows of one loader shard at most 16 land on one context shard, and exactly 16 land on one of them. Up to a relabelling of the context shards, every loader shard sends the same counts. The lengths sum to 32768; document d holds the positions from the sum of the first d lengths on. `dt_decay`: entry [r, 0, h] is a positive step size, entry [r, 1, h] a negative log decay.
All inputs are finite; a program needn't handle non-finite values.
Results may differ from a plain program's by a relative error of at most 0.0035.
Values may be sent and summed in bfloat16 or wider, within the bound.
No kernel may reach another device: no remote copies, remote signals or barrier semaphores. Data moves between devices by JAX's collectives and lax.ppermute only.
A program may use at most 128 MiB of HBM per device.

v0:
```python
import jax
import jax.numpy as jnp
from jax import lax
from jax.sharding import PartitionSpec as P

STRETCH = 256


def shifted_2(x, axis, by):
    devices = lax.axis_size(axis)
    pairs = [(i, i + by) for i in range(devices) if 0 <= i + by < devices]
    return lax.ppermute(x, axis, pairs)


def entering_2(value, axis, join, neutral):
    count, mine = (lax.axis_size(axis), lax.axis_index(axis))
    pieces = jax.tree.map(lambda part: lax.all_gather(part, axis), value)
    so_far = jax.tree.map(
        lambda part, zero: jnp.full_like(part, 0) + jnp.asarray(zero, part.dtype), value, neutral
    )

    def turn(position, so_far):
        longer = join(so_far, jax.tree.map(lambda part: part[position], pieces))
        return jax.tree.map(lambda new, old: jnp.where(position < mine, new, old), longer, so_far)

    return lax.fori_loop(0, count - 1, turn, so_far)


def causal_conv(extended, weight, bias, positions, doc_start):
    tap_count = weight.shape[0]
    row_count = positions.shape[0]
    running = jnp.zeros((row_count, extended.shape[1]), jnp.float32) + bias[None, :]
    for tap_index in range(tap_count):
        lag_rows = tap_count - 1 - tap_index
        shifted = extended[tap_index : tap_index + row_count]
        valid = (positions - lag_rows >= doc_start)[:, None]
        running = running + jnp.where(valid, weight[tap_index][None, :] * shifted, 0.0)
    return jax.nn.silu(running).astype(jnp.bfloat16)


def block_terms(inject, input_map, output_map, logarithm_decay, positions, doc_start):
    cumulative = jnp.cumsum(logarithm_decay, axis=0)
    first_pos = positions[0]
    scores = jnp.dot(output_map, input_map.T, preferred_element_type=jnp.float32)
    keep_mask = (positions[:, None] >= positions[None, :]) & (
        doc_start[:, None] <= positions[None, :]
    )
    log_gap = jnp.where(keep_mask[:, :, None], cumulative[:, None, :] - cumulative[None, :, :], 0.0)
    weights = jnp.where(keep_mask[:, :, None], scores[:, :, None] * jnp.exp(log_gap), 0.0).astype(
        jnp.bfloat16
    )
    inner_part = jnp.einsum("tsh,shp->thp", weights, inject, preferred_element_type=jnp.float32)
    tail_decay = jnp.where(
        (doc_start[-1] <= positions)[:, None], jnp.exp(cumulative[-1][None, :] - cumulative), 0.0
    )
    decayed = (inject * tail_decay[:, :, None]).astype(jnp.bfloat16)
    block_state = jnp.einsum("shp,sn->hpn", decayed, input_map, preferred_element_type=jnp.float32)
    carry_decay = jnp.where(doc_start[-1] < first_pos, jnp.exp(cumulative[-1]), 0.0)
    enter_decay = jnp.where((doc_start < first_pos)[:, None], jnp.exp(cumulative), 0.0)
    return (inner_part, enter_decay, block_state, carry_decay)


def combine(earlier, later):
    return (earlier[0] * later[0], later[0][:, None, None] * earlier[1] + later[1])


def on_device(tokens, dt_decay, dest, lengths, w_x, w_bc, conv_x, conv_bc, bias_x, bias_bc, skip):
    row_count = tokens.shape[0]
    groups = lax.axis_size("ctx")
    capacity = 2 * row_count // groups
    head_count = dt_decay.shape[2]
    head_dim = w_x.shape[1] // head_count
    state_width = w_bc.shape[1] // 2
    first_pos = lax.axis_index("ctx") * row_count
    target = dest // row_count
    local_row = dest % row_count
    onehot = (target[:, None] == jnp.arange(groups, dtype=jnp.int32)[None, :]).astype(jnp.int32)
    slot_rank = jnp.sum((jnp.cumsum(onehot, axis=0) - onehot) * onehot, axis=1)
    slot_pos = (
        jnp.full((groups, capacity), row_count, jnp.int32).at[target, slot_rank].set(local_row)
    )
    arrived = lax.all_to_all(slot_pos, "ctx", split_axis=0, concat_axis=0, tiled=True)
    flat_pos = arrived.reshape(groups * capacity)
    flat_slot = target * capacity + slot_rank
    send_select = (
        jnp.arange(groups * capacity, dtype=jnp.int32)[:, None] == flat_slot[None, :]
    ).astype(jnp.bfloat16)
    take_select = (jnp.arange(row_count, dtype=jnp.int32)[:, None] == flat_pos[None, :]).astype(
        jnp.bfloat16
    )

    def into_slots(payload):
        placed = jnp.dot(send_select, payload, preferred_element_type=jnp.float32).astype(
            payload.dtype
        )
        return placed.reshape(groups, capacity, payload.shape[1])

    def from_slots(payload):
        flat_rows = payload.reshape(groups * capacity, payload.shape[2])
        return jnp.dot(take_select, flat_rows, preferred_element_type=jnp.float32).astype(
            flat_rows.dtype
        )

    step_rows = dt_decay.reshape(row_count, 2 * head_count)
    piece_rows = lax.all_gather(tokens, "head", axis=1, tiled=True)
    inner_proj = jnp.dot(piece_rows, w_x, preferred_element_type=jnp.float32)
    state_proj = jnp.dot(piece_rows, w_bc, preferred_element_type=jnp.float32)
    moved = (
        lax.all_to_all(
            into_slots(inner_proj.astype(jnp.bfloat16)),
            "ctx",
            split_axis=0,
            concat_axis=0,
            tiled=True,
        ),
        lax.all_to_all(
            into_slots(state_proj.astype(jnp.bfloat16)),
            "ctx",
            split_axis=0,
            concat_axis=0,
            tiled=True,
        ),
        lax.all_to_all(into_slots(step_rows), "ctx", split_axis=0, concat_axis=0, tiled=True),
    )
    inner_packed = from_slots(moved[0])
    state_packed = from_slots(moved[1])
    step_packed = from_slots(moved[2])
    starts = jnp.cumsum(lengths) - lengths
    positions = first_pos + jnp.arange(row_count, dtype=jnp.int32)
    doc_start = jnp.max(
        jnp.where(starts[None, :] <= positions[:, None], starts[None, :], 0), axis=1
    )
    tap_count = conv_x.shape[0]
    rim_rows = shifted_2(
        (inner_packed[row_count - tap_count + 1 :], state_packed[row_count - tap_count + 1 :]),
        "ctx",
        1,
    )
    inner_conv = causal_conv(
        jnp.concatenate([rim_rows[0], inner_packed], axis=0), conv_x, bias_x, positions, doc_start
    )
    state_conv = causal_conv(
        jnp.concatenate([rim_rows[1], state_packed], axis=0), conv_bc, bias_bc, positions, doc_start
    )
    input_map = state_conv[:, :state_width]
    output_map = state_conv[:, state_width:]
    step_size = step_packed[:, :head_count].astype(jnp.float32)
    logarithm_decay = step_packed[:, head_count:].astype(jnp.float32)
    inner_heads = inner_conv.reshape(row_count, head_count, head_dim)
    inject = (inner_heads * step_size[:, :, None]).astype(jnp.bfloat16)
    block_rows = min(STRETCH, row_count)
    block_count = row_count // block_rows
    carried = jnp.zeros((head_count, head_dim, state_width), jnp.float32)
    reach_decay = jnp.ones((head_count,), jnp.float32)
    pieces = []
    for block_index in range(block_count):
        row_span = slice(block_index * block_rows, (block_index + 1) * block_rows)
        inner_part, enter_decay, block_state, carry_decay = block_terms(
            inject[row_span],
            input_map[row_span],
            output_map[row_span],
            logarithm_decay[row_span],
            positions[row_span],
            doc_start[row_span],
        )
        pieces.append((inner_part, enter_decay, carried, reach_decay))
        carried = carry_decay[:, None, None] * carried + block_state
        reach_decay = carry_decay * reach_decay
    incoming = entering_2(
        (reach_decay, carried),
        "ctx",
        combine,
        (jnp.ones_like(reach_decay), jnp.zeros_like(carried)),
    )[1]
    outputs = []
    for block_index in range(block_count):
        row_span = slice(block_index * block_rows, (block_index + 1) * block_rows)
        inner_part, enter_decay, local_state, local_reach = pieces[block_index]
        entering = local_state + local_reach[:, None, None] * incoming
        outer_part = (
            jnp.einsum(
                "tn,hpn->thp",
                output_map[row_span].astype(jnp.float32),
                entering,
                precision=lax.Precision.HIGHEST,
            )
            * enter_decay[:, :, None]
        )
        mixed_rows = inner_part + outer_part + skip[None, :, None] * inner_heads[row_span]
        outputs.append(mixed_rows.astype(jnp.bfloat16).reshape(block_rows, head_count * head_dim))
    return jnp.concatenate(outputs, axis=0)


def solution(mesh):
    in_specs = (
        P("ctx", "head"),
        P("ctx", None, "head"),
        P("ctx"),
        P(),
        P(None, "head"),
        P(),
        P(None, "head"),
        P(),
        P("head"),
        P(),
        P("head"),
    )
    out_specs = P("ctx", "head")
    return jax.shard_map(
        on_device, mesh=mesh, in_specs=in_specs, out_specs=out_specs, check_vma=False
    )
```

profile of v0, /device:TPU:1, one launch (start us, length us, event | category | flops | bytes accessed | tf_op | source)
XLA Modules:
  0.0 484.5 jit_solution(4322245013430130874)
XLA Ops:
  9.6 25.2 %scatter_fusion = s32[64,16]{0,1:T(8,128)S(1)} fusion(s32[64,16]{0,1:T(8,128)S(1)} %broadcast_in_dim.192, s32[512]{0:T(512)S(1)} %bitcast.103, s32[512]{0:T(512)S(1)} %get-tuple-element.169), kind=kCustom, calls=%fused_computation | custom fusion | bytes 10240 | tf_op jit(solution)/shard_map/scatter | solution.py:80
  35.5 13.2 %all-to-all-start = ((s32[64,1,16]{2,1,0:T(1,128)}), s32[64,1,16]{2,1,0:T(1,128)S(1)}, u32[]{:S(2)}, u32[]{:S(2)}) async-start(s32[64,1,16]{2,1,0:T(1,128)} %copy.72), calls=%async_computation | async-start | bytes 65536 | tf_op jit(solution)/shard_map/all_to_all | solution.py:82
  50.4 7.4 %all-to-all-done = s32[64,1,16]{2,1,0:T(1,128)S(1)} async-done(((s32[64,1,16]{2,1,0:T(1,128)}), s32[64,1,16]{2,1,0:T(1,128)S(1)}, u32[]{:S(2)}, u32[]{:S(2)}) %all-to-all-start) | async-done | bytes 4128 | tf_op jit(solution)/shard_map/all_to_all | solution.py:82
  57.9 4.7 all-to-all-start.2
  62.6 4.2 fusion.27
  66.9 6.0 %all-to-all-done.2 = bf16[64,2,320]{2,1,0:T(2,128)(2,1)S(1)} async-done(((bf16[64,2,320]{2,1,0:T(2,128)(2,1)}), bf16[64,2,320]{2,1,0:T(2,128)(2,1)S(1)}, u32[]{:S(2)}, u32[]{:S(2)}) %all-to-all-start.2) | async-done | bytes 81952 | tf_op jit(solution)/shard_map/all_to_all | solution.py:123
  72.9 4.5 all-to-all-start.3
  77.4 10.1 %convolution_convert_fusion = bf16[1024,1280]{1,0:T(8,128)(2,1)} fusion(s32[512]{0:T(512)S(1)} %multiply_add_fusion, bf16[512,2560]{1,0:T(8,128)(2,1)} %all-gather.5.cloned.1.call-done, bf16[2560,1280]{1,0:T(8,128)(2,1)} %param.17), kind=kOutput, calls=%fused_computation.6 | convolution fusion | flops 4700110848 | bytes 11798528 | tf_op jit(solution)/shard_map/dot_general | solution.py:93
  87.5 7.3 %all-to-all-done.3 = bf16[64,16,256]{2,1,0:T(8,128)(2,1)S(1)} async-done(((bf16[64,16,256]{2,1,0:T(8,128)(2,1)}), bf16[64,16,256]{2,1,0:T(8,128)(2,1)S(1)}, u32[]{:S(2)}, u32[]{:S(2)}) %all-to-all-start.3) | async-done | bytes 524320 | tf_op jit(solution)/shard_map/all_to_all | solution.py:116
  94.7 6.7 %all-to-all-start.1 = ((bf16[64,16,1280]{2,1,0:T(8,128)(2,1)}), bf16[64,16,1280]{2,1,0:T(8,128)(2,1)}, u32[]{:S(2)}, u32[]{:S(2)}) async-start(bf16[64,16,1280]{2,1,0:T(8,128)(2,1)} %bitcast.109), calls=%async_computation.1 | async-start | bytes 5242880 | tf_op jit(solution)/shard_map/all_to_all | solution.py:109
  106.2 2.6 broadcast_compare_fusion.2
  114.9 3.5 collective-permute-start.1
  118.4 45.2 %all-to-all-done.1 = bf16[64,16,1280]{2,1,0:T(8,128)(2,1)} async-done(((bf16[64,16,1280]{2,1,0:T(8,128)(2,1)}), bf16[64,16,1280]{2,1,0:T(8,128)(2,1)}, u32[]{:S(2)}, u32[]{:S(2)}) %all-to-all-start.1) | async-done | bytes 2621472 | tf_op jit(solution)/shard_map/all_to_all | solution.py:109
  163.6 3.3 convolution_convert_fusion.2
  170.1 3.7 multiply_convert_fusion.1
  181.2 43.3 %all-gather.1 = f32[64,1,20]{2,1,0:T(1,128)} all-gather(f32[1,1,20]{2,1,0:T(1,128)S(1)} %bitcast.130), channel_id=1, replica_groups=mesh['ctx'=64,'head'=4] {'ctx'}, dimensions={0}, use_global_device_ids=true | all-gather | bytes 5200 | tf_op jit(solution)/shard_map/all_gather | solution.py:17
  229.7 3.8 fusion.18
  233.6 2.5 fusion.17
  236.1 108.0 %all-gather.7.cloned.1.call-done = f32[1280,64,128]{2,1,0:T(8,128)} async-done(((f32[20,64,128]{2,1,0:T(8,128)}), f32[1280,64,128]{2,1,0:T(8,128)}) %all-gather.7.cloned.1.call-update) | async-done | bytes 41943056 | tf_op jit(solution)/shard_map/all_gather | solution.py:17
  344.1 121.8 %while.14 = (s32[]{:T(128)}, f32[20,64,128]{2,1,0:T(8,128)S(1)}, s32[]{:T(128)}, f32[64,20]{1,0:T(8,128)}, f32[64,20,64,128]{3,2,1,0:T(8,128)}, /*index=5*/s32[]{:T(128)}, s32[]{:T(128)}) while((s32[]{:T(128)}, f32[20,64,128]{2,1,0:T(8,128)S(1)}, s32[]{:T(128)}, f32[64,20]{1,0:T(8,128)}, f32[64,20,64,128]{3,2,1,0:T(8,128)}, ...), condition=%wide.region_11.12_spmd.clone, body=%wide.region_10.11_spmd.clone.sunk | while | flops 655364 | bytes 1966425 | solution.py:26
  465.9 2.9 fusion.24
  468.7 2.2 copy.82
  470.9 3.2 fusion.23
  475.4 2.2 pad_maximum_fusion.1
  (245 shorter events, 151.1 us)
Async XLA Ops:
  6.5 56.1 %copy-start = (bf16[2560,256]{1,0:T(8,128)(2,1)S(1)}, bf16[2560,256]{1,0:T(8,128)(2,1)}, u32[]{:S(2)}) copy-start(bf16[2560,256]{1,0:T(8,128)(2,1)} %param.18) | copy-start | bytes 3932164
  6.5 56.1 %all-gather.5.cloned.1.call-start = ((), (), s32[]{:S(2)}) async-start(), calls=%async_computation.4 | async-start | bytes 3276800 | tf_op jit(solution)/shard_map/all_gather | solution.py:105
  8.0 40.7 %copy-start.10 = (bf16[512,2,20]{0,1,2:T(2,128)(2,1)S(1)}, bf16[512,2,20]{0,1,2:T(2,128)(2,1)}, u32[]{:S(2)}) copy-start(bf16[512,2,20]{0,1,2:T(2,128)(2,1)} %param.14) | copy-start | bytes 122884
  35.5 22.4 %all-to-all-start = ((s32[64,1,16]{2,1,0:T(1,128)}), s32[64,1,16]{2,1,0:T(1,128)S(1)}, u32[]{:S(2)}, u32[]{:S(2)}) async-start(s32[64,1,16]{2,1,0:T(1,128)} %copy.72), calls=%async_computation | async-start | bytes 65536 | tf_op jit(solution)/shard_map/all_to_all | solution.py:82
  57.9 15.0 %all-to-all-start.2 = ((bf16[64,2,320]{2,1,0:T(2,128)(2,1)}), bf16[64,2,320]{2,1,0:T(2,128)(2,1)S(1)}, u32[]{:S(2)}, u32[]{:S(2)}) async-start(bf16[64,2,320]{2,1,0:T(2,128)(2,1)} %reshape.333), calls=%async_computation.2 | async-start | bytes 196608 | tf_op jit(solution)/shard_map/all_to_all | solution.py:123
  72.9 21.8 %all-to-all-start.3 = ((bf16[64,16,256]{2,1,0:T(8,128)(2,1)}), bf16[64,16,256]{2,1,0:T(8,128)(2,1)S(1)}, u32[]{:S(2)}, u32[]{:S(2)}) async-start(bf16[64,16,256]{2,1,0:T(8,128)(2,1)} %bitcast.13), calls=%async_computation.3 | async-start | bytes 1048576 | tf_op jit(solution)/shard_map/all_to_all | solution.py:116
  94.7 6.9 %copy-start.16 = (s32[128]{0:T(128)S(1)}, s32[128]{0:T(128)}, u32[]{:S(2)}) copy-start(s32[128]{0:T(128)} %param.16) | copy-start | bytes 1540
  94.7 11.4 %copy-start.11 = (f32[4,1280]{1,0:T(4,128)S(1)}, f32[4,1280]{1,0:T(4,128)}, u32[]{:S(2)}) copy-start(f32[4,1280]{1,0:T(4,128)} %param.19) | copy-start | bytes 61444
  94.7 14.1 %copy-start.13 = (f32[4,256]{1,0:T(4,128)S(1)}, f32[4,256]{1,0:T(4,128)}, u32[]{:S(2)}) copy-start(f32[4,256]{1,0:T(4,128)} %param.20) | copy-start | bytes 12292
  94.7 68.9 %all-to-all-start.1 = ((bf16[64,16,1280]{2,1,0:T(8,128)(2,1)}), bf16[64,16,1280]{2,1,0:T(8,128)(2,1)}, u32[]{:S(2)}, u32[]{:S(2)}) async-start(bf16[64,16,1280]{2,1,0:T(8,128)(2,1)} %bitcast.109), calls=%async_computation.1 | async-start | bytes 5242880 | tf_op jit(solution)/shard_map/all_to_all | solution.py:109
  101.4 242.7 %all-gather.7.cloned.1.call-start = ((), (), s32[]{:S(2)}) async-start(), calls=%async_computation.5 | async-start | bytes 42598400 | tf_op jit(solution)/shard_map/all_gather | solution.py:17
  111.9 2.5 copy-start.6
  112.9 1.5 copy-start.7
  114.9 54.1 %collective-permute-start.1 = (bf16[3,256]{1,0:T(4,128)(2,1)S(1)}, bf16[3,256]{1,0:T(4,128)(2,1)S(1)}, u32[]{:S(2)}, u32[]{:S(2)}) collective-permute-start(bf16[3,256]{1,0:T(4,128)(2,1)S(1)} %slice.204), channel_id=1, source_target_pairs={{0,4},{4,8},{8,12},{12,16},{16,20},{20,24},{24,28},{28,32},{32,36}... | collective-permute-start | bytes 4616 | tf_op jit(solution)/shard_map/ppermute | solution.py:12
  163.6 5.4 %copy-start.15 = (f32[256]{0:T(256)S(1)}, f32[256]{0:T(256)}, u32[]{:S(2)}) copy-start(f32[256]{0:T(256)} %param.22) | copy-start | bytes 3076
  163.6 6.4 %copy-start.12 = (f32[1280]{0:T(1024)S(1)}, f32[1280]{0:T(1024)}, u32[]{:S(2)}) copy-start(f32[1280]{0:T(1024)} %param.21) | copy-start | bytes 15364
  167.0 3.1 collective-permute-start
  177.8 1.1 copy-start.2
  229.7 3.9 copy-start.3
  229.7 3.9 copy-start.5
  229.7 3.9 copy-start.8
  229.7 3.9 copy-start.9
  344.1 121.8 %copy-start.14 = (f32[20]{0:T(128)S(1)}, f32[20]{0:T(128)}, u32[]{:S(2)}) copy-start(f32[20]{0:T(128)} %param.23) | copy-start | bytes 244
  470.9 6.7 %copy-start.1 = (bf16[2560,256]{1,0:T(8,128)(2,1)S(1)}, bf16[2560,256]{1,0:T(8,128)(2,1)}, u32[]{:S(2)}) copy-start(bf16[2560,256]{1,0:T(8,128)(2,1)} %param.18) | copy-start | bytes 3932164
  (1 other events, 0.9 us)
Sparse Core Ops, SparseCore 0:
  9.2 41.5 all-gather.4
  180.5 163.5 all-gather.6
where the time goes:
time: 490 us; the launch traced here: 484 us
  waiting for transfers between devices  175 us (36%)
  other arithmetic  97.2 us (20%)
  local copies, waits for them, and re-layouts  81.8 us (17%)
  blocking collectives  43.3 us (9%)
  matrix products  34.8 us (7%)
  starting transfers between devices  34.7 us (7%)
  between operations  16.6 us (3%)
    all_gather x1, waiting for transfers between devices, entering_2(): pieces = jax.tree.map(lambda part: lax.all_gather(part, axis), value)  108 us
    select_n x63, other arithmetic, turn(): jnp.where(position < mine, new, old)  77.4 us
    all_to_all x1, waiting for transfers between devices, on_device(): lax.all_to_all(into_slots(inner_proj.astype(jnp.bfloat16)), 'ctx', split_...  45.2 us
    all_gather x1, blocking collectives, entering_2(): pieces = jax.tree.map(lambda part: lax.all_gather(part, axis), value)  43.3 us
    mul x63, local copies, waits for them, and re-layouts, combine(): later[0][:, None, None] * earlier[1] + later[1]  43.3 us
    scatter x1, local copies, waits for them, and re-layouts, on_device(): jnp.full((groups, capacity), row_count, jnp.int32).at[target, slot_rank]  25.2 us
    dot_general x3, matrix products, into_slots(): jnp.dot(send_select, payload, preferred_element_type=jnp.float32)  14.8 us
    all_to_all x1, starting transfers between devices, on_device(): lax.all_to_all(slot_pos, 'ctx', split_axis=0, concat_axis=0, tiled=True)  13.2 us
  transfers between devices with their start and end apart: 8, of which 6 were waited for; matrix products, arithmetic and copies ran while one was open for 15% of the time, Pallas kernels for 0%

commit v1 on v0

v1 whole, which is shorter than its diff:
```python
import functools

import jax
import jax.numpy as jnp
from jax import lax
from jax.experimental import pallas as pl
from jax.experimental.pallas import tpu as pltpu
from jax.sharding import PartitionSpec as P

BF = jnp.bfloat16
F32 = jnp.float32
CAP = 16
BLK = 256
HD = 64
TILE = 256
HALO = 16
VMEM_LIMIT = 48 * 1024 * 1024


def iota(shape, dim):
    return lax.broadcasted_iota(jnp.int32, shape, dim)


def mm(a, b):
    return jnp.dot(a, b, preferred_element_type=F32)


def mm_nt(a, b):
    return lax.dot_general(a, b, (((1,), (1,)), ((), ())), preferred_element_type=F32)


def mm_tn(a, b):
    return lax.dot_general(a, b, (((0,), (0,)), ((), ())), preferred_element_type=F32)


def as_bf(mask):
    return jnp.where(mask, 1.0, 0.0).astype(BF)


def lower_ones(n):
    return as_bf(iota((n, n), 0) >= iota((n, n), 1))


def params(flops=0, bytes_accessed=0):
    return dict(
        compiler_params=pltpu.CompilerParams(vmem_limit_bytes=VMEM_LIMIT),
        cost_estimate=pl.CostEstimate(
            flops=flops, bytes_accessed=bytes_accessed, transcendentals=0
        ),
    )


def pack_kernel(dest_ref, tok_ref, small_ref, out_ref, slot_ref):
    step = pl.program_id(0)
    rows = tok_ref.shape[0]
    groups = 64
    slots = out_ref.shape[0]

    @pl.when(step == 0)
    def _():
        dest = dest_ref[...]
        target = dest // rows
        onehot = iota((groups, rows), 0) == target
        upper = as_bf(iota((rows, rows), 0) <= iota((rows, rows), 1))
        ranks = mm(as_bf(onehot), upper)
        rank = jnp.sum(jnp.where(onehot, ranks, 0.0), axis=0, keepdims=True) - 1.0
        slot_ref[...] = target * CAP + rank.astype(jnp.int32)

    select = as_bf(iota((slots, rows), 0) + step * slots == slot_ref[...])
    width = tok_ref.shape[1]
    out_ref[:, :width] = mm(select, tok_ref[...]).astype(BF)
    out_ref[:, width:] = mm(select, small_ref[...]).astype(BF)


def pack(dest, tokens, small, groups):
    rows, width = tokens.shape
    steps = 8
    slots = groups * CAP // steps
    full = width + small.shape[1]
    return pl.pallas_call(
        pack_kernel,
        grid=(steps,),
        in_specs=[
            pl.BlockSpec((1, rows), lambda i: (0, 0)),
            pl.BlockSpec((rows, width), lambda i: (0, 0)),
            pl.BlockSpec((rows, small.shape[1]), lambda i: (0, 0)),
        ],
        out_specs=pl.BlockSpec((slots, full), lambda i: (i, 0)),
        out_shape=jax.ShapeDtypeStruct((groups * CAP, full), BF),
        scratch_shapes=[pltpu.VMEM((1, rows), jnp.int32)],
        name="pack",
        **params(2 * rows * groups * CAP * full, 4 * rows * full),
    )(dest, tokens, small)


def unpack_kernel(width, heads, recv_ref, tok_ref, small_ref, pos_ref):
    step = pl.program_id(0)
    rows = tok_ref.shape[0]
    slots = recv_ref.shape[0]

    @pl.when(step == 0)
    def _():
        lane = iota((8, 128), 1)
        pick = jnp.where(
            lane == 2 * heads, 256.0, jnp.where(lane == 2 * heads + 1, 1.0, 0.0)
        ).astype(BF)
        pos_ref[...] = mm_nt(pick, recv_ref[:, width:])[0:1].astype(jnp.int32)

    select = as_bf(iota((rows, slots), 0) + (step * rows + 1) == pos_ref[...])
    tok_ref[...] = mm(select, recv_ref[:, :width]).astype(BF)
    small_ref[...] = mm(select, recv_ref[:, width:]).astype(BF)


def unpack(recv, width, heads, rows):
    slots, full = recv.shape
    steps = 4
    return pl.pallas_call(
        functools.partial(unpack_kernel, width, heads),
        grid=(steps,),
        in_specs=[pl.BlockSpec((slots, full), lambda i: (0, 0))],
        out_specs=[
            pl.BlockSpec((rows // steps, width), lambda i: (i, 0)),
            pl.BlockSpec((rows // steps, full - width), lambda i: (i, 0)),
        ],
        out_shape=[
            jax.ShapeDtypeStruct((rows, width), BF),
            jax.ShapeDtypeStruct((rows, full - width), BF),
        ],
        scratch_shapes=[pltpu.VMEM((1, slots), jnp.int32)],
        name="unpack",
        **params(2 * rows * slots * full, 6 * rows * full),
    )(recv)


def conv_silu(ext, weight, bias, rel, rows):
    total = jnp.zeros((rows, ext.shape[1]), F32) + bias
    taps = weight.shape[0]
    for tap in range(taps):
        lag = taps - 1 - tap
        shifted = ext[HALO - lag : HALO - lag + rows]
        total = total + jnp.where(rel >= lag, weight[tap : tap + 1] * shifted, 0.0)
    return jax.nn.silu(total).astype(BF)


def head_spread(tile, first):
    per = TILE // HD
    return as_bf(iota((128, TILE), 0) == first + per * tile + iota((128, TILE), 1) // HD)


def front_kernel(heads, me_ref, *refs):
    xs, hs, ws, wbs = refs[0:4], refs[4:8], refs[8:12], refs[12:16]
    small_ref, rel_ref, cx_ref, bx_ref, cb_ref, bb_ref = refs[16:22]
    conv_ref, state_ref, mid_ref, in_ref, outmap_ref = refs[22:27]
    xe_ref = refs[27]
    tile = pl.program_id(0)
    rows = xs[0].shape[0]
    rel = rel_ref[...]
    states = in_ref.shape[1]

    def project(weights):
        total = mm(xe_ref[0], weights[0][0])
        for piece in range(1, 4):
            total = total + mm(xe_ref[piece], weights[piece][0])
        return total.astype(BF).astype(F32)

    @pl.when(tile == 0)
    def _():
        for piece in range(4):
            xe_ref[piece, :HALO] = hs[piece][...]
            xe_ref[piece, HALO:] = xs[piece][...]
        both = conv_silu(project(wbs), cb_ref[...], bb_ref[...], rel, rows)
        in_ref[...] = both[:, :states]
        outmap_ref[...] = both[:, states:]
        sums = []
        for block in range(rows // BLK):
            part = small_ref[block * BLK : (block + 1) * BLK]
            last = rel[(block + 1) * BLK - 1 : (block + 1) * BLK]
            total = mm(jnp.ones((8, BLK), BF), part)[0:1]
            sums.append(jnp.where(last > BLK - 1, jnp.exp(total), 0.0))
        reach = sums[0]
        for more in sums[1:]:
            reach = reach * more
        high = reach.astype(BF).astype(F32)
        low = reach - high
        even = iota((128, 128), 0) % 2 == 0
        lane = iota((128, 128), 1)
        keep = (lane >= heads) & (lane < 2 * heads)
        state_ref[:, heads * HD :] = jnp.where(keep, jnp.where(even, high, low), 0.0).astype(BF)

    inner = conv_silu(project(ws), cx_ref[...], bx_ref[...], rel, rows)
    conv_ref[...] = inner
    small = small_ref[...]
    steps = mm(small, head_spread(tile, 0))
    decays = mm(small, head_spread(tile, heads)).astype(BF)
    inject = (inner.astype(F32) * steps).astype(BF).astype(F32)
    ones = lower_ones(BLK)
    carried = None
    for block in range(rows // BLK):
        span = slice(block * BLK, (block + 1) * BLK)
        cumulative = mm(ones, decays[span])
        last = rel[(block + 1) * BLK - 1 : (block + 1) * BLK]
        end = cumulative[BLK - 1 : BLK]
        behind = BLK - 1 - iota((BLK, 1), 0)
        decayed = jnp.where(
            behind <= last, jnp.exp(end - cumulative) * inject[span], 0.0
        ).astype(BF)
        block_state = mm_tn(in_ref[span], decayed)
        carry = jnp.where(last > BLK - 1, jnp.exp(end), 0.0)
        if carried is None:
            carried = block_state
            mid_ref[...] = carried
        else:
            carried = carry * carried + block_state
    state_ref[:, pl.ds(pl.multiple_of(tile * TILE, TILE), TILE)] = carried.astype(BF)


def front(me, xs, hs, w_x, w_bc, small, rel, conv_x, bias_x, conv_bc, bias_bc):
    rows, width = xs[0].shape
    inner = w_x.shape[1]
    heads = inner // HD
    states = w_bc.shape[1] // 2
    tiles = inner // TILE
    w4 = w_x.reshape(4, width, inner)
    wb4 = w_bc.reshape(4, width, 2 * states)

    def whole(shape):
        return pl.BlockSpec(shape, lambda i, m: tuple(0 for _ in shape))

    in_specs = (
        [whole((rows, width))] * 4
        + [whole((HALO, width))] * 4
        + [
            pl.BlockSpec((1, width, TILE), lambda i, m, k=k: ((m[0] + 4 - k) % 4, 0, i))
            for k in range(4)
        ]
        + [
            pl.BlockSpec((1, width, 2 * states), lambda i, m, k=k: ((m[0] + 4 - k) % 4, 0, 0))
            for k in range(4)
        ]
        + [
            whole((rows, 128)),
            whole((rows, 1)),
            pl.BlockSpec((conv_x.shape[0], TILE), lambda i, m: (0, i)),
            pl.BlockSpec((1, TILE), lambda i, m: (0, i)),
            whole(conv_bc.shape),
            whole((1, 2 * states)),
        ]
    )
    out_specs = [
        pl.BlockSpec((rows, TILE), lambda i, m: (0, i)),
        whole((states, inner + 128)),
        pl.BlockSpec((states, TILE), lambda i, m: (0, i)),
        whole((rows, states)),
        whole((rows, states)),
    ]
    return pl.pallas_call(
        functools.partial(front_kernel, heads),
        grid_spec=pltpu.PrefetchScalarGridSpec(
            num_scalar_prefetch=1,
            grid=(tiles,),
            in_specs=in_specs,
            out_specs=out_specs,
            scratch_shapes=[pltpu.VMEM((4, rows + HALO, width), BF)],
        ),
        out_shape=[
            jax.ShapeDtypeStruct((rows, inner), BF),
            jax.ShapeDtypeStruct((states, inner + 128), BF),
            jax.ShapeDtypeStruct((states, inner), F32),
            jax.ShapeDtypeStruct((rows, states), BF),
            jax.ShapeDtypeStruct((rows, states), BF),
        ],
        name="front",
        **params(2 * rows * 4 * width * (inner + 2 * states), 12_000_000),
    )(
        me, *xs, *hs, w4, w4, w4, w4, wb4, wb4, wb4, wb4,
        small, rel, conv_x, bias_x, conv_bc, bias_bc,
    )


def inner_kernel(
    heads, small_ref, rel_ref, in_ref, outmap_ref, conv_ref, mid_ref, skip_ref,
    part_ref, scores_ref, across_ref,
):
    tile = pl.program_id(0)
    rows = conv_ref.shape[0]
    per = TILE // HD
    ones = lower_ones(BLK)

    @pl.when(tile == 0)
    def _():
        for block in range(rows // BLK):
            span = slice(block * BLK, (block + 1) * BLK)
            scores = mm_nt(outmap_ref[span], in_ref[span])
            gap = iota((BLK, BLK), 0) - iota((BLK, BLK), 1)
            keep = (gap >= 0) & (gap <= rel_ref[span])
            scores_ref[block] = jnp.where(keep, scores, 0.0)
            across_ref[block] = mm(ones, small_ref[span]).T

    small = small_ref[...]
    steps = mm(small, head_spread(tile, 0))
    decays = mm(small, head_spread(tile, heads)).astype(BF)
    conv = conv_ref[...].astype(F32)
    inject = (conv * steps).astype(BF)
    lane_head = iota((BLK, TILE), 1) // HD
    for block in range(rows // BLK):
        span = slice(block * BLK, (block + 1) * BLK)
        cumulative = mm(ones, decays[span])
        scores = scores_ref[block]
        total = skip_ref[...] * conv[span]
        if block > 0:
            enter = jnp.where(
                iota((BLK, 1), 0) < rel_ref[span], jnp.exp(cumulative), 0.0
            )
            total = total + enter * mm(outmap_ref[span], mid_ref[...].astype(BF))
        for q in range(per):
            down = cumulative[:, q * HD : q * HD + 1]
            across = across_ref[block, pl.ds(heads + per * tile + q, 1), :]
            weights = (scores * jnp.exp(jnp.minimum(down - across, 0.0))).astype(BF)
            mine = jnp.where(lane_head == q, inject[span], jnp.zeros((), BF))
            total = total + mm(weights, mine)
        part_ref[span] = total


def inner_part(small, rel, input_map, output_map, conv, mid, skip_wide):
    rows, inner = conv.shape
    states = input_map.shape[1]
    heads = inner // HD
    blocks = rows // BLK

    def whole(shape):
        return pl.BlockSpec(shape, lambda i: tuple(0 for _ in shape))

    return pl.pallas_call(
        functools.partial(inner_kernel, heads),
        grid=(inner // TILE,),
        in_specs=[
            whole((rows, 128)),
            whole((rows, 1)),
            whole((rows, states)),
            whole((rows, states)),
            pl.BlockSpec((rows, TILE), lambda i: (0, i)),
            pl.BlockSpec((states, TILE), lambda i: (0, i)),
            pl.BlockSpec((1, TILE), lambda i: (0, i)),
        ],
        out_specs=pl.BlockSpec((rows, TILE), lambda i: (0, i)),
        out_shape=jax.ShapeDtypeStruct((rows, inner), F32),
        scratch_shapes=[
            pltpu.VMEM((blocks, BLK, BLK), F32),
            pltpu.VMEM((blocks, 128, BLK), F32),
        ],
        name="inner_part",
        **params(8 * rows * BLK * inner, 8_000_000),
    )(small, rel, input_map, output_map, conv, mid, skip_wide)


def scan_kernel(heads, recv_ref, out_ref, gain_ref, add_ref, enter_ref):
    count, inner = out_ref.shape
    codes = recv_ref[:, inner:]
    spread = as_bf(iota((128, inner), 0) == heads + iota((128, inner), 1) // HD)
    row, column = iota((count, count), 0), iota((count, count), 1)
    first = row // 2 * 2
    high = mm(as_bf(column == first), codes).astype(BF)
    low = mm(as_bf(column == first + 1), codes).astype(BF)
    gain_ref[...] = mm(high, spread) + mm(low, spread)
    add_ref[...] = recv_ref[:, :inner].astype(F32)

    def body(group, state):
        rows = pl.ds(pl.multiple_of(group * 8, 8), 8)
        gains, adds = gain_ref[rows], add_ref[rows]
        entered = []
        for pair in range(4):
            span = slice(2 * pair, 2 * pair + 2)
            entered.append(state)
            state = gains[span] * state + adds[span]
        enter_ref[rows] = jnp.concatenate(entered, axis=0)
        return state

    lax.fori_loop(0, count // 8, body, jnp.zeros((2, inner), F32))
    out_ref[...] = enter_ref[...].astype(BF)


def scan_shards(recv, heads):
    count, full = recv.shape
    inner = heads * HD
    return pl.pallas_call(
        functools.partial(scan_kernel, heads),
        out_shape=jax.ShapeDtypeStruct((count, inner), BF),
        scratch_shapes=[pltpu.VMEM((count, inner), F32)] * 3,
        name="scan_shards",
        **params(4 * count * 128 * inner, 700_000),
    )(recv)


def final_kernel(heads, small_ref, rel_ref, outmap_ref, part_ref, enter_ref, out_ref):
    tile = pl.program_id(0)
    rows = part_ref.shape[0]
    decays = mm(small_ref[...], head_spread(tile, heads)).astype(BF)
    cumulative = mm(lower_ones(rows), decays)
    gain = jnp.where(iota((rows, 1), 0) < rel_ref[...], jnp.exp(cumulative), 0.0)
    outer = mm(outmap_ref[...], enter_ref[...])
    out_ref[...] = (part_ref[...] + gain * outer).astype(BF)


def final(small, rel, output_map, part, enter):
    rows, inner = part.shape
    states = output_map.shape[1]

    def whole(shape):
        return pl.BlockSpec(shape, lambda i: tuple(0 for _ in shape))

    return pl.pallas_call(
        functools.partial(final_kernel, inner // HD),
        grid=(inner // TILE,),
        in_specs=[
            whole((rows, 128)),
            whole((rows, 1)),
            whole((rows, states)),
            pl.BlockSpec((rows, TILE), lambda i: (0, i)),
            pl.BlockSpec((states, TILE), lambda i: (0, i)),
        ],
        out_specs=pl.BlockSpec((rows, TILE), lambda i: (0, i)),
        out_shape=jax.ShapeDtypeStruct((rows, inner), BF),
        name="final",
        **params(2 * rows * rows * inner, 5_000_000),
    )(small, rel, output_map, part, enter)


def on_device(tokens, dt_decay, dest, lengths, w_x, w_bc, conv_x, conv_bc, bias_x, bias_bc, skip):
    rows, width = tokens.shape
    groups = lax.axis_size("ctx")
    ring = lax.axis_size("head")
    heads = dt_decay.shape[2]
    inner = w_x.shape[1]
    first_pos = lax.axis_index("ctx") * rows

    place = dest % rows + 1
    small = jnp.concatenate(
        [
            dt_decay.reshape(rows, 2 * heads),
            (place // 256).astype(BF)[:, None],
            (place % 256).astype(BF)[:, None],
            jnp.zeros((rows, 128 - 2 * heads - 2), BF),
        ],
        axis=1,
    )
    sent = pack(dest[None, :], tokens, small, groups)
    arrived = lax.all_to_all(
        sent.reshape(groups, CAP, width + 128), "ctx", split_axis=0, concat_axis=0, tiled=True
    ).reshape(groups * CAP, width + 128)
    mine, small = unpack(arrived, width, heads, rows)

    def turned(x, by):
        return lax.ppermute(x, "head", [(i, (i + by) % ring) for i in range(ring)])

    halo = lax.ppermute(
        mine[rows - HALO :], "ctx", [(i, i + 1) for i in range(groups - 1)]
    )
    xs = [mine] + [turned(mine, by) for by in (1, 2, 3)]
    hs = [halo] + [turned(halo, by) for by in (1, 2, 3)]

    starts = jnp.cumsum(lengths) - lengths
    positions = first_pos + jnp.arange(rows, dtype=jnp.int32)
    doc_start = jnp.max(
        jnp.where(starts[None, :] <= positions[:, None], starts[None, :], 0), axis=1
    )
    rel = (positions - doc_start)[:, None]
    me = lax.axis_index("head").astype(jnp.int32)[None]
    conv, state, mid, input_map, output_map = front(
        me, xs, hs, w_x, w_bc, small, rel, conv_x, bias_x[None, :], conv_bc, bias_bc[None, :]
    )
    states = input_map.shape[1]
    share = states // groups
    gathered = lax.all_to_all(
        state.reshape(groups, share, inner + 128), "ctx", split_axis=0, concat_axis=0, tiled=True
    ).reshape(states, inner + 128)
    part = inner_part(
        small, rel, input_map, output_map, conv, mid, jnp.repeat(skip, HD)[None, :]
    )
    entering = scan_shards(gathered, heads)
    enter = lax.all_to_all(
        entering.reshape(groups, share, inner), "ctx", split_axis=0, concat_axis=0, tiled=True
    ).reshape(states, inner)
    return final(small, rel, output_map, part, enter)


def solution(mesh):
    in_specs = (
        P("ctx", "head"),
        P("ctx", None, "head"),
        P("ctx"),
        P(),
        P(None, "head"),
        P(),
        P(None, "head"),
        P(),
        P("head"),
        P(),
        P("head"),
    )
    out_specs = P("ctx", "head")
    return jax.shard_map(
        on_device, mesh=mesh, in_specs=in_specs, out_specs=out_specs, check_vma=False
    )
```

time: 490 us -> 164 us (0.33); the launches traced: 484 us -> 163 us
  waiting for transfers between devices: 175 us -> 23.8 us
  other arithmetic: 97.2 us -> 1.39 us
  local copies, waits for them, and re-layouts: 81.8 us -> 14.6 us
  matrix products: 34.8 us -> 0 us
  blocking collectives: 43.3 us -> 74 us
  Pallas kernels: 0 us -> 30 us
  between operations: 16.6 us -> 0.29 us
  starting transfers between devices: 34.7 us -> 19.3 us
    all_gather x2 -> x0, waiting for transfers between devices: 108 us -> none  [the longest x1 108 us: entering_2(): pieces = jax.tree.map(lambda part: lax.all_gather(part, axis), value)]
    select_n x67 -> x0, other arithmetic: 79.3 us -> none  [the longest x63 77.4 us: turn(): jnp.where(position < mine, new, old)]
    all_to_all x0 -> x2, blocking collectives: none -> 74 us  [the longest x1 52.7 us: on_device(): lax.all_to_all(sent.reshape(groups, CAP, width + 128), 'ctx', split_axis=...]
    all_to_all x4 -> x1, waiting for transfers between devices: 65.9 us -> 4.16 us  [on_device(): lax.all_to_all(entering.reshape(groups, share, inner), 'ctx', split_axis=...]
    all_gather x1 -> x0, blocking collectives: 43.3 us -> none  [entering_2(): pieces = jax.tree.map(lambda part: lax.all_gather(part, axis), value)]
    mul x63 -> x0, local copies, waits for them, and re-layouts: 43.3 us -> none  [combine(): later[0][:, None, None] * earlier[1] + later[1]]
    dot_general x14 -> x0, matrix products: 34.8 us -> none  [the longest x3 14.8 us: into_slots(): jnp.dot(send_select, payload, preferred_element_type=jnp.float32)]
    pallas_call x0 -> x6, Pallas kernels: none -> 30 us  [the longest x1 13.8 us: front(): pl.pallas_call(functools.partial(front_kernel, heads), grid_spec=pltpu.Pr...]
  transfers between devices with their start and end apart: 8 -> 8, of which waited for: 6 -> 4; matrix products, arithmetic and copies ran while one was open for 15% -> 1% of each run, Pallas kernels for 0% -> 4%
where the time goes in v1:
time: 164 us; the launch traced here: 163 us
  blocking collectives  74 us (45%)
  Pallas kernels  30 us (18%)
  waiting for transfers between devices  23.8 us (15%)
  starting transfers between devices  19.3 us (12%)
  local copies, waits for them, and re-layouts  14.6 us (9%)
    all_to_all x1, blocking collectives, on_device(): lax.all_to_all(sent.reshape(groups, CAP, width + 128), 'ctx', split_axis=...  52.7 us
    all_to_all x1, blocking collectives, on_device(): lax.all_to_all(state.reshape(groups, share, inner + 128), 'ctx', split_ax...  21.3 us
    ppermute x6, waiting for transfers between devices, turned(): return lax.ppermute(x, 'head', [(i, (i + by) % ring) for i in range(ring)])  19.2 us
    pallas_call x1, Pallas kernels, front(): pl.pallas_call(functools.partial(front_kernel, heads), grid_spec=pltpu.Pr...  13.8 us
    unnamed x41, local copies, waits for them, and re-layouts  11.5 us
    ppermute x6, starting transfers between devices, turned(): return lax.ppermute(x, 'head', [(i, (i + by) % ring) for i in range(ring)])  9.31 us
    pallas_call x1, Pallas kernels, inner_part(): pl.pallas_call(functools.partial(inner_kernel, heads), grid=(inner // TIL...  6.45 us
    all_to_all x1, starting transfers between devices, on_device(): lax.all_to_all(entering.reshape(groups, share, inner), 'ctx', split_axis=...  6.27 us
  transfers between devices with their start and end apart: 8, of which 4 were waited for; matrix products, arithmetic and copies ran while one was open for 1% of the time, Pallas kernels for 4%

profile of v1, /device:TPU:1, one launch (start us, length us, event | category | flops | bytes accessed | tf_op | source)
XLA Modules:
  0.0 163.4 jit_solution(17983366672613364995)
XLA Ops:
  1.0 0.8 copy.20
  2.8 1.1 copy-done.16
  3.9 2.7 %pack.1 = bf16[1024,768]{1,0:T(8,128)(2,1)S(1)} custom-call(s32[1,512]{1,0:T(1,128)S(1)} %bitcast.13, bf16[512,640]{1,0:T(8,128)(2,1)S(1)} %copy-done.16, bf16[512,128]{1,0:T(8,128)(2,1)S(1)} %maximum_maximum_fusion.small_ref), custom_call_target="tpu_custom_call" | custom-call | flops 805306368 | bytes 1572864 | tf_op jit(solution)/shard_map/pack/pallas_call | solution.py:80
  6.6 52.7 %all_to_all.15 = bf16[64,16,768]{2,1,0:T(8,128)(2,1)S(1)} all-to-all(bf16[64,16,768]{2,1,0:T(8,128)(2,1)S(1)} %bitcast.12), channel_id=1, replica_groups=mesh['ctx'=64,'head'=4] {'ctx'}, dimensions={0} | all-to-all | bytes 3145728 | tf_op jit(solution)/shard_map/all_to_all | solution.py:447
  59.4 2.0 %unpack.1 = (bf16[512,640]{1,0:T(8,128)(2,1)S(1)}, bf16[512,128]{1,0:T(8,128)(2,1)S(1)}) custom-call(bf16[1024,768]{1,0:T(8,128)(2,1)S(1)} %bitcast.11), custom_call_target="tpu_custom_call" | custom-call | flops 805306368 | bytes 2359296 | tf_op jit(solution)/shard_map/unpack/pallas_call | solution.py:117
  61.4 1.3 collective-permute-start
  62.7 2.4 %collective-permute-start.1 = (bf16[512,640]{1,0:T(8,128)(2,1)S(1)}, bf16[512,640]{1,0:T(8,128)(2,1)S(1)}, u32[]{:S(2)}, u32[]{:S(2)}) collective-permute-start(bf16[512,640]{1,0:T(8,128)(2,1)S(1)} %get-tuple-element.13.refs_0_), channel_id=1, source_target_pairs={{0,2},{1,3},{2,0},{3,1},{4,6},{5,7},{6,4},{7,5},{8,10},{9,11},{10,... | collective-permute-start | bytes 1966088 | tf_op jit(solution)/shard_map/ppermute | solution.py:453
  65.2 1.2 collective-permute-start.2
  66.3 3.7 %collective-permute-start.3 = (bf16[16,640]{1,0:T(8,128)(2,1)S(1)}, bf16[16,640]{1,0:T(8,128)(2,1)S(1)}, u32[]{:S(2)}, u32[]{:S(2)}) collective-permute-start(bf16[16,640]{1,0:T(8,128)(2,1)S(1)} %slice.3), channel_id=1, source_target_pairs={{0,4},{4,8},{8,12},{12,16},{16,20},{20,24},{24,28},{28,32},{32,36}... | collective-permute-start | bytes 61448 | tf_op jit(solution)/shard_map/ppermute | solution.py:455
  72.3 18.9 %collective-permute-done.4.refs_5_ = bf16[16,640]{1,0:T(8,128)(2,1)S(1)} collective-permute-done((bf16[16,640]{1,0:T(8,128)(2,1)S(1)}, bf16[16,640]{1,0:T(8,128)(2,1)S(1)}, u32[]{:S(2)}, u32[]{:S(2)}) %collective-permute-start.4) | collective-permute-done | bytes 20512 | tf_op jit(solution)/shard_map/ppermute | solution.py:453
  91.9 3.4 %collective-permute-start.6 = (bf16[16,640]{1,0:T(8,128)(2,1)S(1)}, bf16[16,640]{1,0:T(8,128)(2,1)S(1)}, u32[]{:S(2)}, u32[]{:S(2)}) collective-permute-start(bf16[16,640]{1,0:T(8,128)(2,1)S(1)} %collective-permute-done.3.refs_4_), channel_id=1, source_target_pairs={{0,3},{1,0},{2,1},{3,2},{4,7},{5,4},{6,5},{7,6},{8,11},{9,8},{10,9... | collective-permute-start | bytes 61448 | tf_op jit(solution)/shard_map/ppermute | solution.py:453
  99.0 13.8 %front.1 = (bf16[512,1280]{1,0:T(8,128)(2,1)S(1)}, bf16[128,1408]{1,0:T(8,128)(2,1)S(1)}, f32[128,1280]{1,0:T(8,128)S(1)}, bf16[512,128]{1,0:T(8,128)(2,1)S(1)}, bf16[512,128]{1,0:T(8,128)(2,1)S(1)}) custom-call(s32[1]{0:T(128)} %bitcast.5.me_ref, bf16[512,640]{1,0:T(8,128)(2,1)S(1)} %get-tuple-element.13.refs_0_, ...), custom_call_target="tpu_custom_call" | custom-call | flops 4026531840 | bytes 12000000 | tf_op jit(solution)/shard_map/front/pallas_call | solution.py:256
  112.9 1.0 copy-done
  113.9 0.9 copy-done.2
  115.6 21.3 %all_to_all.16 = bf16[64,2,1408]{2,1,0:T(2,128)(2,1)S(1)} all-to-all(bf16[64,2,1408]{2,1,0:T(2,128)(2,1)S(1)} %reshape.77), channel_id=1, replica_groups=mesh['ctx'=64,'head'=4] {'ctx'}, dimensions={0} | all-to-all | bytes 720896 | tf_op jit(solution)/shard_map/all_to_all | solution.py:473
  137.0 0.9 scan_shards.1
  137.9 0.9 reshape.79
  138.8 6.3 %all-to-all-start.2 = ((bf16[64,2,1280]{2,1,0:T(2,128)(2,1)}), bf16[64,2,1280]{2,1,0:T(2,128)(2,1)}, u32[]{:S(2)}, u32[]{:S(2)}) async-start(bf16[64,2,1280]{2,1,0:T(2,128)(2,1)} %reshape.79), calls=%async_computation.2 | async-start | bytes 655360 | tf_op jit(solution)/shard_map/all_to_all | solution.py:480
  145.2 1.3 copy-done.1
  146.5 1.1 copy-done.3
  147.6 6.4 %inner_part.1.part_ref = f32[512,1280]{1,0:T(8,128)S(1)} custom-call(bf16[512,128]{1,0:T(8,128)(2,1)S(1)} %get-tuple-element.12.refs_16_.small_ref, s32[512,1]{1,0:T(8,128)S(1)} %add_subtract_fusion.refs_17_.rel_ref, bf16[512,128]{1,0:T(8,128)(2,1)S(1)} %copy-done.5, bf16[512,128]{1,0:T(8,128)(2,1)S(1)} %get-tuple-element.14.outmap_ref, ...), custom_call_target="tpu_custom_call" | custom-call | flops 1342177280 | bytes 8000000 | tf_op jit(solution)/shard_map/inner_part/pallas_call | solution.py:333
  154.1 4.2 %all-to-all-done.2 = bf16[64,2,1280]{2,1,0:T(2,128)(2,1)} async-done(((bf16[64,2,1280]{2,1,0:T(2,128)(2,1)}), bf16[64,2,1280]{2,1,0:T(2,128)(2,1)}, u32[]{:S(2)}, u32[]{:S(2)}) %all-to-all-start.2) | async-done | bytes 327712 | tf_op jit(solution)/shard_map/all_to_all | solution.py:480
  158.2 1.1 reshape.80.enter_ref
  159.3 4.1 %final.1 = bf16[512,1280]{1,0:T(8,128)(2,1)} custom-call(bf16[512,128]{1,0:T(8,128)(2,1)S(1)} %get-tuple-element.12.refs_16_.small_ref, s32[512,1]{1,0:T(8,128)S(1)} %add_subtract_fusion.refs_17_.rel_ref, bf16[512,128]{1,0:T(8,128)(2,1)S(1)} %get-tuple-element.14.outmap_ref, f32[512,1280]{1,0:T(8,128)S(1)} %inner_part.1.part_ref, ...), custom_call_target="tpu_custom_call" | custom-call | flops 671088640 | bytes 5000000 | tf_op jit(solution)/shard_map/final/pallas_call | solution.py:411
  (65 shorter events, 9.6 us)
Async XLA Ops:
  2.1 0.7 copy-start.14
  2.8 1.1 copy-start.16
  59.4 10.7 %copy-start.18 = (s32[128]{0:T(128)S(1)}, s32[128]{0:T(128)}, u32[]{:S(2)}) copy-start(s32[128]{0:T(128)} %param.14) | copy-start | bytes 1540
  59.4 35.9 %copy-start.17 = (f32[1280]{0:T(1024)S(1)}, f32[1280]{0:T(1024)}, u32[]{:S(2)}) copy-start(f32[1280]{0:T(1024)} %param.19) | copy-start | bytes 15364
  59.4 37.4 %copy-start.6 = (f32[4,1280]{1,0:T(4,128)S(1)}, f32[4,1280]{1,0:T(4,128)}, u32[]{:S(2)}) copy-start(f32[4,1280]{1,0:T(4,128)} %refs_18_.1) | copy-start | bytes 61444
  59.4 37.4 %copy-start.13 = (f32[4,256]{1,0:T(4,128)S(1)}, f32[4,256]{1,0:T(4,128)}, u32[]{:S(2)}) copy-start(f32[4,256]{1,0:T(4,128)} %refs_20_.1) | copy-start | bytes 12292
  59.4 37.4 %copy-start.15 = (f32[256]{0:T(256)S(1)}, f32[256]{0:T(256)}, u32[]{:S(2)}) copy-start(f32[256]{0:T(256)} %param.20) | copy-start | bytes 3076
  61.4 35.3 %collective-permute-start = (bf16[512,640]{1,0:T(8,128)(2,1)S(1)}, bf16[512,640]{1,0:T(8,128)(2,1)S(1)}, u32[]{:S(2)}, u32[]{:S(2)}) collective-permute-start(bf16[512,640]{1,0:T(8,128)(2,1)S(1)} %get-tuple-element.13.refs_0_), channel_id=1, source_target_pairs={{0,1},{1,2},{2,3},{3,0},{4,5},{5,6},{6,7},{7,4},{8,9},{9,10},{10,1... | collective-permute-start | bytes 1966088 | tf_op jit(solution)/shard_map/ppermute | solution.py:453
  62.7 34.1 %collective-permute-start.1 = (bf16[512,640]{1,0:T(8,128)(2,1)S(1)}, bf16[512,640]{1,0:T(8,128)(2,1)S(1)}, u32[]{:S(2)}, u32[]{:S(2)}) collective-permute-start(bf16[512,640]{1,0:T(8,128)(2,1)S(1)} %get-tuple-element.13.refs_0_), channel_id=1, source_target_pairs={{0,2},{1,3},{2,0},{3,1},{4,6},{5,7},{6,4},{7,5},{8,10},{9,11},{10,... | collective-permute-start | bytes 1966088 | tf_op jit(solution)/shard_map/ppermute | solution.py:453
  65.2 31.6 %collective-permute-start.2 = (bf16[512,640]{1,0:T(8,128)(2,1)S(1)}, bf16[512,640]{1,0:T(8,128)(2,1)S(1)}, u32[]{:S(2)}, u32[]{:S(2)}) collective-permute-start(bf16[512,640]{1,0:T(8,128)(2,1)S(1)} %get-tuple-element.13.refs_0_), channel_id=1, source_target_pairs={{0,3},{1,0},{2,1},{3,2},{4,7},{5,4},{6,5},{7,6},{8,11},{9,8},{10,9... | collective-permute-start | bytes 1966088 | tf_op jit(solution)/shard_map/ppermute | solution.py:453
  66.3 4.6 %collective-permute-start.3 = (bf16[16,640]{1,0:T(8,128)(2,1)S(1)}, bf16[16,640]{1,0:T(8,128)(2,1)S(1)}, u32[]{:S(2)}, u32[]{:S(2)}) collective-permute-start(bf16[16,640]{1,0:T(8,128)(2,1)S(1)} %slice.3), channel_id=1, source_target_pairs={{0,4},{4,8},{8,12},{12,16},{16,20},{20,24},{24,28},{28,32},{32,36}... | collective-permute-start | bytes 61448 | tf_op jit(solution)/shard_map/ppermute | solution.py:455
  70.9 20.3 %collective-permute-start.4 = (bf16[16,640]{1,0:T(8,128)(2,1)S(1)}, bf16[16,640]{1,0:T(8,128)(2,1)S(1)}, u32[]{:S(2)}, u32[]{:S(2)}) collective-permute-start(bf16[16,640]{1,0:T(8,128)(2,1)S(1)} %collective-permute-done.3.refs_4_), channel_id=1, source_target_pairs={{0,1},{1,2},{2,3},{3,0},{4,5},{5,6},{6,7},{7,4},{8,9},{9,10},{10,1... | collective-permute-start | bytes 61448 | tf_op jit(solution)/shard_map/ppermute | solution.py:453
  71.6 23.7 %collective-permute-start.5 = (bf16[16,640]{1,0:T(8,128)(2,1)S(1)}, bf16[16,640]{1,0:T(8,128)(2,1)S(1)}, u32[]{:S(2)}, u32[]{:S(2)}) collective-permute-start(bf16[16,640]{1,0:T(8,128)(2,1)S(1)} %collective-permute-done.3.refs_4_), channel_id=1, source_target_pairs={{0,2},{1,3},{2,0},{3,1},{4,6},{5,7},{6,4},{7,5},{8,10},{9,11},{10,... | collective-permute-start | bytes 61448 | tf_op jit(solution)/shard_map/ppermute | solution.py:453
  91.9 4.3 %collective-permute-start.6 = (bf16[16,640]{1,0:T(8,128)(2,1)S(1)}, bf16[16,640]{1,0:T(8,128)(2,1)S(1)}, u32[]{:S(2)}, u32[]{:S(2)}) collective-permute-start(bf16[16,640]{1,0:T(8,128)(2,1)S(1)} %collective-permute-done.3.refs_4_), channel_id=1, source_target_pairs={{0,3},{1,0},{2,1},{3,2},{4,7},{5,4},{6,5},{7,6},{8,11},{9,8},{10,9... | collective-permute-start | bytes 61448 | tf_op jit(solution)/shard_map/ppermute | solution.py:453
  96.8 0.7 copy-start.8
  97.6 0.7 copy-start.10
  98.3 0.7 copy-start.12
  112.8 1.1 copy-start
  113.9 0.9 copy-start.2
  115.6 29.5 %copy-start.19 = (f32[20]{0:T(128)S(1)}, f32[20]{0:T(128)}, u32[]{:S(2)}) copy-start(f32[20]{0:T(128)} %param.21) | copy-start | bytes 244
  115.6 29.6 %copy-start.5 = (bf16[512,128]{1,0:T(8,128)(2,1)S(1)}, bf16[512,128]{1,0:T(8,128)(2,1)}, u32[]{:S(2)}) copy-start(bf16[512,128]{1,0:T(8,128)(2,1)} %copy-done.4) | copy-start | bytes 393220
  138.8 19.5 %all-to-all-start.2 = ((bf16[64,2,1280]{2,1,0:T(2,128)(2,1)}), bf16[64,2,1280]{2,1,0:T(2,128)(2,1)}, u32[]{:S(2)}, u32[]{:S(2)}) async-start(bf16[64,2,1280]{2,1,0:T(2,128)(2,1)} %reshape.79), calls=%async_computation.2 | async-start | bytes 655360 | tf_op jit(solution)/shard_map/all_to_all | solution.py:480
  145.2 1.3 copy-start.1
  146.5 1.1 copy-start.3
  (4 other events, 2.5 us)

commit v2 on v1

--- a/solution.py
+++ b/solution.py
@@ -14,7 +14,10 @@
 HD = 64
 TILE = 256
 HALO = 16
-VMEM_LIMIT = 48 * 1024 * 1024
+VMEM_LIMIT = 60 * 1024 * 1024
+LANES = 128
+ROWS_SENT = 88
+HIGH_AT, LOW_AT = 40, 104
 
 
 def iota(shape, dim):
@@ -50,85 +53,154 @@
     )
 
 
-def pack_kernel(dest_ref, tok_ref, small_ref, out_ref, slot_ref):
+def pack_kernel(dest_ref, tok_ref, steps_ref, out_ref, slot_ref, code_ref, small_ref):
     step = pl.program_id(0)
-    rows = tok_ref.shape[0]
-    groups = 64
-    slots = out_ref.shape[0]
+    rows, width = tok_ref.shape
+    groups = code_ref.shape[0]
+    per = out_ref.shape[0]
+    slots = per * CAP
 
     @pl.when(step == 0)
     def _():
         dest = dest_ref[...]
         target = dest // rows
+        place = dest % rows + 1
         onehot = iota((groups, rows), 0) == target
         upper = as_bf(iota((rows, rows), 0) <= iota((rows, rows), 1))
         ranks = mm(as_bf(onehot), upper)
         rank = jnp.sum(jnp.where(onehot, ranks, 0.0), axis=0, keepdims=True) - 1.0
-        slot_ref[...] = target * CAP + rank.astype(jnp.int32)
-
-    select = as_bf(iota((slots, rows), 0) + step * slots == slot_ref[...])
-    width = tok_ref.shape[1]
-    out_ref[:, :width] = mm(select, tok_ref[...]).astype(BF)
-    out_ref[:, width:] = mm(select, small_ref[...]).astype(BF)
-
-
-def pack(dest, tokens, small, groups):
+        rank = rank.astype(jnp.int32)
+        slot_ref[...] = target * CAP + rank
+        line = iota((LANES, rows), 0)
+        codes = jnp.where(line == HIGH_AT + rank, place // 256, 0)
+        codes = codes + jnp.where(line == LOW_AT + rank, place % 256, 0)
+        code_ref[...] = mm_nt(as_bf(onehot), codes.astype(F32).astype(BF))
+        small_ref[...] = jnp.zeros_like(small_ref)
+        small_ref[:, : steps_ref.shape[1]] = steps_ref[...]
+
+    slot = slot_ref[...] - step * slots
+    sent = mm(as_bf(iota((slots, rows), 0) == slot), tok_ref[...]).astype(BF)
+    for column in range(width // LANES):
+        out_ref[:, column * CAP : (column + 1) * CAP, :] = sent[
+            :, column * LANES : (column + 1) * LANES
+        ].reshape(per, CAP, LANES)
+    half = CAP // 2
+    line = iota((per * half, rows), 0)
+    line = line + line // half * half
+    small = small_ref[...]
+    pairs = mm(as_bf(line == slot), small)
+    pairs = pairs + pltpu.roll(mm(as_bf(line + half == slot), small), LANES // 2, 1)
+    pairs = pairs.reshape(per, half, LANES)
+    codes = code_ref[pl.ds(pl.multiple_of(step * per, per), per)]
+    first = iota((per, half, LANES), 1) == 0
+    pairs = pairs + jnp.where(first, codes[:, None, :], 0.0)
+    out_ref[:, ROWS_SENT - half :, :] = pairs.astype(BF)
+
+
+def pack(dest, tokens, steps, groups):
     rows, width = tokens.shape
-    steps = 8
-    slots = groups * CAP // steps
-    full = width + small.shape[1]
+    count = 8
+    per = groups // count
     return pl.pallas_call(
         pack_kernel,
-        grid=(steps,),
+        grid=(count,),
         in_specs=[
             pl.BlockSpec((1, rows), lambda i: (0, 0)),
             pl.BlockSpec((rows, width), lambda i: (0, 0)),
-            pl.BlockSpec((rows, small.shape[1]), lambda i: (0, 0)),
-        ],
-        out_specs=pl.BlockSpec((slots, full), lambda i: (i, 0)),
-        out_shape=jax.ShapeDtypeStruct((groups * CAP, full), BF),
-        scratch_shapes=[pltpu.VMEM((1, rows), jnp.int32)],
+            pl.BlockSpec(steps.shape, lambda i: (0, 0)),
+        ],
+        out_specs=pl.BlockSpec((per, ROWS_SENT, LANES), lambda i: (i, 0, 0)),
+        out_shape=jax.ShapeDtypeStruct((groups, ROWS_SENT, LANES), BF),
+        scratch_shapes=[
+            pltpu.VMEM((1, rows), jnp.int32),
+            pltpu.VMEM((groups, LANES), F32),
+            pltpu.VMEM((rows, LANES), BF),
+        ],
         name="pack",
-        **params(2 * rows * groups * CAP * full, 4 * rows * full),
-    )(dest, tokens, small)
-
-
-def unpack_kernel(width, heads, recv_ref, tok_ref, small_ref, pos_ref):
+        **params(2 * rows * groups * CAP * (width + LANES), 4 * rows * width),
+    )(dest, tokens, steps)
+
+
+def unpack_kernel(
+    heads, recv_ref, low_ref, high_ref, small_ref, pos_ref, first_ref, second_ref, mixed_ref
+):
     step = pl.program_id(0)
-    rows = tok_ref.shape[0]
-    slots = recv_ref.shape[0]
+    groups = recv_ref.shape[0]
+    half = CAP // 2
+    rows, width = low_ref.shape
+
+    def places(row_codes, lane_slot, lane_group, count):
+        line = iota((LANES, count), 0)
+        table = jnp.where(
+            line == HIGH_AT + lane_slot, 256.0, jnp.where(line == LOW_AT + lane_slot, 1.0, 0.0)
+        ).astype(BF)
+        wide = mm(row_codes, table)
+        mine = iota((groups, count), 0) == lane_group
+        return jnp.sum(jnp.where(mine, wide, 0.0), axis=0, keepdims=True).astype(jnp.int32)
 
     @pl.when(step == 0)
     def _():
-        lane = iota((8, 128), 1)
-        pick = jnp.where(
-            lane == 2 * heads, 256.0, jnp.where(lane == 2 * heads + 1, 1.0, 0.0)
-        ).astype(BF)
-        pos_ref[...] = mm_nt(pick, recv_ref[:, width:])[0:1].astype(jnp.int32)
-
-    select = as_bf(iota((rows, slots), 0) + (step * rows + 1) == pos_ref[...])
-    tok_ref[...] = mm(select, recv_ref[:, :width]).astype(BF)
-    small_ref[...] = mm(select, recv_ref[:, width:]).astype(BF)
+        small = recv_ref[:, ROWS_SENT - half :, :].astype(F32)
+        mixed_ref[...] = small.reshape(groups * half, LANES).astype(BF)
+        codes = small[:, 0, :].astype(BF)
+        lane = iota((1, groups * CAP), 1)
+        pos_ref[...] = places(codes, lane % CAP, lane // CAP, groups * CAP)
+        lane = iota((1, groups * half), 1)
+        first_ref[...] = places(codes, lane % half, lane // half, groups * half)
+        second_ref[...] = places(codes, lane % half + half, lane // half, groups * half)
+
+    def pick(ref):
+        count = ref.shape[1]
+        return as_bf(iota((rows, count), 0) + (step * rows + 1) == ref[...])
+
+    select = pick(pos_ref)
+    taken = []
+    for column in range(width // LANES):
+        source = recv_ref[:, column * CAP : (column + 1) * CAP, :].reshape(groups * CAP, LANES)
+        taken.append(mm(select, source).astype(BF))
+    taken = jnp.concatenate(taken, axis=1)
+
+    @pl.when(step == 0)
+    def _():
+        low_ref[...] = taken
+
+    @pl.when(step == 1)
+    def _():
+        high_ref[...] = taken
+
+    mixed = mixed_ref[...]
+    small = mm(pick(first_ref), mixed)
+    turned = pltpu.roll(mm(pick(second_ref), mixed), LANES // 2, 1)
+    valid = iota((rows, LANES), 1) < 2 * heads
+    small_ref[...] = jnp.where(valid, small + turned, 0.0).astype(BF)
 
 
 def unpack(recv, width, heads, rows):
-    slots, full = recv.shape
-    steps = 4
+    groups = recv.shape[0]
+    half_rows = rows // 2
+    half_slots = groups * CAP // 2
     return pl.pallas_call(
-        functools.partial(unpack_kernel, width, heads),
-        grid=(steps,),
-        in_specs=[pl.BlockSpec((slots, full), lambda i: (0, 0))],
+        functools.partial(unpack_kernel, heads),
+        grid=(2,),
+        in_specs=[pl.BlockSpec(recv.shape, lambda i: (0, 0, 0))],
         out_specs=[
-            pl.BlockSpec((rows // steps, width), lambda i: (i, 0)),
-            pl.BlockSpec((rows // steps, full - width), lambda i: (i, 0)),
+            pl.BlockSpec((half_rows, width), lambda i: (0, 0)),
+            pl.BlockSpec((half_rows, width), lambda i: (0, 0)),
+            pl.BlockSpec((half_rows, LANES), lambda i: (i, 0)),
         ],
         out_shape=[
-            jax.ShapeDtypeStruct((rows, width), BF),
-            jax.ShapeDtypeStruct((rows, full - width), BF),
-        ],
-        scratch_shapes=[pltpu.VMEM((1, slots), jnp.int32)],
+            jax.ShapeDtypeStruct((half_rows, width), BF),
+            jax.ShapeDtypeStruct((half_rows, width), BF),
+            jax.ShapeDtypeStruct((rows, LANES), BF),
+        ],
+        scratch_shapes=[
+            pltpu.VMEM((1, groups * CAP), jnp.int32),
+            pltpu.VMEM((1, half_slots), jnp.int32),
+            pltpu.VMEM((1, half_slots), jnp.int32),
+            pltpu.VMEM((half_slots, LANES), BF),
+        ],
         name="unpack",
-        **params(2 * rows * slots * full, 6 * rows * full),
+        **params(2 * rows * groups * CAP * width, 6 * rows * width),
     )(recv)
 
 
@@ -148,27 +220,41 @@
 
 
 def front_kernel(heads, me_ref, *refs):
-    xs, hs, ws, wbs = refs[0:4], refs[4:8], refs[8:12], refs[12:16]
+    lows, highs, ws, wbs = refs[0:4], refs[4:8], refs[8:12], refs[12:16]
     small_ref, rel_ref, cx_ref, bx_ref, cb_ref, bb_ref = refs[16:22]
     conv_ref, state_ref, mid_ref, in_ref, outmap_ref = refs[22:27]
-    xe_ref = refs[27]
-    tile = pl.program_id(0)
-    rows = xs[0].shape[0]
-    rel = rel_ref[...]
+    xe_ref, acc_ref, sems = refs[27:30]
+    step = pl.program_id(0)
+    tiles = pl.num_programs(0) - 1
+    half = lows[0].shape[0]
+    rows = 2 * half
     states = in_ref.shape[1]
 
     def project(weights):
         total = mm(xe_ref[0], weights[0][0])
         for piece in range(1, 4):
             total = total + mm(xe_ref[piece], weights[piece][0])
-        return total.astype(BF).astype(F32)
-
-    @pl.when(tile == 0)
-    def _():
+        return total
+
+    def begin():
+        copies = []
         for piece in range(4):
-            xe_ref[piece, :HALO] = hs[piece][...]
-            xe_ref[piece, HALO:] = xs[piece][...]
-        both = conv_silu(project(wbs), cb_ref[...], bb_ref[...], rel, rows)
+            xe = xe_ref.at[piece]
+            for at, (source, target) in enumerate(
+                (
+                    (lows[piece], xe.at[pl.ds(HALO, half)]),
+                    (highs[piece].at[pl.ds(0, HALO)], xe.at[pl.ds(0, HALO)]),
+                    (highs[piece].at[pl.ds(HALO, half)], xe.at[pl.ds(HALO + half, half)]),
+                )
+            ):
+                copy = pltpu.make_async_copy(source, target, sems.at[piece, at])
+                copy.start()
+                copies.append(copy)
+        for copy in copies:
+            copy.wait()
+        rel = rel_ref[...]
+        ext = project(wbs).astype(BF).astype(F32)
+        both = conv_silu(ext, cb_ref[...], bb_ref[...], rel, rows)
         in_ref[...] = both[:, :states]
         outmap_ref[...] = both[:, states:]
         sums = []
@@ -187,35 +273,54 @@
         keep = (lane >= heads) & (lane < 2 * heads)
         state_ref[:, heads * HD :] = jnp.where(keep, jnp.where(even, high, low), 0.0).astype(BF)
 
-    inner = conv_silu(project(ws), cx_ref[...], bx_ref[...], rel, rows)
-    conv_ref[...] = inner
-    small = small_ref[...]
-    steps = mm(small, head_spread(tile, 0))
-    decays = mm(small, head_spread(tile, heads)).astype(BF)
-    inject = (inner.astype(F32) * steps).astype(BF).astype(F32)
-    ones = lower_ones(BLK)
-    carried = None
-    for block in range(rows // BLK):
-        span = slice(block * BLK, (block + 1) * BLK)
-        cumulative = mm(ones, decays[span])
-        last = rel[(block + 1) * BLK - 1 : (block + 1) * BLK]
-        end = cumulative[BLK - 1 : BLK]
-        behind = BLK - 1 - iota((BLK, 1), 0)
-        decayed = jnp.where(
-            behind <= last, jnp.exp(end - cumulative) * inject[span], 0.0
-        ).astype(BF)
-        block_state = mm_tn(in_ref[span], decayed)
-        carry = jnp.where(last > BLK - 1, jnp.exp(end), 0.0)
-        if carried is None:
-            carried = block_state
-            mid_ref[...] = carried
-        else:
-            carried = carry * carried + block_state
-    state_ref[:, pl.ds(pl.multiple_of(tile * TILE, TILE), TILE)] = carried.astype(BF)
-
-
-def front(me, xs, hs, w_x, w_bc, small, rel, conv_x, bias_x, conv_bc, bias_bc):
-    rows, width = xs[0].shape
+    def finish():
+        tile = step - 1
+        rel = rel_ref[...]
+        ext = acc_ref[tile % 2].astype(BF).astype(F32)
+        inner = conv_silu(ext, cx_ref[...], bx_ref[...], rel, rows)
+        conv_ref[...] = inner
+        small = small_ref[...]
+        steps = mm(small, head_spread(tile, 0))
+        decays = mm(small, head_spread(tile, heads)).astype(BF)
+        inject = (inner.astype(F32) * steps).astype(BF).astype(F32)
+        ones = lower_ones(BLK)
+        carried = None
+        for block in range(rows // BLK):
+            span = slice(block * BLK, (block + 1) * BLK)
+            cumulative = mm(ones, decays[span])
+            last = rel[(block + 1) * BLK - 1 : (block + 1) * BLK]
+            end = cumulative[BLK - 1 : BLK]
+            behind = BLK - 1 - iota((BLK, 1), 0)
+            decayed = jnp.where(
+                behind <= last, jnp.exp(end - cumulative) * inject[span], 0.0
+            ).astype(BF)
+            block_state = mm_tn(in_ref[span], decayed)
+            carry = jnp.where(last > BLK - 1, jnp.exp(end), 0.0)
+            if carried is None:
+                carried = block_state
+                mid_ref[...] = carried
+            else:
+                carried = carry * carried + block_state
+        state_ref[:, pl.ds(pl.multiple_of(tile * TILE, TILE), TILE)] = carried.astype(BF)
+
+    @pl.when(step == 0)
+    def _():
+        begin()
+        acc_ref[0] = project(ws)
+
+    @pl.when((step > 0) & (step < tiles))
+    def _():
+        finish()
+        acc_ref[step % 2] = project(ws)
+
+    @pl.when(step == tiles)
+    def _():
+        finish()
+
+
+def front(me, lows, highs, w_x, w_bc, small, rel, conv_x, bias_x, conv_bc, bias_bc):
+    half, width = lows[0].shape
+    rows = 2 * half
     inner = w_x.shape[1]
     heads = inner // HD
     states = w_bc.shape[1] // 2
@@ -226,11 +331,18 @@
     def whole(shape):
         return pl.BlockSpec(shape, lambda i, m: tuple(0 for _ in shape))
 
+    def ahead(i):
+        return jnp.minimum(i, tiles - 1)
+
+    def behind(i):
+        return jnp.maximum(i - 1, 0)
+
     in_specs = (
-        [whole((rows, width))] * 4
-        + [whole((HALO, width))] * 4
+        [pl.BlockSpec(memory_space=pltpu.HBM)] * 8
         + [
-            pl.BlockSpec((1, width, TILE), lambda i, m, k=k: ((m[0] + 4 - k) % 4, 0, i))
+            pl.BlockSpec(
+                (1, width, TILE), lambda i, m, k=k: ((m[0] + 4 - k) % 4, 0, ahead(i))
+            )
             for k in range(4)
         ]
         + [
@@ -240,16 +352,16 @@
         + [
             whole((rows, 128)),
             whole((rows, 1)),
-            pl.BlockSpec((conv_x.shape[0], TILE), lambda i, m: (0, i)),
-            pl.BlockSpec((1, TILE), lambda i, m: (0, i)),
+            pl.BlockSpec((conv_x.shape[0], TILE), lambda i, m: (0, behind(i))),
+            pl.BlockSpec((1, TILE), lambda i, m: (0, behind(i))),
             whole(conv_bc.shape),
             whole((1, 2 * states)),
         ]
     )
     out_specs = [
-        pl.BlockSpec((rows, TILE), lambda i, m: (0, i)),
+        pl.BlockSpec((rows, TILE), lambda i, m: (0, behind(i))),
         whole((states, inner + 128)),
-        pl.BlockSpec((states, TILE), lambda i, m: (0, i)),
+        pl.BlockSpec((states, TILE), lambda i, m: (0, behind(i))),
         whole((rows, states)),
         whole((rows, states)),
     ]
@@ -257,10 +369,14 @@
         functools.partial(front_kernel, heads),
         grid_spec=pltpu.PrefetchScalarGridSpec(
             num_scalar_prefetch=1,
-            grid=(tiles,),
+            grid=(tiles + 1,),
             in_specs=in_specs,
             out_specs=out_specs,
-            scratch_shapes=[pltpu.VMEM((4, rows + HALO, width), BF)],
+            scratch_shapes=[
+                pltpu.VMEM((4, rows + HALO, width), BF),
+                pltpu.VMEM((2, rows + HALO, TILE), F32),
+                pltpu.SemaphoreType.DMA((4, 3)),
+            ],
         ),
         out_shape=[
             jax.ShapeDtypeStruct((rows, inner), BF),
@@ -272,7 +388,7 @@
         name="front",
         **params(2 * rows * 4 * width * (inner + 2 * states), 12_000_000),
     )(
-        me, *xs, *hs, w4, w4, w4, w4, wb4, wb4, wb4, wb4,
+        me, *lows, *highs, w4, w4, w4, w4, wb4, wb4, wb4, wb4,
         small, rel, conv_x, bias_x, conv_bc, bias_bc,
     )
 
@@ -391,11 +507,18 @@
     )(recv)
 
 
-def final_kernel(heads, small_ref, rel_ref, outmap_ref, part_ref, enter_ref, out_ref):
+def final_kernel(
+    heads, small_ref, rel_ref, outmap_ref, part_ref, enter_ref, out_ref, ones_ref
+):
     tile = pl.program_id(0)
     rows = part_ref.shape[0]
+
+    @pl.when(tile == 0)
+    def _():
+        ones_ref[...] = lower_ones(rows)
+
     decays = mm(small_ref[...], head_spread(tile, heads)).astype(BF)
-    cumulative = mm(lower_ones(rows), decays)
+    cumulative = mm(ones_ref[...], decays)
     gain = jnp.where(iota((rows, 1), 0) < rel_ref[...], jnp.exp(cumulative), 0.0)
     outer = mm(outmap_ref[...], enter_ref[...])
     out_ref[...] = (part_ref[...] + gain * outer).astype(BF)
@@ -420,6 +543,7 @@
         ],
         out_specs=pl.BlockSpec((rows, TILE), lambda i: (0, i)),
         out_shape=jax.ShapeDtypeStruct((rows, inner), BF),
+        scratch_shapes=[pltpu.VMEM((rows, rows), BF)],
         name="final",
         **params(2 * rows * rows * inner, 5_000_000),
     )(small, rel, output_map, part, enter)
@@ -433,30 +557,22 @@
     inner = w_x.shape[1]
     first_pos = lax.axis_index("ctx") * rows
 
-    place = dest % rows + 1
-    small = jnp.concatenate(
-        [
-            dt_decay.reshape(rows, 2 * heads),
-            (place // 256).astype(BF)[:, None],
-            (place % 256).astype(BF)[:, None],
-            jnp.zeros((rows, 128 - 2 * heads - 2), BF),
-        ],
-        axis=1,
-    )
-    sent = pack(dest[None, :], tokens, small, groups)
-    arrived = lax.all_to_all(
-        sent.reshape(groups, CAP, width + 128), "ctx", split_axis=0, concat_axis=0, tiled=True
-    ).reshape(groups * CAP, width + 128)
-    mine, small = unpack(arrived, width, heads, rows)
+    sent = pack(dest[None, :], tokens, dt_decay.reshape(rows, 2 * heads), groups)
+    arrived = lax.all_to_all(sent, "ctx", split_axis=0, concat_axis=0, tiled=True)
+    low, high, small = unpack(arrived, width, heads, rows)
 
     def turned(x, by):
         return lax.ppermute(x, "head", [(i, (i + by) % ring) for i in range(ring)])
 
+    low_left, low_right = turned(low, 1), turned(low, ring - 1)
     halo = lax.ppermute(
-        mine[rows - HALO :], "ctx", [(i, i + 1) for i in range(groups - 1)]
-    )
-    xs = [mine] + [turned(mine, by) for by in (1, 2, 3)]
-    hs = [halo] + [turned(halo, by) for by in (1, 2, 3)]
+        high[high.shape[0] - HALO :], "ctx", [(i, i + 1) for i in range(groups - 1)]
+    )
+    high = jnp.concatenate([halo, high], axis=0)
+    high_left, high_right = turned(high, 1), turned(high, ring - 1)
+    low_far, high_far = turned(low_left, 1), turned(high_right, ring - 1)
+    lows = [low, low_left, low_far, low_right]
+    highs = [high, high_left, high_far, high_right]
 
     starts = jnp.cumsum(lengths) - lengths
     positions = first_pos + jnp.arange(rows, dtype=jnp.int32)
@@ -466,7 +582,7 @@
     rel = (positions - doc_start)[:, None]
     me = lax.axis_index("head").astype(jnp.int32)[None]
     conv, state, mid, input_map, output_map = front(
-        me, xs, hs, w_x, w_bc, small, rel, conv_x, bias_x[None, :], conv_bc, bias_bc[None, :]
+        me, lows, highs, w_x, w_bc, small, rel, conv_x, bias_x[None, :], conv_bc, bias_bc[None, :]
     )
     states = input_map.shape[1]
     share = states // groups

time: 164 us -> 167 us (1.018)
  Pallas kernels: 30 us -> 45.1 us
  local copies, waits for them, and re-layouts: 14.6 us -> 10.4 us
  blocking collectives: 74 us -> 69.9 us
  starting transfers between devices: 19.3 us -> 17 us
    unnamed x41 -> x22, local copies, waits for them, and re-layouts: 11.5 us -> 1.62 us
    pallas_call x2, Pallas kernels: 4.74 us -> 10.7 us  [the longest x1 6.07 us: pack(): pl.pallas_call(pack_kernel, grid=(count,), in_specs=[pl.BlockSpec((1, row...]
    pallas_call x1, Pallas kernels: 13.8 us -> 17.1 us  [front(): pl.pallas_call(functools.partial(front_kernel, heads), grid_spec=pltpu.Pr...]
    all_to_all x1, blocking collectives: 52.7 us -> 50.2 us  [on_device(): lax.all_to_all(sent, 'ctx', split_axis=0, concat_axis=0, tiled=True)]
    pallas_call x1, Pallas kernels: 6.45 us -> 8.52 us  [inner_part(): pl.pallas_call(functools.partial(inner_kernel, heads), grid=(inner // TIL...]
    pallas_call x1, Pallas kernels: 4.08 us -> 6.12 us  [final(): pl.pallas_call(functools.partial(final_kernel, inner // HD), grid=(inner...]
    pallas_call x1, Pallas kernels: 0.92 us -> 2.65 us  [scan_shards(): pl.pallas_call(functools.partial(scan_kernel, heads), out_shape=jax.Shape...]
  transfers between devices with their start and end apart: 8 -> 8, of which waited for: 4 -> 5; matrix products, arithmetic and copies ran while one was open for 1% -> 2% of each run, Pallas kernels for 4% -> 5%
where the time goes in v2:
time: 167 us
  blocking collectives  69.9 us (42%)
  Pallas kernels  45.1 us (27%)
  waiting for transfers between devices  22.8 us (14%)
  starting transfers between devices  17 us (10%)
  local copies, waits for them, and re-layouts  10.4 us (6%)
    all_to_all x1, blocking collectives, on_device(): lax.all_to_all(sent, 'ctx', split_axis=0, concat_axis=0, tiled=True)  50.2 us
    all_to_all x1, blocking collectives, on_device(): lax.all_to_all(state.reshape(groups, share, inner + 128), 'ctx', split_ax...  19.6 us
    ppermute x6, waiting for transfers between devices, turned(): return lax.ppermute(x, 'head', [(i, (i + by) % ring) for i in range(ring)])  17.9 us
    pallas_call x1, Pallas kernels, front(): pl.pallas_call(functools.partial(front_kernel, heads), grid_spec=pltpu.Pr...  17.1 us
    pallas_call x1, Pallas kernels, inner_part(): pl.pallas_call(functools.partial(inner_kernel, heads), grid=(inner // TIL...  8.52 us
    ppermute x6, starting transfers between devices, turned(): return lax.ppermute(x, 'head', [(i, (i + by) % ring) for i in range(ring)])  7.98 us
    pallas_call x1, Pallas kernels, final(): pl.pallas_call(functools.partial(final_kernel, inner // HD), grid=(inner...  6.12 us
    all_to_all x1, starting transfers between devices, on_device(): lax.all_to_all(entering.reshape(groups, share, inner), 'ctx', split_axis=...  6.09 us
  transfers between devices with their start and end apart: 8, of which 5 were waited for; matrix products, arithmetic and copies ran while one was open for 2% of the time, Pallas kernels for 5%

profile of v2, /device:TPU:1, one launch (start us, length us, event | category | flops | bytes accessed | tf_op | source)
XLA Modules:
  0.0 166.6 jit_solution(13440880103099539330)
XLA Ops:
  0.0 0.8 copy.18
  1.6 6.1 %pack.1 = bf16[64,88,128]{2,1,0:T(8,128)(2,1)} custom-call(s32[1,512]{1,0:T(1,128)} %bitcast.20, bf16[512,640]{1,0:T(8,128)(2,1)} %tok_ref.1, bf16[512,40]{1,0:T(8,128)(2,1)} %copy.19.steps_ref), custom_call_target="tpu_custom_call" | custom-call | flops 805306368 | bytes 1310720 | tf_op jit(solution)/shard_map/pack/pallas_call | solution.py:104
  7.6 50.2 %all_to_all.15.recv_ref = bf16[64,88,128]{2,1,0:T(8,128)(2,1)} all-to-all(bf16[64,88,128]{2,1,0:T(8,128)(2,1)} %pack.1), channel_id=1, replica_groups=mesh['ctx'=64,'head'=4] {'ctx'}, dimensions={0} | all-to-all | bytes 2883584 | tf_op jit(solution)/shard_map/all_to_all | solution.py:561
  57.9 4.6 %unpack.1 = (bf16[256,640]{1,0:T(8,128)(2,1)}, bf16[256,640]{1,0:T(8,128)(2,1)}, bf16[512,128]{1,0:T(8,128)(2,1)}) custom-call(bf16[64,88,128]{2,1,0:T(8,128)(2,1)} %all_to_all.15.recv_ref), custom_call_target="tpu_custom_call" | custom-call | flops 671088640 | bytes 1966080 | tf_op jit(solution)/shard_map/unpack/pallas_call | solution.py:182
  63.2 3.0 %collective-permute-start.3 = (bf16[16,640]{1,0:T(8,128)(2,1)S(1)}, bf16[16,640]{1,0:T(8,128)(2,1)S(1)}, u32[]{:S(2)}, u32[]{:S(2)}) collective-permute-start(bf16[16,640]{1,0:T(8,128)(2,1)S(1)} %slice.3), channel_id=1, source_target_pairs={{0,4},{4,8},{8,12},{12,16},{16,20},{20,24},{24,28},{28,32},{32,36}... | collective-permute-start | bytes 61448 | tf_op jit(solution)/shard_map/ppermute | solution.py:568
  66.2 0.9 collective-permute-done.3
  67.1 1.0 constant_dynamic-update-slice_fusion.refs_4_
  68.1 2.6 %collective-permute-start.5 = (bf16[272,640]{1,0:T(8,128)(2,1)S(1)}, bf16[272,640]{1,0:T(8,128)(2,1)S(1)}, u32[]{:S(2)}, u32[]{:S(2)}) collective-permute-start(bf16[272,640]{1,0:T(8,128)(2,1)S(1)} %constant_dynamic-update-slice_fusion.refs_4_), channel_id=1, source_target_pairs={{0,3},{1,0},{2,1},{3,2},{4,7},{5,4},{6,5},{7,6},{8,11},{9,8},{10,9... | collective-permute-start | bytes 1044488 | tf_op jit(solution)/shard_map/ppermute | solution.py:565
  71.1 2.8 %collective-permute-start.2 = (bf16[256,640]{1,0:T(8,128)(2,1)}, bf16[256,640]{1,0:T(8,128)(2,1)S(1)}, u32[]{:S(2)}, u32[]{:S(2)}) collective-permute-start(bf16[256,640]{1,0:T(8,128)(2,1)} %get-tuple-element.14.refs_0_), channel_id=1, source_target_pairs={{0,3},{1,0},{2,1},{3,2},{4,7},{5,4},{6,5},{7,6},{8,11},{9,8},{10,9... | collective-permute-start | bytes 983048 | tf_op jit(solution)/shard_map/ppermute | solution.py:565
  73.9 7.9 %collective-permute-done.refs_1_ = bf16[256,640]{1,0:T(8,128)(2,1)S(1)} collective-permute-done((bf16[256,640]{1,0:T(8,128)(2,1)}, bf16[256,640]{1,0:T(8,128)(2,1)S(1)}, u32[]{:S(2)}, u32[]{:S(2)}) %collective-permute-start) | collective-permute-done | bytes 327712 | tf_op jit(solution)/shard_map/ppermute | solution.py:565
  81.7 2.7 %collective-permute-start.6 = (bf16[272,640]{1,0:T(8,128)(2,1)S(1)}, bf16[272,640]{1,0:T(8,128)(2,1)S(1)}, u32[]{:S(2)}, u32[]{:S(2)}) collective-permute-start(bf16[272,640]{1,0:T(8,128)(2,1)S(1)} %collective-permute-done.5.refs_7_), channel_id=1, source_target_pairs={{0,3},{1,0},{2,1},{3,2},{4,7},{5,4},{6,5},{7,6},{8,11},{9,8},{10,9... | collective-permute-start | bytes 1044488 | tf_op jit(solution)/shard_map/ppermute | solution.py:565
  86.1 3.0 %collective-permute-done.4.refs_5_ = bf16[272,640]{1,0:T(8,128)(2,1)S(1)} collective-permute-done((bf16[272,640]{1,0:T(8,128)(2,1)S(1)}, bf16[272,640]{1,0:T(8,128)(2,1)S(1)}, u32[]{:S(2)}, u32[]{:S(2)}) %collective-permute-start.4) | collective-permute-done | bytes 348192 | tf_op jit(solution)/shard_map/ppermute | solution.py:565
  89.2 7.0 %collective-permute-done.1.refs_2_ = bf16[256,640]{1,0:T(8,128)(2,1)S(1)} collective-permute-done((bf16[256,640]{1,0:T(8,128)(2,1)S(1)}, bf16[256,640]{1,0:T(8,128)(2,1)S(1)}, u32[]{:S(2)}, u32[]{:S(2)}) %collective-permute-start.1) | collective-permute-done | bytes 327712 | tf_op jit(solution)/shard_map/ppermute | solution.py:565
  97.0 17.1 %front.1 = (bf16[512,1280]{1,0:T(8,128)(2,1)}, bf16[128,1408]{1,0:T(8,128)(2,1)}, f32[128,1280]{1,0:T(8,128)}, bf16[512,128]{1,0:T(8,128)(2,1)}, bf16[512,128]{1,0:T(8,128)(2,1)}) custom-call(s32[1]{0:T(128)} %bitcast.3.me_ref, bf16[256,640]{1,0:T(8,128)(2,1)} %get-tuple-element.14.refs_0_, bf16[256,640]{1,0:T(8,128)(2,1)} %copy-done.4, ...), custom_call_target="tpu_custom_call" | custom-call | flops 4026531840 | bytes 12000000 | tf_op jit(solution)/shard_map/front/pallas_call | solution.py:368
  114.1 1.1 reshape.69
  115.3 19.6 %all_to_all.16 = bf16[64,2,1408]{2,1,0:T(2,128)(2,1)S(1)} all-to-all(bf16[64,2,1408]{2,1,0:T(2,128)(2,1)S(1)} %reshape.69), channel_id=1, replica_groups=mesh['ctx'=64,'head'=4] {'ctx'}, dimensions={0} | all-to-all | bytes 720896 | tf_op jit(solution)/shard_map/all_to_all | solution.py:589
  134.9 0.9 reshape.70.recv_ref
  135.8 2.6 %scan_shards.1 = bf16[128,1280]{1,0:T(8,128)(2,1)} custom-call(bf16[128,1408]{1,0:T(8,128)(2,1)} %reshape.70.recv_ref), custom_call_target="tpu_custom_call" | custom-call | flops 83886080 | bytes 700000 | tf_op jit(solution)/shard_map/scan_shards/pallas_call | solution.py:501
  138.4 1.8 %reshape.71 = bf16[64,2,1280]{2,1,0:T(2,128)(2,1)} reshape(bf16[128,1280]{1,0:T(8,128)(2,1)} %scan_shards.1) | data formatting | bytes 655360 | tf_op jit(solution)/shard_map/reshape | solution.py:597
  140.2 6.1 %all-to-all-start.2 = ((bf16[64,2,1280]{2,1,0:T(2,128)(2,1)}), bf16[64,2,1280]{2,1,0:T(2,128)(2,1)S(1)}, u32[]{:S(2)}, u32[]{:S(2)}) async-start(bf16[64,2,1280]{2,1,0:T(2,128)(2,1)} %reshape.71), calls=%async_computation.2 | async-start | bytes 655360 | tf_op jit(solution)/shard_map/all_to_all | solution.py:596
  147.1 8.5 %inner_part.1.part_ref = f32[512,1280]{1,0:T(8,128)} custom-call(bf16[512,128]{1,0:T(8,128)(2,1)} %get-tuple-element.13.refs_16_.small_ref, s32[512,1]{1,0:T(8,128)} %add_subtract_fusion.refs_17_.rel_ref, bf16[512,128]{1,0:T(8,128)(2,1)} %get-tuple-element.17.in_ref, bf16[512,128]{1,0:T(8,128)(2,1)} %get-tuple-element.16.outmap_ref, ...), custom_call_target="tpu_custom_call" | custom-call | flops 1342177280 | bytes 8000000 | tf_op jit(solution)/shard_map/inner_part/pallas_call | solution.py:449
  155.6 4.0 %all-to-all-done.2 = bf16[64,2,1280]{2,1,0:T(2,128)(2,1)S(1)} async-done(((bf16[64,2,1280]{2,1,0:T(2,128)(2,1)}), bf16[64,2,1280]{2,1,0:T(2,128)(2,1)S(1)}, u32[]{:S(2)}, u32[]{:S(2)}) %all-to-all-start.2) | async-done | bytes 327712 | tf_op jit(solution)/shard_map/all_to_all | solution.py:596
  159.6 0.8 reshape.72.enter_ref
  160.4 6.1 %final.1 = bf16[512,1280]{1,0:T(8,128)(2,1)} custom-call(bf16[512,128]{1,0:T(8,128)(2,1)} %get-tuple-element.13.refs_16_.small_ref, s32[512,1]{1,0:T(8,128)} %add_subtract_fusion.refs_17_.rel_ref, bf16[512,128]{1,0:T(8,128)(2,1)} %get-tuple-element.16.outmap_ref, f32[512,1280]{1,0:T(8,128)} %inner_part.1.part_ref, bf16[128,1280]{1,0:T(8,128)(2,1)} %reshape.72.enter_ref), custom_call_target="tpu_custom_call" | custom-call | flops 671088640 | bytes 5000000 | tf_op jit(solution)/shard_map/final/pallas_call | solution.py:534
  (41 shorter events, 5.2 us)
Async XLA Ops:
  57.9 12.8 %copy-start.8 = (s32[128]{0:T(128)S(1)}, s32[128]{0:T(128)}, u32[]{:S(2)}) copy-start(s32[128]{0:T(128)} %param.14) | copy-start | bytes 1540
  57.9 26.9 %copy-start.7 = (f32[1280]{0:T(1024)S(1)}, f32[1280]{0:T(1024)}, u32[]{:S(2)}) copy-start(f32[1280]{0:T(1024)} %param.19) | copy-start | bytes 15364
  63.2 3.9 %collective-permute-start.3 = (bf16[16,640]{1,0:T(8,128)(2,1)S(1)}, bf16[16,640]{1,0:T(8,128)(2,1)S(1)}, u32[]{:S(2)}, u32[]{:S(2)}) collective-permute-start(bf16[16,640]{1,0:T(8,128)(2,1)S(1)} %slice.3), channel_id=1, source_target_pairs={{0,4},{4,8},{8,12},{12,16},{16,20},{20,24},{24,28},{28,32},{32,36}... | collective-permute-start | bytes 61448 | tf_op jit(solution)/shard_map/ppermute | solution.py:568
  68.1 28.1 %copy-start = (bf16[272,640]{1,0:T(8,128)(2,1)}, bf16[272,640]{1,0:T(8,128)(2,1)S(1)}, u32[]{:S(2)}) copy-start(bf16[272,640]{1,0:T(8,128)(2,1)S(1)} %constant_dynamic-update-slice_fusion.refs_4_) | copy-start | bytes 1044484
  68.1 13.6 %collective-permute-start.5 = (bf16[272,640]{1,0:T(8,128)(2,1)S(1)}, bf16[272,640]{1,0:T(8,128)(2,1)S(1)}, u32[]{:S(2)}, u32[]{:S(2)}) collective-permute-start(bf16[272,640]{1,0:T(8,128)(2,1)S(1)} %constant_dynamic-update-slice_fusion.refs_4_), channel_id=1, source_target_pairs={{0,3},{1,0},{2,1},{3,2},{4,7},{5,4},{6,5},{7,6},{8,11},{9,8},{10,9... | collective-permute-start | bytes 1044488 | tf_op jit(solution)/shard_map/ppermute | solution.py:565
  70.7 11.0 %collective-permute-start = (bf16[256,640]{1,0:T(8,128)(2,1)}, bf16[256,640]{1,0:T(8,128)(2,1)S(1)}, u32[]{:S(2)}, u32[]{:S(2)}) collective-permute-start(bf16[256,640]{1,0:T(8,128)(2,1)} %get-tuple-element.14.refs_0_), channel_id=1, source_target_pairs={{0,1},{1,2},{2,3},{3,0},{4,5},{5,6},{6,7},{7,4},{8,9},{9,10},{10,1... | collective-permute-start | bytes 983048 | tf_op jit(solution)/shard_map/ppermute | solution.py:565
  71.1 15.0 %collective-permute-start.2 = (bf16[256,640]{1,0:T(8,128)(2,1)}, bf16[256,640]{1,0:T(8,128)(2,1)S(1)}, u32[]{:S(2)}, u32[]{:S(2)}) collective-permute-start(bf16[256,640]{1,0:T(8,128)(2,1)} %get-tuple-element.14.refs_0_), channel_id=1, source_target_pairs={{0,3},{1,0},{2,1},{3,2},{4,7},{5,4},{6,5},{7,6},{8,11},{9,8},{10,9... | collective-permute-start | bytes 983048 | tf_op jit(solution)/shard_map/ppermute | solution.py:565
  73.8 15.3 %collective-permute-start.4 = (bf16[272,640]{1,0:T(8,128)(2,1)S(1)}, bf16[272,640]{1,0:T(8,128)(2,1)S(1)}, u32[]{:S(2)}, u32[]{:S(2)}) collective-permute-start(bf16[272,640]{1,0:T(8,128)(2,1)S(1)} %constant_dynamic-update-slice_fusion.refs_4_), channel_id=1, source_target_pairs={{0,1},{1,2},{2,3},{3,0},{4,5},{5,6},{6,7},{7,4},{8,9},{9,10},{10,1... | collective-permute-start | bytes 1044488 | tf_op jit(solution)/shard_map/ppermute | solution.py:565
  81.7 14.5 %copy-start.4 = (bf16[256,640]{1,0:T(8,128)(2,1)}, bf16[256,640]{1,0:T(8,128)(2,1)S(1)}, u32[]{:S(2)}) copy-start(bf16[256,640]{1,0:T(8,128)(2,1)S(1)} %collective-permute-done.refs_1_) | copy-start | bytes 983044
  81.7 14.5 %collective-permute-start.1 = (bf16[256,640]{1,0:T(8,128)(2,1)S(1)}, bf16[256,640]{1,0:T(8,128)(2,1)S(1)}, u32[]{:S(2)}, u32[]{:S(2)}) collective-permute-start(bf16[256,640]{1,0:T(8,128)(2,1)S(1)} %collective-permute-done.refs_1_), channel_id=1, source_target_pairs={{0,1},{1,2},{2,3},{3,0},{4,5},{5,6},{6,7},{7,4},{8,9},{9,10},{10,1... | collective-permute-start | bytes 983048 | tf_op jit(solution)/shard_map/ppermute | solution.py:565
  81.7 14.5 %copy-start.1 = (bf16[272,640]{1,0:T(8,128)(2,1)}, bf16[272,640]{1,0:T(8,128)(2,1)S(1)}, u32[]{:S(2)}) copy-start(bf16[272,640]{1,0:T(8,128)(2,1)S(1)} %collective-permute-done.5.refs_7_) | copy-start | bytes 1044484
  81.7 14.5 %collective-permute-start.6 = (bf16[272,640]{1,0:T(8,128)(2,1)S(1)}, bf16[272,640]{1,0:T(8,128)(2,1)S(1)}, u32[]{:S(2)}, u32[]{:S(2)}) collective-permute-start(bf16[272,640]{1,0:T(8,128)(2,1)S(1)} %collective-permute-done.5.refs_7_), channel_id=1, source_target_pairs={{0,3},{1,0},{2,1},{3,2},{4,7},{5,4},{6,5},{7,6},{8,11},{9,8},{10,9... | collective-permute-start | bytes 1044488 | tf_op jit(solution)/shard_map/ppermute | solution.py:565
  86.1 10.1 %copy-start.5 = (bf16[256,640]{1,0:T(8,128)(2,1)}, bf16[256,640]{1,0:T(8,128)(2,1)S(1)}, u32[]{:S(2)}) copy-start(bf16[256,640]{1,0:T(8,128)(2,1)S(1)} %collective-permute-done.2.refs_3_) | copy-start | bytes 983044
  89.2 7.1 %copy-start.2 = (bf16[272,640]{1,0:T(8,128)(2,1)}, bf16[272,640]{1,0:T(8,128)(2,1)S(1)}, u32[]{:S(2)}) copy-start(bf16[272,640]{1,0:T(8,128)(2,1)S(1)} %collective-permute-done.4.refs_5_) | copy-start | bytes 1044484
  96.2 0.7 copy-start.6
  96.2 0.8 copy-start.3
  134.9 11.4 %copy-start.9 = (f32[20]{0:T(128)S(1)}, f32[20]{0:T(128)}, u32[]{:S(2)}) copy-start(f32[20]{0:T(128)} %param.21) | copy-start | bytes 244
  140.2 19.3 %all-to-all-start.2 = ((bf16[64,2,1280]{2,1,0:T(2,128)(2,1)}), bf16[64,2,1280]{2,1,0:T(2,128)(2,1)S(1)}, u32[]{:S(2)}, u32[]{:S(2)}) async-start(bf16[64,2,1280]{2,1,0:T(2,128)(2,1)} %reshape.71), calls=%async_computation.2 | async-start | bytes 655360 | tf_op jit(solution)/shard_map/all_to_all | solution.py:596

commit v3 on v0

v3 whole, which is shorter than its diff:
```python
import functools

import jax
import jax.numpy as jnp
from jax import lax
from jax.experimental import pallas as pl
from jax.experimental.pallas import tpu as pltpu
from jax.sharding import PartitionSpec as P

BF = jnp.bfloat16
F32 = jnp.float32
CAP = 16
BLK = 256
HD = 64
TILE = 256
HALO = 16
LANES = 128
ROWS_SENT = 88
DECAY_AT = 24
SMALL_END = 44
HIGH_AT, LOW_AT = 44, 108
PIECE = 24


def iota(shape, dim):
    return lax.broadcasted_iota(jnp.int32, shape, dim)


def mm(a, b):
    return jnp.dot(a, b, preferred_element_type=F32)


def mm_nt(a, b):
    return lax.dot_general(a, b, (((1,), (1,)), ((), ())), preferred_element_type=F32)


def mm_tn(a, b):
    return lax.dot_general(a, b, (((0,), (0,)), ((), ())), preferred_element_type=F32)


def as_bf(mask):
    return jnp.where(mask, 1.0, 0.0).astype(BF)


def lower_ones(n):
    return as_bf(iota((n, n), 0) >= iota((n, n), 1))


def params(mib, flops=0, bytes_accessed=0):
    return dict(
        compiler_params=pltpu.CompilerParams(vmem_limit_bytes=mib * 1024 * 1024),
        cost_estimate=pl.CostEstimate(
            flops=flops, bytes_accessed=bytes_accessed, transcendentals=0
        ),
    )


def vmem(count):
    return [pl.BlockSpec(memory_space=pltpu.VMEM)] * count


def near(x):
    return pltpu.with_memory_space_constraint(x, pltpu.VMEM)


def far(x):
    return pltpu.with_memory_space_constraint(x, pltpu.HBM)


def hbm(count):
    return [pl.BlockSpec(memory_space=pltpu.HBM)] * count


def fetch(source, target, sem):
    copy = pltpu.make_async_copy(source, target, sem)
    copy.start()
    return copy


def pack_kernel(
    dest_hbm, steps_hbm, tok_hbm, out_ref,
    dest_ref, steps_ref, tok_ref, slot_ref, code_ref, small_ref, sems,
):
    get_dest = fetch(dest_hbm, dest_ref, sems.at[0])
    get_steps = fetch(steps_hbm, steps_ref, sems.at[1])
    get_tokens = fetch(tok_hbm, tok_ref, sems.at[2])
    rows, width = tok_ref.shape
    groups = code_ref.shape[0]
    heads = steps_ref.shape[0]
    per = 8
    slots = per * CAP
    get_dest.wait()
    dest = dest_ref[...]
    target = dest // rows
    place = dest % rows + 1
    onehot = iota((groups, rows), 0) == target
    upper = as_bf(iota((rows, rows), 0) <= iota((rows, rows), 1))
    ranks = mm(as_bf(onehot), upper)
    rank = jnp.sum(jnp.where(onehot, ranks, 0.0), axis=0, keepdims=True) - 1.0
    rank = rank.astype(jnp.int32)
    slot_ref[...] = target * CAP + rank
    line = iota((LANES, rows), 0)
    codes = jnp.where(line == HIGH_AT + rank, place // 256, 0)
    codes = codes + jnp.where(line == LOW_AT + rank, place % 256, 0)
    code_ref[...] = mm_nt(as_bf(onehot), codes.astype(F32).astype(BF))
    get_steps.wait()
    steps = steps_ref[...].astype(F32)
    small_ref[...] = jnp.zeros_like(small_ref)
    small_ref[:heads] = steps[:, 0, :]
    small_ref[DECAY_AT : DECAY_AT + heads] = steps[:, 1, :]
    get_tokens.wait()

    def body(step, _):
        slot = slot_ref[...] - step * slots
        here = pl.ds(pl.multiple_of(step * per, per), per)
        sent = mm(as_bf(iota((slots, rows), 0) == slot), tok_ref[...]).astype(BF)
        for column in range(width // LANES):
            out_ref[here, column * CAP : (column + 1) * CAP, :] = sent[
                :, column * LANES : (column + 1) * LANES
            ].reshape(per, CAP, LANES)
        half = CAP // 2
        line = iota((per * half, rows), 0)
        line = line + line // half * half
        small = small_ref[...].astype(BF)
        pairs = mm_nt(as_bf(line == slot), small)
        pairs = pairs + pltpu.roll(mm_nt(as_bf(line + half == slot), small), LANES // 2, 1)
        pairs = pairs.reshape(per, half, LANES)
        first = iota((per, half, LANES), 1) == 0
        pairs = pairs + jnp.where(first, code_ref[here][:, None, :], 0.0)
        out_ref[here, ROWS_SENT - half :, :] = pairs.astype(BF)
        return 0

    lax.fori_loop(0, groups // per, body, 0)


def pack(dest, tokens, steps, groups):
    rows, width = tokens.shape
    return pl.pallas_call(
        pack_kernel,
        in_specs=hbm(3),
        out_specs=pl.BlockSpec(memory_space=pltpu.VMEM),
        out_shape=jax.ShapeDtypeStruct((groups, ROWS_SENT, LANES), BF),
        scratch_shapes=[
            pltpu.VMEM((1, rows), jnp.int32),
            pltpu.VMEM(steps.shape, BF),
            pltpu.VMEM((rows, width), BF),
            pltpu.VMEM((1, rows), jnp.int32),
            pltpu.VMEM((groups, LANES), F32),
            pltpu.VMEM((LANES, rows), F32),
            pltpu.SemaphoreType.DMA((3,)),
        ],
        name="pack",
        **params(16, 2 * rows * groups * CAP * (width + LANES), 4 * rows * width),
    )(far(dest), far(steps), far(tokens))


def places(row_codes, groups, lane_slot, lane_group, count):
    line = iota((LANES, count), 0)
    table = jnp.where(
        line == HIGH_AT + lane_slot, 256.0, jnp.where(line == LOW_AT + lane_slot, 1.0, 0.0)
    ).astype(BF)
    wide = mm(row_codes, table)
    mine = iota((groups, count), 0) == lane_group
    return jnp.sum(jnp.where(mine, wide, 0.0), axis=0, keepdims=True).astype(jnp.int32)


def pick(pos, first, rows):
    return as_bf(iota((rows, pos.shape[1]), 0) + (first + 1) == pos)


def take(select, recv_ref, target, first_row):
    groups = recv_ref.shape[0]
    rows = select.shape[0]
    for column in range(target.shape[1] // LANES):
        source = recv_ref[:, column * CAP : (column + 1) * CAP, :]
        target[first_row : first_row + rows, column * LANES : (column + 1) * LANES] = mm(
            select, source.reshape(groups * CAP, LANES)
        ).astype(BF)


def unpack_low_kernel(recv_ref, low_ref, edge_ref, pos_ref):
    groups = recv_ref.shape[0]
    half = CAP // 2
    rows = 2 * low_ref.shape[0]
    codes = recv_ref[:, ROWS_SENT - half :, :].astype(F32)[:, 0, :].astype(BF)
    lane = iota((1, groups * CAP), 1)
    pos = places(codes, groups, lane % CAP, lane // CAP, groups * CAP)
    pos_ref[...] = pos
    take(pick(pos, 0, rows // 2), recv_ref, low_ref, 0)
    take(pick(pos, rows - HALO, HALO), recv_ref, edge_ref, 0)


def unpack_high_kernel(recv_ref, pos_ref, high_ref, small_hbm, small_ref, mixed_ref, sem):
    groups = recv_ref.shape[0]
    half = CAP // 2
    rows = high_ref.shape[0] - HALO
    small = recv_ref[:, ROWS_SENT - half :, :].astype(F32)
    mixed_ref[...] = small.reshape(groups * half, LANES).astype(BF)
    codes = small[:, 0, :].astype(BF)
    lane = iota((1, groups * half), 1)
    first = places(codes, groups, lane % half, lane // half, groups * half)
    second = places(codes, groups, lane % half + half, lane // half, groups * half)
    mixed = mixed_ref[...]
    values = mm(pick(first, 0, 2 * rows), mixed)
    turned = pltpu.roll(mm(pick(second, 0, 2 * rows), mixed), LANES // 2, 1)
    valid = iota((2 * rows, LANES), 1) < SMALL_END
    small_ref[...] = jnp.where(valid, values + turned, 0.0).astype(BF)
    put = fetch(small_ref, small_hbm, sem)
    high_ref[:HALO] = jnp.zeros((HALO, high_ref.shape[1]), BF)
    take(pick(pos_ref[...], rows, rows), recv_ref, high_ref, HALO)
    put.wait()


def unpack(recv, width, rows):
    groups = recv.shape[0]
    slots = groups * CAP
    low, edge, pos = pl.pallas_call(
        unpack_low_kernel,
        in_specs=vmem(1),
        out_specs=vmem(3),
        out_shape=[
            jax.ShapeDtypeStruct((rows // 2, width), BF),
            jax.ShapeDtypeStruct((HALO, width), BF),
            jax.ShapeDtypeStruct((1, slots), jnp.int32),
        ],
        name="unpack_low",
        **params(12, rows * slots * width, 3 * rows * width),
    )(recv)
    high, small = pl.pallas_call(
        unpack_high_kernel,
        in_specs=vmem(2),
        out_specs=vmem(1) + hbm(1),
        out_shape=[
            jax.ShapeDtypeStruct((rows // 2 + HALO, width), BF),
            pltpu.HBM((rows, LANES), BF),
        ],
        scratch_shapes=[
            pltpu.VMEM((rows, LANES), BF),
            pltpu.VMEM((slots // 2, LANES), BF),
            pltpu.SemaphoreType.DMA,
        ],
        name="unpack_high",
        **params(12, rows * slots * width, 3 * rows * width),
    )(recv, pos)
    return low, edge, high, small


def conv_silu(ext, weight, bias, rel, rows):
    total = jnp.zeros((rows, ext.shape[1]), F32) + bias
    taps = weight.shape[0]
    for tap in range(taps):
        lag = taps - 1 - tap
        shifted = ext[HALO - lag : HALO - lag + rows]
        total = total + jnp.where(rel >= lag, weight[tap : tap + 1] * shifted, 0.0)
    return jax.nn.silu(total).astype(BF)


def head_spread(tile, first):
    per = TILE // HD
    return as_bf(iota((128, TILE), 0) == first + per * tile + iota((128, TILE), 1) // HD)


def piece_tiles(dest):
    base = dest // 2 * 5
    first = (base, base + 1) if dest % 2 == 0 else (base + 3, base + 4)
    return first + (base + 2,)


def near_kernel(
    me_ref, low0, low1, low3, high0, high1, high3, w_hbm, wbc_hbm,
    total_ref, far_ref, xe_ref, w_ref, gets,
):
    half, width = low0.shape
    inner = w_hbm.shape[1]
    copies = []
    for at, turn in enumerate((0, 1, 3, 2)):
        owner = lax.rem(me_ref[0] + 4 - turn, 4)
        lines = pl.ds(pl.multiple_of(owner * width, width), width)
        target = w_ref.at[pl.ds(at * width, width)] if at < 3 else far_ref
        copies.append(
            fetch(w_hbm.at[lines], target.at[:, pl.ds(0, inner)], gets.at[at, 0])
        )
        copies.append(
            fetch(
                wbc_hbm.at[lines],
                target.at[:, pl.ds(inner, wbc_hbm.shape[1])],
                gets.at[at, 1],
            )
        )
    for at, (low, high) in enumerate(((low0, high0), (low1, high1), (low3, high3))):
        columns = slice(at * width, (at + 1) * width)
        xe_ref[:HALO, columns] = high[:HALO]
        xe_ref[HALO : HALO + half, columns] = low[...]
        xe_ref[HALO + half :, columns] = high[HALO:]
    for copy in copies:
        copy.wait()

    def body(tile, _):
        columns = pl.ds(pl.multiple_of(tile * TILE, TILE), TILE)
        total_ref[:, columns] = mm(xe_ref[...], w_ref[:, columns])
        return 0

    lax.fori_loop(0, total_ref.shape[1] // TILE, body, 0)


def project_near(me, lows, highs, w_x, w_bc):
    half, width = lows[0].shape
    rows = 2 * half + HALO
    full = w_x.shape[1] + w_bc.shape[1]
    return pl.pallas_call(
        near_kernel,
        in_specs=[pl.BlockSpec(memory_space=pltpu.SMEM)] + vmem(6) + hbm(2),
        out_specs=vmem(2),
        out_shape=[pltpu.VMEM((rows, full), F32), pltpu.VMEM((width, full), BF)],
        scratch_shapes=[
            pltpu.VMEM((rows, 3 * width), BF),
            pltpu.VMEM((3 * width, full), BF),
            pltpu.SemaphoreType.DMA((4, 2)),
        ],
        name="project_near",
        **params(24, 6 * rows * width * full, 8_000_000),
    )(me, *[near(x) for x in (*lows, *highs)], far(w_x), far(w_bc))


def front_kernel(
    low_ref, high_ref, total_ref, w_ref, rel_ref,
    small_hbm, cx_hbm, bx_hbm, cb_hbm, bb_hbm,
    conv_hbm, sent_ref, mid_hbm, in_hbm, outmap_hbm,
    small_ref, cx_ref, bx_ref, cb_ref, bb_ref,
    conv_ref, mid_ref, in_ref, outmap_ref,
    xe_ref, state_ref, gain_ref, gets, puts,
):
    half, width = low_ref.shape
    rows = 2 * half
    states = in_ref.shape[1]
    tiles = conv_ref.shape[0]
    inner = tiles * TILE
    rest = [
        fetch(source, target, gets.at[at])
        for at, (source, target) in enumerate(
            (
                (small_hbm, small_ref), (cx_hbm, cx_ref), (bx_hbm, bx_ref),
                (cb_hbm, cb_ref), (bb_hbm, bb_ref),
            )
        )
    ]
    xe_ref[:HALO] = high_ref[:HALO]
    xe_ref[HALO : HALO + half] = low_ref[...]
    xe_ref[HALO + half :] = high_ref[HALO:]

    def project(columns):
        total = total_ref[:, columns] + mm(xe_ref[...], w_ref[:, columns])
        return total.astype(BF).astype(F32)

    def tile_columns(tile):
        return pl.ds(pl.multiple_of(tile * TILE, TILE), TILE)

    rel = rel_ref[...]
    ext = project(slice(inner, inner + 2 * states))
    for copy in rest:
        copy.wait()
    both = conv_silu(ext, cb_ref[...], bb_ref[...], rel, rows)
    in_ref[...] = both[:, :states]
    outmap_ref[...] = both[:, states:]
    put_maps = [
        fetch(in_ref, in_hbm, puts.at[0]), fetch(outmap_ref, outmap_hbm, puts.at[1])
    ]

    def finish(tile):
        columns = tile_columns(tile)
        rel = rel_ref[...]
        ext = project(columns)
        inner = conv_silu(ext, cx_ref[:, columns], bx_ref[:, columns], rel, rows)
        conv_ref[tile] = inner
        pltpu.make_async_copy(
            conv_ref.at[tile], conv_hbm.at[:, columns], puts.at[2 + tile]
        ).start()
        small = small_ref[...]
        steps = mm(small, head_spread(tile, 0))
        decays = mm(small, head_spread(tile, DECAY_AT)).astype(BF)
        inject = (inner.astype(F32) * steps).astype(BF).astype(F32)
        ones = lower_ones(BLK)
        carried, reach = None, None
        for block in range(rows // BLK):
            span = slice(block * BLK, (block + 1) * BLK)
            cumulative = mm(ones, decays[span])
            last = rel[(block + 1) * BLK - 1 : (block + 1) * BLK]
            end = cumulative[BLK - 1 : BLK]
            behind = BLK - 1 - iota((BLK, 1), 0)
            decayed = jnp.where(
                behind <= last, jnp.exp(end - cumulative) * inject[span], 0.0
            ).astype(BF)
            block_state = mm_tn(in_ref[span], decayed)
            carry = jnp.where(last > BLK - 1, jnp.exp(end), 0.0)
            if carried is None:
                carried, reach = block_state, carry
                mid_ref[:, columns] = carried.astype(BF)
            else:
                carried = carry * carried + block_state
                reach = reach * carry
        state_ref[:, columns] = carried
        gain_ref[:, columns] = jnp.broadcast_to(reach, (8, TILE))

    def body(tile, _):
        finish(tile)
        return 0

    lax.fori_loop(0, tiles, body, 0)
    put_mid = fetch(mid_ref, mid_hbm, puts.at[2 + tiles])

    lines = states // 8

    def tile_of(index):
        column, line = index // lines, index % lines
        return state_ref[line * 8 : line * 8 + 8, column * LANES : (column + 1) * LANES]

    def codes_of(column):
        gain = gain_ref[0:1, column * LANES : (column + 1) * LANES]
        high = gain.astype(BF).astype(F32)
        return high, gain - high

    for dest in range(sent_ref.shape[0]):
        first, second, shared = piece_tiles(dest)
        columns = [index // lines for index in (first, second, shared)]
        middle = tile_of(shared)[4 * (dest % 2) : 4 * (dest % 2) + 4]
        piece = [tile_of(first), tile_of(second), middle]
        piece += [*codes_of(min(columns)), *codes_of(max(columns))]
        sent_ref[dest] = jnp.concatenate(piece, axis=0).astype(BF)
    put_mid.wait()
    for copy in put_maps:
        copy.wait()
    for tile in range(tiles):
        pltpu.make_async_copy(
            conv_ref.at[tile], conv_hbm.at[:, pl.ds(tile * TILE, TILE)], puts.at[2 + tile]
        ).wait()


def front(low, high, total, w_far, small, rel, conv_x, bias_x, conv_bc, bias_bc, groups):
    half, width = low.shape
    rows = 2 * half
    inner = conv_x.shape[1]
    states = conv_bc.shape[1] // 2
    tiles = inner // TILE
    return pl.pallas_call(
        front_kernel,
        in_specs=vmem(5) + hbm(5),
        out_specs=hbm(1) + vmem(1) + hbm(3),
        out_shape=[
            pltpu.HBM((rows, inner), BF),
            jax.ShapeDtypeStruct((groups, PIECE, LANES), BF),
            pltpu.HBM((states, inner), BF),
            pltpu.HBM((rows, states), BF),
            pltpu.HBM((rows, states), BF),
        ],
        scratch_shapes=[
            pltpu.VMEM(small.shape, BF),
            pltpu.VMEM(conv_x.shape, F32),
            pltpu.VMEM(bias_x.shape, F32),
            pltpu.VMEM(conv_bc.shape, F32),
            pltpu.VMEM(bias_bc.shape, F32),
            pltpu.VMEM((tiles, rows, TILE), BF),
            pltpu.VMEM((states, inner), BF),
            pltpu.VMEM((rows, states), BF),
            pltpu.VMEM((rows, states), BF),
            pltpu.VMEM((rows + HALO, width), BF),
            pltpu.VMEM((states, inner), F32),
            pltpu.VMEM((8, inner), F32),
            pltpu.SemaphoreType.DMA((5,)),
            pltpu.SemaphoreType.DMA((tiles + 3,)),
        ],
        name="front",
        **params(20, 2 * rows * width * (inner + 2 * states), 12_000_000),
    )(
        *[near(x) for x in (low, high, total, w_far, rel)],
        *[far(x) for x in (small, conv_x, bias_x, conv_bc, bias_bc)],
    )


def inner_kernel(
    rel_ref, skip_ref, small_hbm, in_hbm, outmap_hbm, conv_hbm, mid_hbm, part_hbm, codes_hbm,
    small_ref, in_ref, outmap_ref, conv_ref, mid_ref, part_ref, codes_ref,
    scores_ref, across_ref, gets, puts,
):
    gets = [
        fetch(source, target, gets.at[at])
        for at, (source, target) in enumerate(
            (
                (small_hbm, small_ref), (in_hbm, in_ref), (outmap_hbm, outmap_ref),
                (conv_hbm, conv_ref), (mid_hbm, mid_ref),
            )
        )
    ]
    for copy in gets:
        copy.wait()
    rows, inner = conv_ref.shape
    tiles = inner // TILE
    per = TILE // HD
    ones = lower_ones(BLK)
    before = None
    for block in range(rows // BLK):
        span = slice(block * BLK, (block + 1) * BLK)
        scores = mm_nt(outmap_ref[span], in_ref[span])
        gap = iota((BLK, BLK), 0) - iota((BLK, BLK), 1)
        keep = (gap >= 0) & (gap <= rel_ref[span])
        scores_ref[block] = jnp.where(keep, scores, 0.0)
        so_far = mm(ones, small_ref[span])
        across_ref[block] = so_far.T
        if block > 0:
            so_far = so_far + before
        before = so_far[BLK - 1 : BLK]
        lane = iota((BLK, LANES), 1)
        reached = (iota((BLK, LANES), 0) + block * BLK < rel_ref[span]) & (
            (lane >= DECAY_AT) & (lane < SMALL_END)
        )
        gain = jnp.where(reached, jnp.exp(jnp.where(reached, so_far, 0.0)), 0.0)
        high = gain.astype(BF)
        codes_ref[0, span] = high
        codes_ref[1, span] = (gain - high.astype(F32)).astype(BF)
    put_codes = fetch(codes_ref, codes_hbm, puts.at[tiles])

    def body(tile, _):
        columns = pl.ds(pl.multiple_of(tile * TILE, TILE), TILE)
        small = small_ref[...]
        steps = mm(small, head_spread(tile, 0))
        decays = mm(small, head_spread(tile, DECAY_AT)).astype(BF)
        conv = conv_ref[:, columns].astype(F32)
        inject = (conv * steps).astype(BF)
        lane_head = iota((BLK, TILE), 1) // HD
        for block in range(rows // BLK):
            span = slice(block * BLK, (block + 1) * BLK)
            cumulative = mm(ones, decays[span])
            scores = scores_ref[block]
            total = skip_ref[:, columns] * conv[span]
            if block > 0:
                enter = jnp.where(
                    iota((BLK, 1), 0) < rel_ref[span], jnp.exp(cumulative), 0.0
                )
                total = total + enter * mm(outmap_ref[span], mid_ref[:, columns])
            for q in range(per):
                down = cumulative[:, q * HD : q * HD + 1]
                across = across_ref[block, pl.ds(DECAY_AT + per * tile + q, 1), :]
                weights = (scores * jnp.exp(jnp.minimum(down - across, 0.0))).astype(BF)
                mine = jnp.where(lane_head == q, inject[span], jnp.zeros((), BF))
                total = total + mm(weights, mine)
            part_ref[tile, span] = total
        pltpu.make_async_copy(
            part_ref.at[tile], part_hbm.at[tile], puts.at[tile]
        ).start()
        return 0

    lax.fori_loop(0, tiles, body, 0)
    put_codes.wait()
    for tile in range(tiles):
        pltpu.make_async_copy(part_ref.at[tile], part_hbm.at[tile], puts.at[tile]).wait()


def inner_part(small, rel, input_map, output_map, conv, mid, skip_wide):
    rows, inner = conv.shape
    blocks = rows // BLK
    tiles = inner // TILE
    return pl.pallas_call(
        inner_kernel,
        in_specs=vmem(2) + hbm(5),
        out_specs=hbm(2),
        out_shape=[
            pltpu.HBM((tiles, rows, TILE), F32),
            pltpu.HBM((2, rows, LANES), BF),
        ],
        scratch_shapes=[
            pltpu.VMEM(small.shape, BF),
            pltpu.VMEM(input_map.shape, BF),
            pltpu.VMEM(output_map.shape, BF),
            pltpu.VMEM(conv.shape, BF),
            pltpu.VMEM(mid.shape, BF),
            pltpu.VMEM((tiles, rows, TILE), F32),
            pltpu.VMEM((2, rows, LANES), BF),
            pltpu.VMEM((blocks, BLK, BLK), F32),
            pltpu.VMEM((blocks, 128, BLK), F32),
            pltpu.SemaphoreType.DMA((5,)),
            pltpu.SemaphoreType.DMA((tiles + 1,)),
        ],
        name="inner_part",
        **params(24, 8 * rows * BLK * inner, 8_000_000),
    )(rel, skip_wide, *[far(x) for x in (small, input_map, output_map, conv, mid)])


def scan_kernel(lines, me_ref, recv_ref, out_ref):
    groups = recv_ref.shape[0]
    me = me_ref[0]
    base = me // 2 * 5
    odd = lax.rem(me, 2)
    columns = [(base + 3 * odd) // lines, (base + 1 + 3 * odd) // lines, (base + 2) // lines]
    least = jnp.minimum(jnp.minimum(columns[0], columns[1]), columns[2])
    near_first = [
        jnp.where(jnp.full((8, LANES), column, jnp.int32) == least, 1.0, 0.0) for column in columns
    ]

    def body(shard, state):
        piece = recv_ref[shard].astype(F32)
        out_ref[shard] = jnp.concatenate(state, axis=0).astype(BF)
        gain_a = piece[20:21] + piece[21:22]
        gain_b = piece[22:23] + piece[23:24]
        return tuple(
            jnp.where(first > 0.5, gain_a, gain_b) * old + piece[8 * at : 8 * at + 8]
            for at, (first, old) in enumerate(zip(near_first, state))
        )

    lax.fori_loop(0, groups, body, (jnp.zeros((8, LANES), F32),) * 3, unroll=4)


def scan_shards(me, recv, lines):
    return pl.pallas_call(
        functools.partial(scan_kernel, lines),
        in_specs=[pl.BlockSpec(memory_space=pltpu.SMEM)] + vmem(1),
        out_specs=pl.BlockSpec(memory_space=pltpu.VMEM),
        out_shape=jax.ShapeDtypeStruct(recv.shape, BF),
        name="scan_shards",
        **params(8, 10_000_000, 800_000),
    )(me, recv)


def final_kernel(
    recv_ref, outmap_hbm, codes_hbm, part_hbm, out_hbm,
    outmap_ref, codes_ref, part_ref, held_ref, gets, puts,
):
    tiles, rows = part_ref.shape[0], part_ref.shape[1]
    states = outmap_ref.shape[1]
    lines = states // 8
    get_map = fetch(outmap_hbm, outmap_ref, gets.at[tiles])
    get_codes = fetch(codes_hbm, codes_ref, gets.at[tiles + 1])
    get_parts = [
        fetch(part_hbm.at[tile], part_ref.at[tile], gets.at[tile]) for tile in range(tiles)
    ]
    where = {}
    for dest in range(recv_ref.shape[0]):
        first, second, shared = piece_tiles(dest)
        where[first] = (dest, 0)
        where[second] = (dest, 1)
        where.setdefault(shared, dest)

    def tile_of(index):
        if isinstance(where[index], tuple):
            dest, at = where[index]
            return recv_ref[dest].astype(F32)[8 * at : 8 * at + 8]
        dest = where[index]
        upper = recv_ref[dest].astype(F32)[16:20]
        lower = recv_ref[dest + 1].astype(F32)[16:20]
        return jnp.concatenate([upper, lower], axis=0)

    def column_of(column):
        parts = [tile_of(column * lines + line) for line in range(lines)]
        return jnp.concatenate(parts, axis=0).astype(BF)

    get_map.wait()
    get_codes.wait()
    copies = []
    for tile in range(tiles):
        per = TILE // LANES
        entering = jnp.concatenate([column_of(tile * per + at) for at in range(per)], axis=1)
        outer = mm(outmap_ref[...], entering)
        spread = head_spread(tile, DECAY_AT)
        gain = mm(codes_ref[0], spread) + mm(codes_ref[1], spread)
        get_parts[tile].wait()
        held_ref[tile] = (part_ref[tile] + gain * outer).astype(BF)
        copies.append(
            fetch(held_ref.at[tile], out_hbm.at[:, pl.ds(tile * TILE, TILE)], puts.at[tile])
        )
    for copy in copies:
        copy.wait()


def final(output_map, part, codes, recv):
    tiles, rows, _ = part.shape
    return pl.pallas_call(
        final_kernel,
        in_specs=vmem(1) + hbm(3),
        out_specs=pl.BlockSpec(memory_space=pltpu.HBM),
        out_shape=jax.ShapeDtypeStruct((rows, tiles * TILE), BF),
        scratch_shapes=[
            pltpu.VMEM(output_map.shape, BF),
            pltpu.VMEM(codes.shape, BF),
            pltpu.VMEM(part.shape, F32),
            pltpu.VMEM((tiles, rows, TILE), BF),
            pltpu.SemaphoreType.DMA((tiles + 2,)),
            pltpu.SemaphoreType.DMA((tiles,)),
        ],
        name="final",
        **params(16, 2 * rows * 128 * tiles * TILE, 5_000_000),
    )(near(recv), far(output_map), far(codes), far(part))


def on_device(tokens, dt_decay, dest, lengths, w_x, w_bc, conv_x, conv_bc, bias_x, bias_bc, skip):
    rows, width = tokens.shape
    groups = lax.axis_size("ctx")
    ring = lax.axis_size("head")
    first_pos = lax.axis_index("ctx") * rows

    sent = pack(dest[None, :], tokens, jnp.transpose(dt_decay, (2, 1, 0)), groups)
    arrived = lax.all_to_all(sent, "ctx", split_axis=0, concat_axis=0, tiled=True)
    low, edge, high, small = unpack(arrived, width, rows)

    def turned(x, by):
        return lax.ppermute(x, "head", [(i, (i + by) % ring) for i in range(ring)])

    low_left, low_right = turned(low, 1), turned(low, ring - 1)
    halo = lax.ppermute(edge, "ctx", [(i, i + 1) for i in range(groups - 1)])
    high = lax.dynamic_update_slice(high, halo, (0, 0))
    high_left, high_right = turned(high, 1), turned(high, ring - 1)
    low_far, high_far = turned(low_left, 1), turned(high_right, ring - 1)

    starts = jnp.cumsum(lengths) - lengths
    positions = first_pos + jnp.arange(rows, dtype=jnp.int32)
    doc_start = jnp.max(
        jnp.where(starts[None, :] <= positions[:, None], starts[None, :], 0), axis=1
    )
    rel = (positions - doc_start)[:, None]
    me = lax.axis_index("head").astype(jnp.int32)[None]
    total, w_far = project_near(
        me, [low, low_left, low_right], [high, high_left, high_right], w_x, w_bc
    )
    conv, state, mid, input_map, output_map = front(
        low_far, high_far, total, w_far, small, rel,
        conv_x, bias_x[None, :], conv_bc, bias_bc[None, :], groups,
    )
    gathered = lax.all_to_all(state, "ctx", split_axis=0, concat_axis=0, tiled=True)
    part, gain = inner_part(
        small, rel, input_map, output_map, conv, mid, jnp.repeat(skip, HD)[None, :]
    )
    gathered, part = lax.optimization_barrier((gathered, part))
    spot = lax.axis_index("ctx").astype(jnp.int32)[None]
    entering = scan_shards(spot, gathered, input_map.shape[1] // 8)
    enter = lax.all_to_all(entering, "ctx", split_axis=0, concat_axis=0, tiled=True)
    return final(output_map, part, gain, enter)


def solution(mesh):
    in_specs = (
        P("ctx", "head"),
        P("ctx", None, "head"),
        P("ctx"),
        P(),
        P(None, "head"),
        P(),
        P(None, "head"),
        P(),
        P("head"),
        P(),
        P("head"),
    )
    out_specs = P("ctx", "head")
    return jax.shard_map(
        on_device, mesh=mesh, in_specs=in_specs, out_specs=out_specs, check_vma=False
    )
```

time: 490 us -> 149 us (0.30)
  waiting for transfers between devices: 175 us -> 17.2 us
  other arithmetic: 97.2 us -> 0.54 us
  local copies, waits for them, and re-layouts: 81.8 us -> 1.04 us
  Pallas kernels: 0 us -> 38.3 us
  matrix products: 34.8 us -> 0 us
  blocking collectives: 43.3 us -> 70.5 us
  between operations: 16.6 us -> 0.32 us
  starting transfers between devices: 34.7 us -> 20.5 us
    all_gather x2 -> x0, waiting for transfers between devices: 108 us -> none  [the longest x1 108 us: entering_2(): pieces = jax.tree.map(lambda part: lax.all_gather(part, axis), value)]
    select_n x67 -> x0, other arithmetic: 79.3 us -> none  [the longest x63 77.4 us: turn(): jnp.where(position < mine, new, old)]
    all_to_all x0 -> x2, blocking collectives: none -> 70.5 us  [the longest x1 49.9 us: on_device(): lax.all_to_all(sent, 'ctx', split_axis=0, concat_axis=0, tiled=True)]
    all_to_all x4 -> x1, waiting for transfers between devices: 65.9 us -> 5.86 us  [on_device(): lax.all_to_all(state, 'ctx', split_axis=0, concat_axis=0, tiled=True)]
    all_gather x1 -> x0, blocking collectives: 43.3 us -> none  [entering_2(): pieces = jax.tree.map(lambda part: lax.all_gather(part, axis), value)]
    mul x63 -> x0, local copies, waits for them, and re-layouts: 43.3 us -> none  [combine(): later[0][:, None, None] * earlier[1] + later[1]]
    pallas_call x0 -> x8, Pallas kernels: none -> 38.3 us  [the longest x1 10.3 us: front(): pl.pallas_call(front_kernel, in_specs=vmem(5) + hbm(5), out_specs=hbm(1)...]
    dot_general x14 -> x0, matrix products: 34.8 us -> none  [the longest x3 14.8 us: into_slots(): jnp.dot(send_select, payload, preferred_element_type=jnp.float32)]
  transfers between devices with their start and end apart: 8 -> 8, of which waited for: 6 -> 4; matrix products, arithmetic and copies ran while one was open for 15% -> 1% of each run, Pallas kernels for 0% -> 12%
where the time goes in v3:
time: 149 us; the launch traced here: 148 us
  blocking collectives  70.5 us (47%)
  Pallas kernels  38.3 us (26%)
  starting transfers between devices  20.5 us (14%)
  waiting for transfers between devices  17.2 us (12%)
    all_to_all x1, blocking collectives, on_device(): lax.all_to_all(sent, 'ctx', split_axis=0, concat_axis=0, tiled=True)  49.9 us
    all_to_all x1, blocking collectives, on_device(): lax.all_to_all(entering, 'ctx', split_axis=0, concat_axis=0, tiled=True)  20.6 us
    ppermute x6, waiting for transfers between devices, turned(): return lax.ppermute(x, 'head', [(i, (i + by) % ring) for i in range(ring)])  11.3 us
    pallas_call x1, Pallas kernels, front(): pl.pallas_call(front_kernel, in_specs=vmem(5) + hbm(5), out_specs=hbm(1)...  10.3 us
    all_to_all x1, starting transfers between devices, on_device(): lax.all_to_all(state, 'ctx', split_axis=0, concat_axis=0, tiled=True)  9.37 us
    pallas_call x1, Pallas kernels, inner_part(): pl.pallas_call(inner_kernel, in_specs=vmem(2) + hbm(5), out_specs=hbm(2),...  8.58 us
    ppermute x6, starting transfers between devices, turned(): return lax.ppermute(x, 'head', [(i, (i + by) % ring) for i in range(ring)])  7.99 us
    pallas_call x1, Pallas kernels, project_near(): pl.pallas_call(near_kernel, in_specs=[pl.BlockSpec(memory_space=pltpu.SME...  7.72 us
  transfers between devices with their start and end apart: 8, of which 4 were waited for; matrix products, arithmetic and copies ran while one was open for 1% of the time, Pallas kernels for 12%

profile of v3, /device:TPU:1, one launch (start us, length us, event | category | flops | bytes accessed | tf_op | source)
XLA Modules:
  0.0 148.4 jit_solution(989140981053022218)
XLA Ops:
  0.0 4.4 %pack.1 = bf16[64,88,128]{2,1,0:T(8,128)(2,1)S(1)} custom-call(s32[1,512]{1,0:T(1,128)} %bitcast.11, bf16[20,2,512]{2,1,0:T(2,128)(2,1)} %bitcast.10, bf16[512,640]{1,0:T(8,128)(2,1)} %tok_hbm.1), custom_call_target="tpu_custom_call" | custom-call | flops 805306368 | bytes 1310720 | tf_op jit(solution)/shard_map/pack/pallas_call | solution.py:138
  4.4 49.9 %all_to_all.15.recv_ref = bf16[64,88,128]{2,1,0:T(8,128)(2,1)S(1)} all-to-all(bf16[64,88,128]{2,1,0:T(8,128)(2,1)S(1)} %pack.1), channel_id=1, replica_groups=mesh['ctx'=64,'head'=4] {'ctx'}, dimensions={0} | all-to-all | bytes 2883584 | tf_op jit(solution)/shard_map/all_to_all | solution.py:699
  54.3 1.2 unpack_low.1
  55.5 3.1 %collective-permute-start.2 = (bf16[16,640]{1,0:T(8,128)(2,1)S(1)}, bf16[16,640]{1,0:T(8,128)(2,1)S(1)}, u32[]{:S(2)}, u32[]{:S(2)}) collective-permute-start(bf16[16,640]{1,0:T(8,128)(2,1)S(1)} %get-tuple-element.24), channel_id=1, source_target_pairs={{0,4},{4,8},{8,12},{12,16},{16,20},{20,24},{24,28},{28,32},{32,36}... | collective-permute-start | bytes 61448 | tf_op jit(solution)/shard_map/ppermute | solution.py:706
  58.6 1.3 unpack_high.1
  59.9 2.6 %collective-permute-start.3 = (bf16[272,640]{1,0:T(8,128)(2,1)S(1)}, bf16[272,640]{1,0:T(8,128)(2,1)S(1)}, u32[]{:S(2)}, u32[]{:S(2)}) collective-permute-start(bf16[272,640]{1,0:T(8,128)(2,1)S(1)} %constant_dynamic-update-slice_fusion.high0), channel_id=1, source_target_pairs={{0,3},{1,0},{2,1},{3,2},{4,7},{5,4},{6,5},{7,6},{8,11},{9,8},{10,9... | collective-permute-start | bytes 1044488 | tf_op jit(solution)/shard_map/ppermute | solution.py:703
  62.5 0.1 copy.15
  62.6 0.2 reduce-window.9
  62.9 2.8 %collective-permute-start.5 = (bf16[256,640]{1,0:T(8,128)(2,1)S(1)}, bf16[256,640]{1,0:T(8,128)(2,1)S(1)}, u32[]{:S(2)}, u32[]{:S(2)}) collective-permute-start(bf16[256,640]{1,0:T(8,128)(2,1)S(1)} %get-tuple-element.21.low0), channel_id=1, source_target_pairs={{0,3},{1,0},{2,1},{3,2},{4,7},{5,4},{6,5},{7,6},{8,11},{9,8},{10,9... | collective-permute-start | bytes 983048 | tf_op jit(solution)/shard_map/ppermute | solution.py:703
  65.7 0.2 select_reduce_fusion
  65.9 0.1 copy.16
  66.1 7.2 %collective-permute-done.low1 = bf16[256,640]{1,0:T(8,128)(2,1)S(1)} collective-permute-done((bf16[256,640]{1,0:T(8,128)(2,1)S(1)}, bf16[256,640]{1,0:T(8,128)(2,1)S(1)}, u32[]{:S(2)}, u32[]{:S(2)}) %collective-permute-start) | collective-permute-done | bytes 327712 | tf_op jit(solution)/shard_map/ppermute | solution.py:703
  73.3 2.7 %collective-permute-start.4 = (bf16[272,640]{1,0:T(8,128)(2,1)S(1)}, bf16[272,640]{1,0:T(8,128)(2,1)S(1)}, u32[]{:S(2)}, u32[]{:S(2)}) collective-permute-start(bf16[272,640]{1,0:T(8,128)(2,1)S(1)} %collective-permute-done.3.high3), channel_id=1, source_target_pairs={{0,3},{1,0},{2,1},{3,2},{4,7},{5,4},{6,5},{7,6},{8,11},{9,8},{10,9... | collective-permute-start | bytes 1044488 | tf_op jit(solution)/shard_map/ppermute | solution.py:703
  76.0 0.6 broadcast_in_dim.36.bx_hbm
  76.6 0.9 collective-permute-done.5.low3
  77.5 3.2 %collective-permute-done.6.high1 = bf16[272,640]{1,0:T(8,128)(2,1)S(1)} collective-permute-done((bf16[272,640]{1,0:T(8,128)(2,1)S(1)}, bf16[272,640]{1,0:T(8,128)(2,1)S(1)}, u32[]{:S(2)}, u32[]{:S(2)}) %collective-permute-start.6) | collective-permute-done | bytes 348192 | tf_op jit(solution)/shard_map/ppermute | solution.py:703
  80.7 7.7 %project_near.1 = (f32[528,1536]{1,0:T(8,128)S(1)}, bf16[640,1536]{1,0:T(8,128)(2,1)S(1)}) custom-call(s32[1]{0:T(128)} %bitcast.3.me_ref, bf16[256,640]{1,0:T(8,128)(2,1)S(1)} %get-tuple-element.21.low0, bf16[256,640]{1,0:T(8,128)(2,1)S(1)} %collective-permute-done.low1, bf16[256,640]{1,0:T(8,128)(2,1)S(1)} %collective-permute-done.5.low3, ...), custom_call_target="tpu_custom_call" | custom-call | flops 3114270720 | bytes 8000000 | tf_op jit(solution)/shard_map/project_near/pallas_call | solution.py:310
  88.5 10.3 %front.1 = (bf16[512,1280]{1,0:T(8,128)(2,1)}, bf16[64,24,128]{2,1,0:T(8,128)(2,1)}, bf16[128,1280]{1,0:T(8,128)(2,1)}, bf16[512,128]{1,0:T(8,128)(2,1)}, bf16[512,128]{1,0:T(8,128)(2,1)}) custom-call(bf16[256,640]{1,0:T(8,128)(2,1)S(1)} %collective-permute-done.1.low_ref, bf16[272,640]{1,0:T(8,128)(2,1)S(1)} %collective-permute-done.4.high_ref, ...), custom_call_target="tpu_custom_call" | custom-call | flops 1006632960 | bytes 12000000 | tf_op jit(solution)/shard_map/front/pallas_call | solution.py:444
  98.7 9.4 %all-to-all-start.1 = ((bf16[64,24,128]{2,1,0:T(8,128)(2,1)}), bf16[64,24,128]{2,1,0:T(8,128)(2,1)S(1)}, u32[]{:S(2)}, u32[]{:S(2)}) async-start(bf16[64,24,128]{2,1,0:T(8,128)(2,1)} %get-tuple-element.28), calls=%async_computation.1 | async-start | bytes 786432 | tf_op jit(solution)/shard_map/all_to_all | solution.py:725
  108.3 8.6 %inner_part.1 = (f32[5,512,256]{2,1,0:T(8,128)}, bf16[2,512,128]{2,1,0:T(8,128)(2,1)}) custom-call(s32[512,1]{1,0:T(8,128)S(1)} %add_subtract_fusion.rel_ref, f32[1,1280]{1,0:T(1,128)S(1)} %broadcast_in_dim_reshape.3.skip_ref, bf16[512,128]{1,0:T(8,128)(2,1)} %get-tuple-element.27.small_hbm, bf16[512,128]{1,0:T(8,128)(2,1)} %get-tuple-element.29.in_hbm, ...), custom_call_target="tpu_custom_call" | custom-call | flops 1342177280 | bytes 8000000 | tf_op jit(solution)/shard_map/inner_part/pallas_call | solution.py:561
  116.9 5.9 %all-to-all-done.1.recv_ref = bf16[64,24,128]{2,1,0:T(8,128)(2,1)S(1)} async-done(((bf16[64,24,128]{2,1,0:T(8,128)(2,1)}), bf16[64,24,128]{2,1,0:T(8,128)(2,1)S(1)}, u32[]{:S(2)}, u32[]{:S(2)}) %all-to-all-start.1) | async-done | bytes 393248 | tf_op jit(solution)/shard_map/all_to_all | solution.py:725
  122.7 0.2 scan_shards.1
  123.0 20.6 %all_to_all.16.recv_ref = bf16[64,24,128]{2,1,0:T(8,128)(2,1)S(1)} all-to-all(bf16[64,24,128]{2,1,0:T(8,128)(2,1)S(1)} %scan_shards.1), channel_id=1, replica_groups=mesh['ctx'=64,'head'=4] {'ctx'}, dimensions={0} | all-to-all | bytes 786432 | tf_op jit(solution)/shard_map/all_to_all | solution.py:732
  143.6 4.6 %final.1 = bf16[512,1280]{1,0:T(8,128)(2,1)} custom-call(bf16[64,24,128]{2,1,0:T(8,128)(2,1)S(1)} %all_to_all.16.recv_ref, bf16[512,128]{1,0:T(8,128)(2,1)} %get-tuple-element.30.outmap_hbm, bf16[2,512,128]{2,1,0:T(8,128)(2,1)} %get-tuple-element.35.codes_hbm, f32[5,512,256]{2,1,0:T(8,128)} %get-tuple-element.36.part_hbm), custom_call_target="tpu_custom_call" | custom-call | flops 167772160 | bytes 5000000 | tf_op jit(solution)/shard_map/final/pallas_call | solution.py:674
  (20 shorter events, 0.3 us)
Async XLA Ops:
  54.3 8.2 %copy-start.1 = (s32[128]{0:T(128)S(1)}, s32[128]{0:T(128)}, u32[]{:S(2)}) copy-start(s32[128]{0:T(128)} %param.14) | copy-start | bytes 1540
  55.5 20.5 %copy-start = (f32[1280]{0:T(1024)S(1)}, f32[1280]{0:T(1024)}, u32[]{:S(2)}) copy-start(f32[1280]{0:T(1024)} %param.19) | copy-start | bytes 15364
  55.5 4.4 %collective-permute-start.2 = (bf16[16,640]{1,0:T(8,128)(2,1)S(1)}, bf16[16,640]{1,0:T(8,128)(2,1)S(1)}, u32[]{:S(2)}, u32[]{:S(2)}) collective-permute-start(bf16[16,640]{1,0:T(8,128)(2,1)S(1)} %get-tuple-element.24), channel_id=1, source_target_pairs={{0,4},{4,8},{8,12},{12,16},{16,20},{20,24},{24,28},{28,32},{32,36}... | collective-permute-start | bytes 61448 | tf_op jit(solution)/shard_map/ppermute | solution.py:706
  59.9 13.3 %collective-permute-start.3 = (bf16[272,640]{1,0:T(8,128)(2,1)S(1)}, bf16[272,640]{1,0:T(8,128)(2,1)S(1)}, u32[]{:S(2)}, u32[]{:S(2)}) collective-permute-start(bf16[272,640]{1,0:T(8,128)(2,1)S(1)} %constant_dynamic-update-slice_fusion.high0), channel_id=1, source_target_pairs={{0,3},{1,0},{2,1},{3,2},{4,7},{5,4},{6,5},{7,6},{8,11},{9,8},{10,9... | collective-permute-start | bytes 1044488 | tf_op jit(solution)/shard_map/ppermute | solution.py:703
  62.5 10.7 %collective-permute-start = (bf16[256,640]{1,0:T(8,128)(2,1)S(1)}, bf16[256,640]{1,0:T(8,128)(2,1)S(1)}, u32[]{:S(2)}, u32[]{:S(2)}) collective-permute-start(bf16[256,640]{1,0:T(8,128)(2,1)S(1)} %get-tuple-element.21.low0), channel_id=1, source_target_pairs={{0,1},{1,2},{2,3},{3,0},{4,5},{5,6},{6,7},{7,4},{8,9},{9,10},{10,1... | collective-permute-start | bytes 983048 | tf_op jit(solution)/shard_map/ppermute | solution.py:703
  62.9 14.6 %collective-permute-start.5 = (bf16[256,640]{1,0:T(8,128)(2,1)S(1)}, bf16[256,640]{1,0:T(8,128)(2,1)S(1)}, u32[]{:S(2)}, u32[]{:S(2)}) collective-permute-start(bf16[256,640]{1,0:T(8,128)(2,1)S(1)} %get-tuple-element.21.low0), channel_id=1, source_target_pairs={{0,3},{1,0},{2,1},{3,2},{4,7},{5,4},{6,5},{7,6},{8,11},{9,8},{10,9... | collective-permute-start | bytes 983048 | tf_op jit(solution)/shard_map/ppermute | solution.py:703
  65.7 15.0 %collective-permute-start.6 = (bf16[272,640]{1,0:T(8,128)(2,1)S(1)}, bf16[272,640]{1,0:T(8,128)(2,1)S(1)}, u32[]{:S(2)}, u32[]{:S(2)}) collective-permute-start(bf16[272,640]{1,0:T(8,128)(2,1)S(1)} %constant_dynamic-update-slice_fusion.high0), channel_id=1, source_target_pairs={{0,1},{1,2},{2,3},{3,0},{4,5},{5,6},{6,7},{7,4},{8,9},{9,10},{10,1... | collective-permute-start | bytes 1044488 | tf_op jit(solution)/shard_map/ppermute | solution.py:703
  73.2 15.2 %collective-permute-start.1 = (bf16[256,640]{1,0:T(8,128)(2,1)S(1)}, bf16[256,640]{1,0:T(8,128)(2,1)S(1)}, u32[]{:S(2)}, u32[]{:S(2)}) collective-permute-start(bf16[256,640]{1,0:T(8,128)(2,1)S(1)} %collective-permute-done.low1), channel_id=1, source_target_pairs={{0,1},{1,2},{2,3},{3,0},{4,5},{5,6},{6,7},{7,4},{8,9},{9,10},{10,1... | collective-permute-start | bytes 983048 | tf_op jit(solution)/shard_map/ppermute | solution.py:703
  73.3 15.2 %collective-permute-start.4 = (bf16[272,640]{1,0:T(8,128)(2,1)S(1)}, bf16[272,640]{1,0:T(8,128)(2,1)S(1)}, u32[]{:S(2)}, u32[]{:S(2)}) collective-permute-start(bf16[272,640]{1,0:T(8,128)(2,1)S(1)} %collective-permute-done.3.high3), channel_id=1, source_target_pairs={{0,3},{1,0},{2,1},{3,2},{4,7},{5,4},{6,5},{7,6},{8,11},{9,8},{10,9... | collective-permute-start | bytes 1044488 | tf_op jit(solution)/shard_map/ppermute | solution.py:703
  88.5 19.7 %copy-start.2 = (f32[20]{0:T(128)S(1)}, f32[20]{0:T(128)}, u32[]{:S(2)}) copy-start(f32[20]{0:T(128)} %param.21) | copy-start | bytes 244
  98.7 24.0 %all-to-all-start.1 = ((bf16[64,24,128]{2,1,0:T(8,128)(2,1)}), bf16[64,24,128]{2,1,0:T(8,128)(2,1)S(1)}, u32[]{:S(2)}, u32[]{:S(2)}) async-start(bf16[64,24,128]{2,1,0:T(8,128)(2,1)} %get-tuple-element.28), calls=%async_computation.1 | async-start | bytes 786432 | tf_op jit(solution)/shard_map/all_to_all | solution.py:725

commit v4 on v3

v4 whole, which is shorter than its diff:
```python
import functools

import jax
import jax.numpy as jnp
from jax import lax
from jax.experimental import pallas as pl
from jax.experimental.pallas import tpu as pltpu
from jax.sharding import PartitionSpec as P

BF = jnp.bfloat16
F32 = jnp.float32
CAP = 16
BLK = 256
HD = 64
TILE = 256
HALO = 16
LANES = 128
ROWS_SENT = 88
DECAY_AT = 24
SMALL_END = 44
HIGH_AT, LOW_AT = 44, 108
PIECE = 24
TAKEN = 128


def iota(shape, dim):
    return lax.broadcasted_iota(jnp.int32, shape, dim)


def mm(a, b):
    return jnp.dot(a, b, preferred_element_type=F32)


def mm_nt(a, b):
    return lax.dot_general(a, b, (((1,), (1,)), ((), ())), preferred_element_type=F32)


def mm_tn(a, b):
    return lax.dot_general(a, b, (((0,), (0,)), ((), ())), preferred_element_type=F32)


def as_bf(mask):
    return jnp.where(mask, 1.0, 0.0).astype(BF)


def lower_ones(n):
    return as_bf(iota((n, n), 0) >= iota((n, n), 1))


def params(mib, flops=0, bytes_accessed=0):
    return dict(
        compiler_params=pltpu.CompilerParams(vmem_limit_bytes=mib * 1024 * 1024),
        cost_estimate=pl.CostEstimate(
            flops=flops, bytes_accessed=bytes_accessed, transcendentals=0
        ),
    )


def vmem(count):
    return [pl.BlockSpec(memory_space=pltpu.VMEM)] * count


def near(x):
    return pltpu.with_memory_space_constraint(x, pltpu.VMEM)


def far(x):
    return pltpu.with_memory_space_constraint(x, pltpu.HBM)


def hbm(count):
    return [pl.BlockSpec(memory_space=pltpu.HBM)] * count


def fetch(source, target, sem):
    copy = pltpu.make_async_copy(source, target, sem)
    copy.start()
    return copy


def pack_kernel(
    dest_hbm, steps_hbm, tok_hbm, out_ref,
    dest_ref, steps_ref, tok_ref, slot_ref, code_ref, small_ref, turned_ref, upper_ref,
    sems,
):
    get_dest = fetch(dest_hbm, dest_ref, sems.at[0])
    get_steps = fetch(steps_hbm, steps_ref, sems.at[1])
    get_tokens = fetch(tok_hbm, tok_ref, sems.at[2])
    rows, width = tok_ref.shape
    groups = code_ref.shape[0]
    heads = steps_ref.shape[0]
    per = 8
    slots = per * CAP
    upper_ref[...] = as_bf(iota((rows, rows), 0) <= iota((rows, rows), 1))
    small_ref[...] = jnp.zeros_like(small_ref)
    get_dest.wait()
    dest = dest_ref[...]
    target = dest // rows
    place = dest % rows + 1
    onehot = iota((groups, rows), 0) == target
    ranks = mm(as_bf(onehot), upper_ref[...])
    rank = jnp.sum(jnp.where(onehot, ranks, 0.0), axis=0, keepdims=True) - 1.0
    rank = rank.astype(jnp.int32)
    slot_ref[...] = target * CAP + rank
    line = iota((LANES, rows), 0)
    codes = jnp.where(line == HIGH_AT + rank, place // 256, 0)
    codes = codes + jnp.where(line == LOW_AT + rank, place % 256, 0)
    code_ref[...] = mm_nt(as_bf(onehot), codes.astype(F32).astype(BF))
    get_steps.wait()
    steps = steps_ref[...].astype(F32)
    small_ref[:heads] = steps[:, 0, :]
    small_ref[DECAY_AT : DECAY_AT + heads] = steps[:, 1, :]
    turned_ref[...] = small_ref[...].T.astype(BF)
    get_tokens.wait()

    def body(step, _):
        slot = slot_ref[...] - step * slots
        here = pl.ds(pl.multiple_of(step * per, per), per)
        select = as_bf(iota((slots, rows), 0) == slot)
        sent = mm(select, tok_ref[...]).astype(BF)
        for column in range(width // LANES):
            out_ref[here, column * CAP : (column + 1) * CAP, :] = sent[
                :, column * LANES : (column + 1) * LANES
            ].reshape(per, CAP, LANES)
        half = CAP // 2
        small = mm(select, turned_ref[...]).reshape(per, CAP, LANES)
        pairs = small[:, :half, :] + pltpu.roll(small[:, half:, :], LANES // 2, 2)
        first = iota((per, half, LANES), 1) == 0
        pairs = pairs + jnp.where(first, code_ref[here][:, None, :], 0.0)
        out_ref[here, ROWS_SENT - half :, :] = pairs.astype(BF)
        return 0

    lax.fori_loop(0, groups // per, body, 0, unroll=2)


def pack(dest, tokens, steps, groups):
    rows, width = tokens.shape
    return pl.pallas_call(
        pack_kernel,
        in_specs=hbm(3),
        out_specs=pl.BlockSpec(memory_space=pltpu.VMEM),
        out_shape=jax.ShapeDtypeStruct((groups, ROWS_SENT, LANES), BF),
        scratch_shapes=[
            pltpu.VMEM((1, rows), jnp.int32),
            pltpu.VMEM(steps.shape, BF),
            pltpu.VMEM((rows, width), BF),
            pltpu.VMEM((1, rows), jnp.int32),
            pltpu.VMEM((groups, LANES), F32),
            pltpu.VMEM((LANES, rows), F32),
            pltpu.VMEM((rows, LANES), BF),
            pltpu.VMEM((rows, rows), BF),
            pltpu.SemaphoreType.DMA((3,)),
        ],
        name="pack",
        **params(16, 2 * rows * groups * CAP * (width + LANES), 4 * rows * width),
    )(far(dest), far(steps), far(tokens))


def places(row_codes, groups, lane_slot, lane_group, count):
    line = iota((LANES, count), 0)
    table = jnp.where(
        line == HIGH_AT + lane_slot, 256.0, jnp.where(line == LOW_AT + lane_slot, 1.0, 0.0)
    ).astype(BF)
    wide = mm(row_codes, table)
    mine = iota((groups, count), 0) == lane_group
    return jnp.sum(jnp.where(mine, wide, 0.0), axis=0, keepdims=True).astype(jnp.int32)


def pick(pos, first, rows):
    return as_bf(iota((rows, pos.shape[1]), 0) + (first + 1) == pos)


def take(select, recv_ref, target, first_row):
    groups = recv_ref.shape[0]
    rows = select.shape[0]
    for column in range(target.shape[1] // LANES):
        source = recv_ref[:, column * CAP : (column + 1) * CAP, :]
        target[first_row : first_row + rows, column * LANES : (column + 1) * LANES] = mm(
            select, source.reshape(groups * CAP, LANES)
        ).astype(BF)


def paired_rows(recv_ref, rows_ref):
    groups = recv_ref.shape[0]
    half = CAP // 2
    pairs = recv_ref[:, ROWS_SENT - half :, :].astype(F32)
    both = jnp.concatenate([pairs, pltpu.roll(pairs, LANES // 2, 2)], axis=1)
    rows_ref[...] = both.reshape(groups * CAP, LANES).astype(BF)
    return pairs[:, 0, :].astype(BF)


def take_small(select, rows_ref):
    values = mm(select, rows_ref[...])
    valid = iota(values.shape, 1) < SMALL_END
    return jnp.where(valid, values, 0.0).astype(BF)


def unpack_low_kernel(
    recv_ref, low_ref, pos_ref, small_hbm, rows_ref, small_ref, sem
):
    groups = recv_ref.shape[0]
    rows = 2 * low_ref.shape[0]
    codes = paired_rows(recv_ref, rows_ref)
    lane = iota((1, groups * CAP), 1)
    pos = places(codes, groups, lane % CAP, lane // CAP, groups * CAP)
    pos_ref[...] = pos
    select = pick(pos, 0, rows // 2)
    small_ref[...] = take_small(select, rows_ref)
    put = fetch(small_ref, small_hbm, sem)
    take(select, recv_ref, low_ref, 0)
    put.wait()


def unpack_high_kernel(
    recv_ref, pos_ref, high_ref, edge_ref, small_hbm, rows_ref, small_ref, sem
):
    rows = high_ref.shape[0] - HALO
    paired_rows(recv_ref, rows_ref)
    select = pick(pos_ref[...], rows, rows)
    small_ref[...] = take_small(select, rows_ref)
    put = fetch(small_ref, small_hbm, sem)
    high_ref[:HALO] = jnp.zeros((HALO, high_ref.shape[1]), BF)
    take(select, recv_ref, high_ref, HALO)
    edge_ref[...] = high_ref[rows:]
    put.wait()


def unpack(recv, width, rows):
    groups = recv.shape[0]
    slots = groups * CAP
    half = rows // 2
    scratch = [
        pltpu.VMEM((slots, LANES), BF),
        pltpu.VMEM((half, LANES), BF),
        pltpu.SemaphoreType.DMA,
    ]
    low, pos, small_low = pl.pallas_call(
        unpack_low_kernel,
        in_specs=vmem(1),
        out_specs=vmem(2) + hbm(1),
        out_shape=[
            jax.ShapeDtypeStruct((half, width), BF),
            jax.ShapeDtypeStruct((1, slots), jnp.int32),
            pltpu.HBM((half, LANES), BF),
        ],
        scratch_shapes=scratch,
        name="unpack_low",
        **params(12, rows * slots * width, 3 * rows * width),
    )(recv)
    high, edge, small_high = pl.pallas_call(
        unpack_high_kernel,
        in_specs=vmem(2),
        out_specs=vmem(2) + hbm(1),
        out_shape=[
            jax.ShapeDtypeStruct((half + HALO, width), BF),
            jax.ShapeDtypeStruct((HALO, width), BF),
            pltpu.HBM((half, LANES), BF),
        ],
        scratch_shapes=scratch,
        name="unpack_high",
        **params(12, rows * slots * width, 3 * rows * width),
    )(recv, pos)
    return low, edge, high, (small_low, small_high)


def conv_silu(ext_ref, weight, bias, rel, rows):
    taps = weight.shape[0]
    total = bias + weight[taps - 1 : taps] * ext_ref[HALO : HALO + rows]
    for lag in range(1, taps):
        tap = taps - 1 - lag
        shifted = ext_ref[HALO - lag : HALO - lag + rows]
        total = total + jnp.where(rel >= lag, weight[tap : tap + 1] * shifted, 0.0)
    return jax.nn.silu(total).astype(BF)


def head_spread(tile, first):
    per = TILE // HD
    return as_bf(iota((128, TILE), 0) == first + per * tile + iota((128, TILE), 1) // HD)


def piece_tiles(dest):
    base = dest // 2 * 5
    first = (base, base + 1) if dest % 2 == 0 else (base + 3, base + 4)
    return first + (base + 2,)


def decay_kernel(
    rel_ref, low_hbm, high_hbm, steps_hbm, tail_hbm, carry_ref,
    small_ref, steps_ref, tail_ref, gets, puts,
):
    tiles, rows = tail_ref.shape[0], tail_ref.shape[1]
    half = rows // 2
    copies = [
        fetch(low_hbm, small_ref.at[pl.ds(0, half)], gets.at[0]),
        fetch(high_hbm, small_ref.at[pl.ds(half, half)], gets.at[1]),
    ]
    for copy in copies:
        copy.wait()
    ones = lower_ones(BLK)
    rel = rel_ref[...]

    def body(tile, _):
        small = small_ref[...]
        steps_ref[tile] = mm(small, head_spread(tile, 0)).astype(BF)
        decays = mm(small, head_spread(tile, DECAY_AT)).astype(BF)
        reach, lines = None, []
        for block in range(rows // BLK):
            span = slice(block * BLK, (block + 1) * BLK)
            cumulative = mm(ones, decays[span])
            last = rel[(block + 1) * BLK - 1 : (block + 1) * BLK]
            end = cumulative[BLK - 1 : BLK]
            behind = BLK - 1 - iota((BLK, 1), 0)
            tail_ref[tile, span] = jnp.where(behind <= last, jnp.exp(end - cumulative), 0.0)
            carry = jnp.where(last > BLK - 1, jnp.exp(end), 0.0)
            lines.append(carry)
            reach = carry if reach is None else reach * carry
        lines.append(reach)
        lines.append(jnp.zeros((8 - len(lines), TILE), F32))
        carry_ref[tile] = jnp.concatenate(lines, axis=0)
        pltpu.make_async_copy(steps_ref.at[tile], steps_hbm.at[tile], puts.at[tile]).start()
        pltpu.make_async_copy(
            tail_ref.at[tile], tail_hbm.at[tile], puts.at[tiles + tile]
        ).start()
        return 0

    lax.fori_loop(0, tiles, body, 0)
    for tile in range(tiles):
        pltpu.make_async_copy(steps_ref.at[tile], steps_hbm.at[tile], puts.at[tile]).wait()
        pltpu.make_async_copy(
            tail_ref.at[tile], tail_hbm.at[tile], puts.at[tiles + tile]
        ).wait()


def decay_factors(rel, small, inner):
    rows = rel.shape[0]
    tiles = inner // TILE
    return pl.pallas_call(
        decay_kernel,
        in_specs=vmem(1) + hbm(2),
        out_specs=hbm(2) + vmem(1),
        out_shape=[
            pltpu.HBM((tiles, rows, TILE), BF),
            pltpu.HBM((tiles, rows, TILE), F32),
            jax.ShapeDtypeStruct((tiles, 8, TILE), F32),
        ],
        scratch_shapes=[
            pltpu.VMEM((rows, LANES), BF),
            pltpu.VMEM((tiles, rows, TILE), BF),
            pltpu.VMEM((tiles, rows, TILE), F32),
            pltpu.SemaphoreType.DMA((2,)),
            pltpu.SemaphoreType.DMA((2 * tiles,)),
        ],
        name="decay_factors",
        **params(16, 4 * rows * BLK * inner, 7_000_000),
    )(rel, *[far(x) for x in small])


def assemble(xe_ref, low_ref, high_ref, columns):
    half = low_ref.shape[0]
    xe_ref[:HALO, columns] = high_ref[:HALO]
    xe_ref[HALO : HALO + half, columns] = low_ref[...]
    xe_ref[HALO + half :, columns] = high_ref[HALO:]


def own_kernel(
    me_ref, low_ref, high_ref, w_hbm, wbc_hbm,
    total_ref, left_ref, right_ref, far_ref, xe_ref, w_ref, gets,
):
    width = low_ref.shape[1]
    inner, rest = w_hbm.shape[1], wbc_hbm.shape[1]
    copies = []
    for turn, target in enumerate((w_ref, left_ref, far_ref, right_ref)):
        owner = lax.rem(me_ref[0] + 4 - turn, 4)
        lines = pl.ds(pl.multiple_of(owner * width, width), width)
        copies.append(
            (
                fetch(w_hbm.at[lines], target.at[:, pl.ds(0, inner)], gets.at[turn, 0]),
                fetch(wbc_hbm.at[lines], target.at[:, pl.ds(inner, rest)], gets.at[turn, 1]),
            )
        )
    assemble(xe_ref, low_ref, high_ref, slice(None))
    for copy in copies[0]:
        copy.wait()

    def body(tile, _):
        columns = pl.ds(pl.multiple_of(tile * TILE, TILE), TILE)
        total_ref[:, columns] = mm(xe_ref[...], w_ref[:, columns])
        return 0

    lax.fori_loop(0, total_ref.shape[1] // TILE, body, 0)
    for pair in copies[1:]:
        for copy in pair:
            copy.wait()


def project_own(me, low, high, w_x, w_bc):
    half, width = low.shape
    rows = 2 * half + HALO
    full = w_x.shape[1] + w_bc.shape[1]
    return pl.pallas_call(
        own_kernel,
        in_specs=[pl.BlockSpec(memory_space=pltpu.SMEM)] + vmem(2) + hbm(2),
        out_specs=vmem(4),
        out_shape=[pltpu.VMEM((rows, full), F32)] + [pltpu.VMEM((width, full), BF)] * 3,
        scratch_shapes=[
            pltpu.VMEM((rows, width), BF),
            pltpu.VMEM((width, full), BF),
            pltpu.SemaphoreType.DMA((4, 2)),
        ],
        name="project_own",
        **params(8, 2 * rows * width * full, 8_000_000),
    )(me, near(low), near(high), far(w_x), far(w_bc))


def near_kernel(
    low1, high1, low3, high3, left_ref, right_ref, sofar_ref, total_ref, xe_ref
):
    width = low1.shape[1]
    assemble(xe_ref, low1, high1, slice(0, width))
    assemble(xe_ref, low3, high3, slice(width, 2 * width))

    def body(tile, _):
        columns = pl.ds(pl.multiple_of(tile * TILE, TILE), TILE)
        weights = jnp.concatenate([left_ref[:, columns], right_ref[:, columns]], axis=0)
        total_ref[:, columns] = sofar_ref[:, columns] + mm(xe_ref[...], weights)
        return 0

    lax.fori_loop(0, total_ref.shape[1] // TILE, body, 0)


def project_near(left, right, w_left, w_right, total):
    width = left[0].shape[1]
    rows, full = total.shape
    return pl.pallas_call(
        near_kernel,
        in_specs=vmem(7),
        out_specs=vmem(1)[0],
        out_shape=pltpu.VMEM((rows, full), F32),
        scratch_shapes=[pltpu.VMEM((rows, 2 * width), BF)],
        name="project_near",
        **params(6, 4 * rows * width * full, 8_000_000),
    )(*[near(x) for x in (*left, *right, w_left, w_right, total)])


def piece_tiles(dest):
    base = dest // 2 * 5
    first = (base, base + 1) if dest % 2 == 0 else (base + 3, base + 4)
    return first + (base + 2,)


def front_kernel(
    low_ref, high_ref, total_ref, w_ref, rel_ref, carry_ref, cx_ref, bx_ref, cb_ref, bb_ref,
    steps_hbm, tail_hbm,
    conv_hbm, sent_ref, mid_hbm, in_hbm, outmap_hbm,
    steps_ref, tail_ref, conv_ref, mid_ref, in_ref, outmap_ref, across_ref,
    xe_ref, ext_ref, state_ref, gets, puts,
):
    half, width = low_ref.shape
    rows = 2 * half
    states = in_ref.shape[1]
    tiles = conv_ref.shape[0]
    inner = tiles * TILE
    for tile in range(tiles):
        fetch(steps_hbm.at[tile], steps_ref.at[tile], gets.at[0, tile])
        fetch(tail_hbm.at[tile], tail_ref.at[tile], gets.at[1, tile])
    assemble(xe_ref, low_ref, high_ref, slice(None))

    def project(columns):
        total = total_ref[:, columns] + mm(xe_ref[...], w_ref[:, columns])
        ext_ref[...] = total.astype(BF).astype(F32)

    rel = rel_ref[...]
    project(slice(inner, inner + 2 * states))
    both = conv_silu(ext_ref, cb_ref[...], bb_ref[...], rel, rows)
    in_ref[...] = both[:, :states]
    outmap_ref[...] = both[:, states:]
    put_maps = [
        fetch(in_ref, in_hbm, puts.at[0]), fetch(outmap_ref, outmap_hbm, puts.at[1])
    ]
    across_ref[...] = both[:, :states].astype(F32).T.astype(BF)

    def body(tile, _):
        columns = pl.ds(pl.multiple_of(tile * TILE, TILE), TILE)
        project(columns)
        inner_rows = conv_silu(ext_ref, cx_ref[:, columns], bx_ref[:, columns], rel_ref[...], rows)
        conv_ref[tile] = inner_rows
        pltpu.make_async_copy(
            conv_ref.at[tile], conv_hbm.at[:, columns], puts.at[2 + tile]
        ).start()
        for at, (source, target) in enumerate(((steps_hbm, steps_ref), (tail_hbm, tail_ref))):
            pltpu.make_async_copy(source.at[tile], target.at[tile], gets.at[at, tile]).wait()
        inject = (inner_rows.astype(F32) * steps_ref[tile].astype(F32)).astype(BF)
        decayed = (tail_ref[tile] * inject.astype(F32)).astype(BF)
        carried = None
        for block in range(rows // BLK):
            span = slice(block * BLK, (block + 1) * BLK)
            block_state = mm(across_ref[:, span], decayed[span])
            if carried is None:
                carried = block_state
                mid_ref[:, columns] = carried.astype(BF)
            else:
                carried = carry_ref[tile, block : block + 1] * carried + block_state
        state_ref[:, columns] = carried
        return 0

    lax.fori_loop(0, tiles, body, 0)
    put_mid = fetch(mid_ref, mid_hbm, puts.at[2 + tiles])
    lines = states // 8

    def tile_of(index):
        column, line = index // lines, index % lines
        return state_ref[line * 8 : line * 8 + 8, column * LANES : (column + 1) * LANES]

    def codes_of(column):
        per = TILE // LANES
        at = rows // BLK
        lanes = slice(column % per * LANES, (column % per + 1) * LANES)
        gain = carry_ref[column // per, at : at + 1, lanes]
        high = gain.astype(BF).astype(F32)
        return high, gain - high

    for dest in range(sent_ref.shape[0]):
        first, second, shared = piece_tiles(dest)
        columns = [index // lines for index in (first, second, shared)]
        middle = tile_of(shared)[4 * (dest % 2) : 4 * (dest % 2) + 4]
        piece = [tile_of(first), tile_of(second), middle]
        piece += [*codes_of(min(columns)), *codes_of(max(columns))]
        sent_ref[dest] = jnp.concatenate(piece, axis=0).astype(BF)
    put_mid.wait()
    for copy in put_maps:
        copy.wait()
    for tile in range(tiles):
        pltpu.make_async_copy(
            conv_ref.at[tile], conv_hbm.at[:, pl.ds(tile * TILE, TILE)], puts.at[2 + tile]
        ).wait()


def front(piece, total, w_far, rel, carry, steps, tail, conv_x, bias_x, conv_bc, bias_bc, groups):
    half, width = piece[0].shape
    rows = 2 * half
    inner = conv_x.shape[1]
    states = conv_bc.shape[1] // 2
    tiles = inner // TILE
    return pl.pallas_call(
        front_kernel,
        in_specs=vmem(10) + hbm(2),
        out_specs=hbm(1) + vmem(1) + hbm(3),
        out_shape=[
            pltpu.HBM((rows, inner), BF),
            jax.ShapeDtypeStruct((groups, PIECE, LANES), BF),
            pltpu.HBM((states, inner), BF),
            pltpu.HBM((rows, states), BF),
            pltpu.HBM((rows, states), BF),
        ],
        scratch_shapes=[
            pltpu.VMEM(steps.shape, BF),
            pltpu.VMEM(tail.shape, F32),
            pltpu.VMEM((tiles, rows, TILE), BF),
            pltpu.VMEM((states, inner), BF),
            pltpu.VMEM((rows, states), BF),
            pltpu.VMEM((rows, states), BF),
            pltpu.VMEM((states, rows), BF),
            pltpu.VMEM((rows + HALO, width), BF),
            pltpu.VMEM((rows + HALO, TILE), F32),
            pltpu.VMEM((states, inner), F32),
            pltpu.SemaphoreType.DMA((2, tiles)),
            pltpu.SemaphoreType.DMA((tiles + 3,)),
        ],
        name="front",
        **params(20, 2 * rows * width * (inner + 2 * states), 12_000_000),
    )(
        *[near(x) for x in (*piece, total, w_far)], rel, carry,
        conv_x, bias_x, conv_bc, bias_bc, far(steps), far(tail),
    )


def inner_kernel(
    rel_ref, skip_ref, low_hbm, high_hbm, in_hbm, outmap_hbm, conv_hbm, mid_hbm, part_hbm,
    small_ref, in_ref, outmap_ref, conv_ref, mid_ref, part_ref,
    scores_ref, across_ref, gets, puts,
):
    half = low_hbm.shape[0]
    gets = [
        fetch(source, target, gets.at[at])
        for at, (source, target) in enumerate(
            (
                (low_hbm, small_ref.at[pl.ds(0, half)]),
                (high_hbm, small_ref.at[pl.ds(half, half)]),
                (in_hbm, in_ref), (outmap_hbm, outmap_ref),
                (conv_hbm, conv_ref), (mid_hbm, mid_ref),
            )
        )
    ]
    for copy in gets:
        copy.wait()
    rows, inner = conv_ref.shape
    tiles = inner // TILE
    per = TILE // HD
    ones = lower_ones(BLK)
    for block in range(rows // BLK):
        span = slice(block * BLK, (block + 1) * BLK)
        scores = mm_nt(outmap_ref[span], in_ref[span])
        gap = iota((BLK, BLK), 0) - iota((BLK, BLK), 1)
        keep = (gap >= 0) & (gap <= rel_ref[span])
        scores_ref[block] = jnp.where(keep, scores, 0.0)
        across_ref[block] = mm(ones, small_ref[span]).T

    def body(tile, _):
        columns = pl.ds(pl.multiple_of(tile * TILE, TILE), TILE)
        small = small_ref[...]
        steps = mm(small, head_spread(tile, 0))
        decays = mm(small, head_spread(tile, DECAY_AT)).astype(BF)
        conv = conv_ref[:, columns].astype(F32)
        inject = (conv * steps).astype(BF)
        lane_head = iota((BLK, TILE), 1) // HD
        for block in range(rows // BLK):
            span = slice(block * BLK, (block + 1) * BLK)
            cumulative = mm(ones, decays[span])
            scores = scores_ref[block]
            total = skip_ref[:, columns] * conv[span]
            if block > 0:
                enter = jnp.where(
                    iota((BLK, 1), 0) < rel_ref[span], jnp.exp(cumulative), 0.0
                )
                total = total + enter * mm(outmap_ref[span], mid_ref[:, columns])
            for q in range(per):
                down = cumulative[:, q * HD : q * HD + 1]
                across = across_ref[block, pl.ds(DECAY_AT + per * tile + q, 1), :]
                weights = (scores * jnp.exp(jnp.minimum(down - across, 0.0))).astype(BF)
                mine = jnp.where(lane_head == q, inject[span], jnp.zeros((), BF))
                total = total + mm(weights, mine)
            part_ref[span, columns] = total
        pltpu.make_async_copy(
            part_ref.at[:, columns], part_hbm.at[:, columns], puts.at[tile]
        ).start()
        return 0

    lax.fori_loop(0, tiles, body, 0)
    for tile in range(tiles):
        columns = pl.ds(tile * TILE, TILE)
        pltpu.make_async_copy(
            part_ref.at[:, columns], part_hbm.at[:, columns], puts.at[tile]
        ).wait()


def inner_part(small, rel, input_map, output_map, conv, mid, skip_wide):
    rows, inner = conv.shape
    blocks = rows // BLK
    tiles = inner // TILE
    return pl.pallas_call(
        inner_kernel,
        in_specs=vmem(2) + hbm(6),
        out_specs=hbm(1)[0],
        out_shape=pltpu.HBM((rows, inner), F32),
        scratch_shapes=[
            pltpu.VMEM((rows, LANES), BF),
            pltpu.VMEM(input_map.shape, BF),
            pltpu.VMEM(output_map.shape, BF),
            pltpu.VMEM(conv.shape, BF),
            pltpu.VMEM(mid.shape, BF),
            pltpu.VMEM((rows, inner), F32),
            pltpu.VMEM((blocks, BLK, BLK), F32),
            pltpu.VMEM((blocks, 128, BLK), F32),
            pltpu.SemaphoreType.DMA((6,)),
            pltpu.SemaphoreType.DMA((tiles,)),
        ],
        name="inner_part",
        **params(24, 8 * rows * BLK * inner, 8_000_000),
    )(rel, skip_wide, *[far(x) for x in (*small, input_map, output_map, conv, mid)])


def scan_kernel(lines, me_ref, recv_ref, out_ref):
    groups = recv_ref.shape[0]
    me = me_ref[0]
    base = me // 2 * 5
    odd = lax.rem(me, 2)
    columns = [(base + 3 * odd) // lines, (base + 1 + 3 * odd) // lines, (base + 2) // lines]
    least = jnp.minimum(jnp.minimum(columns[0], columns[1]), columns[2])
    near_first = [
        jnp.where(jnp.full((8, LANES), column, jnp.int32) == least, 1.0, 0.0) for column in columns
    ]

    def body(shard, state):
        piece = recv_ref[shard].astype(F32)
        out_ref[shard] = jnp.concatenate(state, axis=0).astype(BF)
        gain_a = piece[20:21] + piece[21:22]
        gain_b = piece[22:23] + piece[23:24]
        return tuple(
            jnp.where(first > 0.5, gain_a, gain_b) * old + piece[8 * at : 8 * at + 8]
            for at, (first, old) in enumerate(zip(near_first, state))
        )

    lax.fori_loop(0, groups, body, (jnp.zeros((8, LANES), F32),) * 3, unroll=4)


def scan_shards(me, recv, lines):
    return pl.pallas_call(
        functools.partial(scan_kernel, lines),
        in_specs=[pl.BlockSpec(memory_space=pltpu.SMEM)] + vmem(1),
        out_specs=pl.BlockSpec(memory_space=pltpu.VMEM),
        out_shape=jax.ShapeDtypeStruct(recv.shape, BF),
        name="scan_shards",
        **params(8, 10_000_000, 800_000),
    )(me, recv)


def prepare_kernel(rel_ref, low_hbm, high_hbm, gain_ref, small_ref, ones_ref, sems):
    rows, inner = gain_ref.shape
    half = rows // 2
    get_small = [
        fetch(low_hbm, small_ref.at[pl.ds(0, half)], sems.at[0]),
        fetch(high_hbm, small_ref.at[pl.ds(half, half)], sems.at[1]),
    ]
    ones_ref[...] = lower_ones(rows)
    reached = iota((rows, 1), 0) < rel_ref[...]
    for copy in get_small:
        copy.wait()

    def body(tile, _):
        decays = mm(small_ref[...], head_spread(tile, DECAY_AT)).astype(BF)
        cumulative = mm(ones_ref[...], decays)
        gain_ref[:, pl.ds(pl.multiple_of(tile * TILE, TILE), TILE)] = jnp.where(
            reached, jnp.exp(cumulative), 0.0
        )
        return 0

    lax.fori_loop(0, inner // TILE, body, 0)


def prepare(rel, small, inner):
    rows = rel.shape[0]
    return pl.pallas_call(
        prepare_kernel,
        in_specs=vmem(1) + hbm(2),
        out_specs=vmem(1)[0],
        out_shape=pltpu.VMEM((rows, inner), F32),
        scratch_shapes=[
            pltpu.VMEM((rows, LANES), BF),
            pltpu.VMEM((rows, rows), BF),
            pltpu.SemaphoreType.DMA((2,)),
        ],
        name="prepare",
        **params(8, 2 * rows * rows * inner, 8_000_000),
    )(rel, *[far(x) for x in small])


def final_kernel(
    recv_ref, gain_ref, outmap_hbm, part_hbm, out_hbm,
    outmap_ref, part_ref, enter_ref, held_ref, gets, puts,
):
    rows, inner = part_ref.shape
    states = outmap_ref.shape[1]
    lines = states // 8
    steps = rows // TAKEN
    spans = [pl.ds(step * TAKEN, TAKEN) for step in range(steps)]
    get_map = fetch(outmap_hbm, outmap_ref, gets.at[steps])
    copies = [
        fetch(part_hbm.at[span], part_ref.at[span], gets.at[step])
        for step, span in enumerate(spans)
    ]
    where = {}
    for dest in range(recv_ref.shape[0]):
        first, second, shared = piece_tiles(dest)
        where[first] = (dest, 0)
        where[second] = (dest, 1)
        where.setdefault(shared, dest)

    def tile_of(index):
        if isinstance(where[index], tuple):
            dest, at = where[index]
            return recv_ref[dest].astype(F32)[8 * at : 8 * at + 8]
        dest = where[index]
        upper = recv_ref[dest].astype(F32)[16:20]
        lower = recv_ref[dest + 1].astype(F32)[16:20]
        return jnp.concatenate([upper, lower], axis=0)

    def column_of(column):
        parts = [tile_of(column * lines + line) for line in range(lines)]
        return jnp.concatenate(parts, axis=0).astype(BF)

    for column in range(inner // LANES):
        enter_ref[:, column * LANES : (column + 1) * LANES] = column_of(column)
    get_map.wait()
    puts_made = []
    for step, span in enumerate(spans):
        outer = mm(outmap_ref[span], enter_ref[...])
        copies[step].wait()
        held_ref[span] = (part_ref[span] + gain_ref[span] * outer).astype(BF)
        puts_made.append(fetch(held_ref.at[span], out_hbm.at[span], puts.at[step]))
    for copy in puts_made:
        copy.wait()


def final(output_map, part, gain, recv):
    rows, inner = part.shape
    states = output_map.shape[1]
    return pl.pallas_call(
        final_kernel,
        in_specs=vmem(2) + hbm(2),
        out_specs=hbm(1)[0],
        out_shape=jax.ShapeDtypeStruct((rows, inner), BF),
        scratch_shapes=[
            pltpu.VMEM((rows, states), BF),
            pltpu.VMEM((rows, inner), F32),
            pltpu.VMEM((states, inner), BF),
            pltpu.VMEM((rows, inner), BF),
            pltpu.SemaphoreType.DMA((rows // TAKEN + 1,)),
            pltpu.SemaphoreType.DMA((rows // TAKEN,)),
        ],
        name="final",
        **params(16, 2 * rows * states * inner, 7_000_000),
    )(near(recv), near(gain), far(output_map), far(part))


def on_device(tokens, dt_decay, dest, lengths, w_x, w_bc, conv_x, conv_bc, bias_x, bias_bc, skip):
    rows, width = tokens.shape
    groups = lax.axis_size("ctx")
    ring = lax.axis_size("head")
    first_pos = lax.axis_index("ctx") * rows

    sent = pack(dest[None, :], tokens, jnp.transpose(dt_decay, (2, 1, 0)), groups)
    arrived = lax.all_to_all(sent, "ctx", split_axis=0, concat_axis=0, tiled=True)
    low, edge, high, small = unpack(arrived, width, rows)

    def turned(x, by):
        return lax.ppermute(x, "head", [(i, (i + by) % ring) for i in range(ring)])

    low_left, low_right = turned(low, 1), turned(low, ring - 1)
    halo = lax.ppermute(edge, "ctx", [(i, i + 1) for i in range(groups - 1)])
    high = lax.dynamic_update_slice(high, halo, (0, 0))
    high_right = turned(high, ring - 1)

    starts = jnp.cumsum(lengths) - lengths
    positions = first_pos + jnp.arange(rows, dtype=jnp.int32)
    doc_start = jnp.max(
        jnp.where(starts[None, :] <= positions[:, None], starts[None, :], 0), axis=1
    )
    rel = (positions - doc_start)[:, None]
    me = lax.axis_index("head").astype(jnp.int32)[None]
    inner = w_x.shape[1]
    steps, tail, carry = decay_factors(rel, small, inner)
    later, carry = lax.optimization_barrier((high, carry))
    high_left = turned(later, 1)
    low_far, high_far = turned(low_left, 1), turned(high_right, ring - 1)
    total, w_left, w_right, w_far = project_own(me, low, high, w_x, w_bc)
    total = project_near(
        (low_left, high_left), (low_right, high_right), w_left, w_right, total
    )
    conv, state, mid, input_map, output_map = front(
        (low_far, high_far), total, w_far, rel, carry, steps, tail,
        conv_x, bias_x[None, :], conv_bc, bias_bc[None, :], groups,
    )
    gathered = lax.all_to_all(state, "ctx", split_axis=0, concat_axis=0, tiled=True)
    part = inner_part(
        small, rel, input_map, output_map, conv, mid, jnp.repeat(skip, HD)[None, :]
    )
    gathered, part = lax.optimization_barrier((gathered, part))
    spot = lax.axis_index("ctx").astype(jnp.int32)[None]
    entering = scan_shards(spot, gathered, input_map.shape[1] // 8)
    entering, rel = lax.optimization_barrier((entering, rel))
    gain = prepare(rel, small, inner)
    enter = lax.all_to_all(entering, "ctx", split_axis=0, concat_axis=0, tiled=True)
    return final(output_map, part, gain, enter)


def solution(mesh):
    in_specs = (
        P("ctx", "head"),
        P("ctx", None, "head"),
        P("ctx"),
        P(),
        P(None, "head"),
        P(),
        P(None, "head"),
        P(),
        P("head"),
        P(),
        P("head"),
    )
    out_specs = P("ctx", "head")
    return jax.shard_map(
        on_device, mesh=mesh, in_specs=in_specs, out_specs=out_specs, check_vma=False
    )
```

time: 149 us -> 140 us (0.940)
  blocking collectives: 70.5 us -> 0 us
  waiting for transfers between devices: 17.2 us -> 58.8 us
  starting transfers between devices: 20.5 us -> 37 us
  Pallas kernels: 38.3 us -> 42.4 us
    all_to_all x2 -> x0, blocking collectives: 70.5 us -> none  [the longest x1 49.9 us: on_device(): lax.all_to_all(sent, 'ctx', split_axis=0, concat_axis=0, tiled=True)]
    all_to_all x0 -> x2, waiting for transfers between devices: none -> 47.5 us  [the longest x1 36.6 us: on_device(): lax.all_to_all(sent, 'ctx', split_axis=0, concat_axis=0, tiled=True)]
    all_to_all x0 -> x2, starting transfers between devices: none -> 19.4 us  [the longest x1 13.2 us: on_device(): lax.all_to_all(sent, 'ctx', split_axis=0, concat_axis=0, tiled=True)]
    ppermute x6, waiting for transfers between devices: 11.3 us -> 5.42 us  [turned(): return lax.ppermute(x, 'head', [(i, (i + by) % ring) for i in range(ring)])]
    all_to_all x1, starting transfers between devices: 9.37 us -> 5.89 us  [on_device(): lax.all_to_all(state, 'ctx', split_axis=0, concat_axis=0, tiled=True)]
    pallas_call x6 -> x9, Pallas kernels: 33.6 us -> 37 us  [the longest x1 8.55 us: inner_part(): pl.pallas_call(inner_kernel, in_specs=vmem(2) + hbm(6), out_specs=hbm(1)[...]
  transfers between devices with their start and end apart: 8 -> 10, of which waited for: 4 -> 8; matrix products, arithmetic and copies ran while one was open for 1% -> 1% of each run, Pallas kernels for 12% -> 17%
where the time goes in v4:
time: 140 us
  waiting for transfers between devices  58.8 us (42%)
  Pallas kernels  42.4 us (30%)
  starting transfers between devices  37 us (26%)
    all_to_all x1, waiting for transfers between devices, on_device(): lax.all_to_all(sent, 'ctx', split_axis=0, concat_axis=0, tiled=True)  36.6 us
    all_to_all x1, starting transfers between devices, on_device(): lax.all_to_all(sent, 'ctx', split_axis=0, concat_axis=0, tiled=True)  13.2 us
    all_to_all x1, waiting for transfers between devices, on_device(): lax.all_to_all(entering, 'ctx', split_axis=0, concat_axis=0, tiled=True)  10.9 us
    ppermute x6, starting transfers between devices, turned(): return lax.ppermute(x, 'head', [(i, (i + by) % ring) for i in range(ring)])  8.72 us
    pallas_call x1, Pallas kernels, inner_part(): pl.pallas_call(inner_kernel, in_specs=vmem(2) + hbm(6), out_specs=hbm(1)[...  8.55 us
    pallas_call x1, Pallas kernels, front(): pl.pallas_call(front_kernel, in_specs=vmem(10) + hbm(2), out_specs=hbm(1)...  7.97 us
    all_to_all x1, starting transfers between devices, on_device(): lax.all_to_all(entering, 'ctx', split_axis=0, concat_axis=0, tiled=True)  6.2 us
    all_to_all x1, starting transfers between devices, on_device(): lax.all_to_all(state, 'ctx', split_axis=0, concat_axis=0, tiled=True)  5.89 us
  transfers between devices with their start and end apart: 10, of which 8 were waited for; matrix products, arithmetic and copies ran while one was open for 1% of the time, Pallas kernels for 17%

profile of v4, /device:TPU:1, one launch (start us, length us, event | category | flops | bytes accessed | tf_op | source)
XLA Modules:
  0.0 139.6 jit_solution(5475900197921247752)
XLA Ops:
  0.0 4.4 %pack.1 = bf16[64,88,128]{2,1,0:T(8,128)(2,1)} custom-call(s32[1,512]{1,0:T(1,128)} %bitcast.11, bf16[20,2,512]{2,1,0:T(2,128)(2,1)} %bitcast.10, bf16[512,640]{1,0:T(8,128)(2,1)} %tok_hbm.1), custom_call_target="tpu_custom_call" | custom-call | flops 805306368 | bytes 1310720 | tf_op jit(solution)/shard_map/pack/pallas_call | solution.py:138
  4.4 13.2 %all-to-all-start = ((bf16[64,88,128]{2,1,0:T(8,128)(2,1)}), bf16[64,88,128]{2,1,0:T(8,128)(2,1)S(1)}, u32[]{:S(2)}, u32[]{:S(2)}) async-start(bf16[64,88,128]{2,1,0:T(8,128)(2,1)} %pack.1), calls=%async_computation | async-start | bytes 2883584 | tf_op jit(solution)/shard_map/all_to_all | solution.py:822
  18.0 36.6 %all-to-all-done.recv_ref = bf16[64,88,128]{2,1,0:T(8,128)(2,1)S(1)} async-done(((bf16[64,88,128]{2,1,0:T(8,128)(2,1)}), bf16[64,88,128]{2,1,0:T(8,128)(2,1)S(1)}, u32[]{:S(2)}, u32[]{:S(2)}) %all-to-all-start) | async-done | bytes 1441824 | tf_op jit(solution)/shard_map/all_to_all | solution.py:822
  54.6 1.2 unpack_low.1
  55.8 1.1 unpack_high.1
  56.9 3.0 %collective-permute-start.2 = (bf16[16,640]{1,0:T(8,128)(2,1)S(1)}, bf16[16,640]{1,0:T(8,128)(2,1)S(1)}, u32[]{:S(2)}, u32[]{:S(2)}) collective-permute-start(bf16[16,640]{1,0:T(8,128)(2,1)S(1)} %get-tuple-element.32), channel_id=1, source_target_pairs={{0,4},{4,8},{8,12},{12,16},{16,20},{20,24},{24,28},{28,32},{32,36}... | collective-permute-start | bytes 61448 | tf_op jit(solution)/shard_map/ppermute | solution.py:829
  60.3 1.3 collective-permute-start
  61.6 1.7 %collective-permute-start.3 = (bf16[272,640]{1,0:T(8,128)(2,1)S(1)}, bf16[272,640]{1,0:T(8,128)(2,1)S(1)}, u32[]{:S(2)}, u32[]{:S(2)}) collective-permute-start(bf16[272,640]{1,0:T(8,128)(2,1)S(1)} %constant_dynamic-update-slice_fusion.high_ref), channel_id=1, source_target_pairs={{0,3},{1,0},{2,1},{3,2},{4,7},{5,4},{6,5},{7,6},{8,11},{9,8},{10,9... | collective-permute-start | bytes 1044488 | tf_op jit(solution)/shard_map/ppermute | solution.py:826
  63.3 4.4 %decay_factors.1 = (bf16[5,512,256]{2,1,0:T(8,128)(2,1)}, f32[5,512,256]{2,1,0:T(8,128)}, f32[5,8,256]{2,1,0:T(8,128)S(1)}) custom-call(s32[512,1]{1,0:T(8,128)S(1)} %add_subtract_fusion.rel_ref, bf16[256,128]{1,0:T(8,128)(2,1)} %get-tuple-element.33.low_hbm, bf16[256,128]{1,0:T(8,128)(2,1)} %get-tuple-element.34.high_hbm), custom_call_target="tpu_custom_call" | custom-call | flops 671088640 | bytes 7000000 | tf_op jit(solution)/shard_map/decay_factors/pallas_call | solution.py:337
  67.8 2.7 %collective-permute-start.6 = (bf16[256,640]{1,0:T(8,128)(2,1)S(1)}, bf16[256,640]{1,0:T(8,128)(2,1)S(1)}, u32[]{:S(2)}, u32[]{:S(2)}) collective-permute-start(bf16[256,640]{1,0:T(8,128)(2,1)S(1)} %get-tuple-element.29.low_ref), channel_id=1, source_target_pairs={{0,3},{1,0},{2,1},{3,2},{4,7},{5,4},{6,5},{7,6},{8,11},{9,8},{10,9... | collective-permute-start | bytes 983048 | tf_op jit(solution)/shard_map/ppermute | solution.py:826
  70.4 1.1 collective-permute-done.3.high3
  71.5 3.0 %collective-permute-start.4 = (bf16[272,640]{1,0:T(8,128)(2,1)S(1)}, bf16[272,640]{1,0:T(8,128)(2,1)S(1)}, u32[]{:S(2)}, u32[]{:S(2)}) collective-permute-start(bf16[272,640]{1,0:T(8,128)(2,1)S(1)} %collective-permute-done.3.high3), channel_id=1, source_target_pairs={{0,3},{1,0},{2,1},{3,2},{4,7},{5,4},{6,5},{7,6},{8,11},{9,8},{10,9... | collective-permute-start | bytes 1044488 | tf_op jit(solution)/shard_map/ppermute | solution.py:826
  74.6 3.9 %project_own.1 = (f32[528,1536]{1,0:T(8,128)S(1)}, bf16[640,1536]{1,0:T(8,128)(2,1)S(1)}, bf16[640,1536]{1,0:T(8,128)(2,1)S(1)}, bf16[640,1536]{1,0:T(8,128)(2,1)S(1)}) custom-call(s32[1]{0:T(128)} %bitcast.5.me_ref, bf16[256,640]{1,0:T(8,128)(2,1)S(1)} %get-tuple-element.29.low_ref, bf16[272,640]{1,0:T(8,128)(2,1)S(1)} %constant_dynamic-update-slice_fusion.high_ref, ...), custom_call_target="tpu_custom_call" | custom-call | flops 1038090240 | bytes 8000000 | tf_op jit(solution)/shard_map/project_own/pallas_call | solution.py:400
  78.9 3.2 %project_near.1.total_ref = f32[528,1536]{1,0:T(8,128)S(1)} custom-call(bf16[256,640]{1,0:T(8,128)(2,1)S(1)} %collective-permute-done.low1, bf16[272,640]{1,0:T(8,128)(2,1)S(1)} %collective-permute-done.5.high1, bf16[256,640]{1,0:T(8,128)(2,1)S(1)} %collective-permute-done.6.low3, bf16[272,640]{1,0:T(8,128)(2,1)S(1)} %collective-permute-done.3.high3, ...), custom_call_target="tpu_custom_call" | custom-call | flops 2076180480 | bytes 8000000 | tf_op jit(solution)/shard_map/project_near/pallas_call | solution.py:434
  82.2 3.5 %collective-permute-done.1.low_ref = bf16[256,640]{1,0:T(8,128)(2,1)S(1)} collective-permute-done((bf16[256,640]{1,0:T(8,128)(2,1)S(1)}, bf16[256,640]{1,0:T(8,128)(2,1)S(1)}, u32[]{:S(2)}, u32[]{:S(2)}) %collective-permute-start.1) | collective-permute-done | bytes 327712 | tf_op jit(solution)/shard_map/ppermute | solution.py:826
  86.0 8.0 %front.1 = (bf16[512,1280]{1,0:T(8,128)(2,1)}, bf16[64,24,128]{2,1,0:T(8,128)(2,1)}, bf16[128,1280]{1,0:T(8,128)(2,1)}, bf16[512,128]{1,0:T(8,128)(2,1)}, bf16[512,128]{1,0:T(8,128)(2,1)}) custom-call(bf16[256,640]{1,0:T(8,128)(2,1)S(1)} %collective-permute-done.1.low_ref, bf16[272,640]{1,0:T(8,128)(2,1)S(1)} %collective-permute-done.4.high_ref, ...), custom_call_target="tpu_custom_call" | custom-call | flops 1006632960 | bytes 12000000 | tf_op jit(solution)/shard_map/front/pallas_call | solution.py:544
  94.0 5.9 %all-to-all-start.1 = ((bf16[64,24,128]{2,1,0:T(8,128)(2,1)}), bf16[64,24,128]{2,1,0:T(8,128)(2,1)S(1)}, u32[]{:S(2)}, u32[]{:S(2)}) async-start(bf16[64,24,128]{2,1,0:T(8,128)(2,1)} %get-tuple-element.44), calls=%async_computation.1 | async-start | bytes 786432 | tf_op jit(solution)/shard_map/all_to_all | solution.py:853
  100.1 8.6 %inner_part.1.part_hbm = f32[512,1280]{1,0:T(8,128)} custom-call(s32[512,1]{1,0:T(8,128)S(1)} %add_subtract_fusion.rel_ref, f32[1,1280]{1,0:T(1,128)S(1)} %broadcast_in_dim_reshape.3.skip_ref, bf16[256,128]{1,0:T(8,128)(2,1)} %get-tuple-element.33.low_hbm, bf16[256,128]{1,0:T(8,128)(2,1)} %get-tuple-element.34.high_hbm, ...), custom_call_target="tpu_custom_call" | custom-call | flops 1342177280 | bytes 8000000 | tf_op jit(solution)/shard_map/inner_part/pallas_call | solution.py:650
  108.6 5.9 %all-to-all-done.1.recv_ref = bf16[64,24,128]{2,1,0:T(8,128)(2,1)S(1)} async-done(((bf16[64,24,128]{2,1,0:T(8,128)(2,1)}), bf16[64,24,128]{2,1,0:T(8,128)(2,1)S(1)}, u32[]{:S(2)}, u32[]{:S(2)}) %all-to-all-start.1) | async-done | bytes 393248 | tf_op jit(solution)/shard_map/all_to_all | solution.py:853
  114.5 1.0 scan_shards.1
  115.5 6.2 %all-to-all-start.2 = ((bf16[64,24,128]{2,1,0:T(8,128)(2,1)}), bf16[64,24,128]{2,1,0:T(8,128)(2,1)S(1)}, u32[]{:S(2)}, u32[]{:S(2)}) async-start(bf16[64,24,128]{2,1,0:T(8,128)(2,1)} %scan_shards.1), calls=%async_computation.2 | async-start | bytes 786432 | tf_op jit(solution)/shard_map/all_to_all | solution.py:862
  121.7 3.7 %prepare.1.gain_ref = f32[512,1280]{1,0:T(8,128)S(1)} custom-call(s32[512,1]{1,0:T(8,128)S(1)} %add_subtract_fusion.rel_ref, bf16[256,128]{1,0:T(8,128)(2,1)} %get-tuple-element.33.low_hbm, bf16[256,128]{1,0:T(8,128)(2,1)} %get-tuple-element.34.high_hbm), custom_call_target="tpu_custom_call" | custom-call | flops 671088640 | bytes 8000000 | tf_op jit(solution)/shard_map/prepare/pallas_call | solution.py:732
  125.4 10.9 %all-to-all-done.2.recv_ref = bf16[64,24,128]{2,1,0:T(8,128)(2,1)S(1)} async-done(((bf16[64,24,128]{2,1,0:T(8,128)(2,1)}), bf16[64,24,128]{2,1,0:T(8,128)(2,1)S(1)}, u32[]{:S(2)}, u32[]{:S(2)}) %all-to-all-start.2) | async-done | bytes 393248 | tf_op jit(solution)/shard_map/all_to_all | solution.py:862
  136.3 3.1 %final.1 = bf16[512,1280]{1,0:T(8,128)(2,1)} custom-call(bf16[64,24,128]{2,1,0:T(8,128)(2,1)S(1)} %all-to-all-done.2.recv_ref, f32[512,1280]{1,0:T(8,128)S(1)} %prepare.1.gain_ref, bf16[512,128]{1,0:T(8,128)(2,1)} %get-tuple-element.46.outmap_hbm, f32[512,1280]{1,0:T(8,128)} %inner_part.1.part_hbm), custom_call_target="tpu_custom_call" | custom-call | flops 167772160 | bytes 7000000 | tf_op jit(solution)/shard_map/final/pallas_call | solution.py:797
  (31 shorter events, 1.9 us)
Async XLA Ops:
  4.4 13.2 %copy-start.4 = (s32[128]{0:T(128)S(1)}, s32[128]{0:T(128)}, u32[]{:S(2)}) copy-start(s32[128]{0:T(128)} %param.14) | copy-start | bytes 1540
  4.4 50.2 %all-to-all-start = ((bf16[64,88,128]{2,1,0:T(8,128)(2,1)}), bf16[64,88,128]{2,1,0:T(8,128)(2,1)S(1)}, u32[]{:S(2)}, u32[]{:S(2)}) async-start(bf16[64,88,128]{2,1,0:T(8,128)(2,1)} %pack.1), calls=%async_computation | async-start | bytes 2883584 | tf_op jit(solution)/shard_map/all_to_all | solution.py:822
  56.9 17.7 %copy-start.3 = (f32[1280]{0:T(1024)S(1)}, f32[1280]{0:T(1024)}, u32[]{:S(2)}) copy-start(f32[1280]{0:T(1024)} %param.19) | copy-start | bytes 15364
  56.9 4.7 %collective-permute-start.2 = (bf16[16,640]{1,0:T(8,128)(2,1)S(1)}, bf16[16,640]{1,0:T(8,128)(2,1)S(1)}, u32[]{:S(2)}, u32[]{:S(2)}) collective-permute-start(bf16[16,640]{1,0:T(8,128)(2,1)S(1)} %get-tuple-element.32), channel_id=1, source_target_pairs={{0,4},{4,8},{8,12},{12,16},{16,20},{20,24},{24,28},{28,32},{32,36}... | collective-permute-start | bytes 61448 | tf_op jit(solution)/shard_map/ppermute | solution.py:829
  60.3 14.3 %collective-permute-start = (bf16[256,640]{1,0:T(8,128)(2,1)S(1)}, bf16[256,640]{1,0:T(8,128)(2,1)S(1)}, u32[]{:S(2)}, u32[]{:S(2)}) collective-permute-start(bf16[256,640]{1,0:T(8,128)(2,1)S(1)} %get-tuple-element.29.low_ref), channel_id=1, source_target_pairs={{0,1},{1,2},{2,3},{3,0},{4,5},{5,6},{6,7},{7,4},{8,9},{9,10},{10,1... | collective-permute-start | bytes 983048 | tf_op jit(solution)/shard_map/ppermute | solution.py:826
  61.6 10.0 %collective-permute-start.3 = (bf16[272,640]{1,0:T(8,128)(2,1)S(1)}, bf16[272,640]{1,0:T(8,128)(2,1)S(1)}, u32[]{:S(2)}, u32[]{:S(2)}) collective-permute-start(bf16[272,640]{1,0:T(8,128)(2,1)S(1)} %constant_dynamic-update-slice_fusion.high_ref), channel_id=1, source_target_pairs={{0,3},{1,0},{2,1},{3,2},{4,7},{5,4},{6,5},{7,6},{8,11},{9,8},{10,9... | collective-permute-start | bytes 1044488 | tf_op jit(solution)/shard_map/ppermute | solution.py:826
  67.7 11.2 %collective-permute-start.5 = (bf16[272,640]{1,0:T(8,128)(2,1)S(1)}, bf16[272,640]{1,0:T(8,128)(2,1)S(1)}, u32[]{:S(2)}, u32[]{:S(2)}) collective-permute-start(bf16[272,640]{1,0:T(8,128)(2,1)S(1)} %constant_dynamic-update-slice_fusion.high_ref), channel_id=1, source_target_pairs={{0,1},{1,2},{2,3},{3,0},{4,5},{5,6},{6,7},{7,4},{8,9},{9,10},{10,1... | collective-permute-start | bytes 1044488 | tf_op jit(solution)/shard_map/ppermute | solution.py:826
  67.8 10.8 %collective-permute-start.6 = (bf16[256,640]{1,0:T(8,128)(2,1)S(1)}, bf16[256,640]{1,0:T(8,128)(2,1)S(1)}, u32[]{:S(2)}, u32[]{:S(2)}) collective-permute-start(bf16[256,640]{1,0:T(8,128)(2,1)S(1)} %get-tuple-element.29.low_ref), channel_id=1, source_target_pairs={{0,3},{1,0},{2,1},{3,2},{4,7},{5,4},{6,5},{7,6},{8,11},{9,8},{10,9... | collective-permute-start | bytes 983048 | tf_op jit(solution)/shard_map/ppermute | solution.py:826
  71.5 14.5 %collective-permute-start.4 = (bf16[272,640]{1,0:T(8,128)(2,1)S(1)}, bf16[272,640]{1,0:T(8,128)(2,1)S(1)}, u32[]{:S(2)}, u32[]{:S(2)}) collective-permute-start(bf16[272,640]{1,0:T(8,128)(2,1)S(1)} %collective-permute-done.3.high3), channel_id=1, source_target_pairs={{0,3},{1,0},{2,1},{3,2},{4,7},{5,4},{6,5},{7,6},{8,11},{9,8},{10,9... | collective-permute-start | bytes 1044488 | tf_op jit(solution)/shard_map/ppermute | solution.py:826
  74.5 11.1 %collective-permute-start.1 = (bf16[256,640]{1,0:T(8,128)(2,1)S(1)}, bf16[256,640]{1,0:T(8,128)(2,1)S(1)}, u32[]{:S(2)}, u32[]{:S(2)}) collective-permute-start(bf16[256,640]{1,0:T(8,128)(2,1)S(1)} %collective-permute-done.low1), channel_id=1, source_target_pairs={{0,1},{1,2},{2,3},{3,0},{4,5},{5,6},{6,7},{7,4},{8,9},{9,10},{10,1... | collective-permute-start | bytes 983048 | tf_op jit(solution)/shard_map/ppermute | solution.py:826
  78.9 7.1 %copy-start = (f32[4,1280]{1,0:T(4,128)S(1)}, f32[4,1280]{1,0:T(4,128)}, u32[]{:S(2)}) copy-start(f32[4,1280]{1,0:T(4,128)} %cx_ref.1) | copy-start | bytes 61444
  78.9 7.1 %copy-start.1 = (f32[4,256]{1,0:T(4,128)S(1)}, f32[4,256]{1,0:T(4,128)}, u32[]{:S(2)}) copy-start(f32[4,256]{1,0:T(4,128)} %cb_ref.1) | copy-start | bytes 12292
  78.9 7.1 %copy-start.2 = (f32[256]{0:T(256)S(1)}, f32[256]{0:T(256)}, u32[]{:S(2)}) copy-start(f32[256]{0:T(256)} %param.20) | copy-start | bytes 3076
  86.0 13.9 %copy-start.5 = (f32[20]{0:T(128)S(1)}, f32[20]{0:T(128)}, u32[]{:S(2)}) copy-start(f32[20]{0:T(128)} %param.21) | copy-start | bytes 244
  94.0 20.5 %all-to-all-start.1 = ((bf16[64,24,128]{2,1,0:T(8,128)(2,1)}), bf16[64,24,128]{2,1,0:T(8,128)(2,1)S(1)}, u32[]{:S(2)}, u32[]{:S(2)}) async-start(bf16[64,24,128]{2,1,0:T(8,128)(2,1)} %get-tuple-element.44), calls=%async_computation.1 | async-start | bytes 786432 | tf_op jit(solution)/shard_map/all_to_all | solution.py:853
  115.5 20.8 %all-to-all-start.2 = ((bf16[64,24,128]{2,1,0:T(8,128)(2,1)}), bf16[64,24,128]{2,1,0:T(8,128)(2,1)S(1)}, u32[]{:S(2)}, u32[]{:S(2)}) async-start(bf16[64,24,128]{2,1,0:T(8,128)(2,1)} %scan_shards.1), calls=%async_computation.2 | async-start | bytes 786432 | tf_op jit(solution)/shard_map/all_to_all | solution.py:862

commit v5 on v4

--- a/solution.py
+++ b/solution.py
@@ -80,13 +80,13 @@
 
 def pack_kernel(
     dest_hbm, steps_hbm, tok_hbm, out_ref,
-    dest_ref, steps_ref, tok_ref, slot_ref, code_ref, small_ref, turned_ref, upper_ref,
+    dest_ref, steps_ref, tok_ref, slot_ref, code_ref, small_ref, upper_ref,
     sems,
 ):
     get_dest = fetch(dest_hbm, dest_ref, sems.at[0])
     get_steps = fetch(steps_hbm, steps_ref, sems.at[1])
-    get_tokens = fetch(tok_hbm, tok_ref, sems.at[2])
-    rows, width = tok_ref.shape
+    rows, width = tok_hbm.shape
+    get_tokens = fetch(tok_hbm, tok_ref.at[:, pl.ds(0, width)], sems.at[2])
     groups = code_ref.shape[0]
     heads = steps_ref.shape[0]
     per = 8
@@ -110,27 +110,28 @@
     steps = steps_ref[...].astype(F32)
     small_ref[:heads] = steps[:, 0, :]
     small_ref[DECAY_AT : DECAY_AT + heads] = steps[:, 1, :]
-    turned_ref[...] = small_ref[...].T.astype(BF)
+    tok_ref[:, width:] = small_ref[...].T.astype(BF)
     get_tokens.wait()
 
     def body(step, _):
         slot = slot_ref[...] - step * slots
         here = pl.ds(pl.multiple_of(step * per, per), per)
         select = as_bf(iota((slots, rows), 0) == slot)
-        sent = mm(select, tok_ref[...]).astype(BF)
+        both = mm(select, tok_ref[...])
+        sent = both[:, :width].astype(BF)
         for column in range(width // LANES):
             out_ref[here, column * CAP : (column + 1) * CAP, :] = sent[
                 :, column * LANES : (column + 1) * LANES
             ].reshape(per, CAP, LANES)
         half = CAP // 2
-        small = mm(select, turned_ref[...]).reshape(per, CAP, LANES)
+        small = both[:, width:].reshape(per, CAP, LANES)
         pairs = small[:, :half, :] + pltpu.roll(small[:, half:, :], LANES // 2, 2)
         first = iota((per, half, LANES), 1) == 0
         pairs = pairs + jnp.where(first, code_ref[here][:, None, :], 0.0)
         out_ref[here, ROWS_SENT - half :, :] = pairs.astype(BF)
         return 0
 
-    lax.fori_loop(0, groups // per, body, 0, unroll=2)
+    lax.fori_loop(0, groups // per, body, 0, unroll=8)
 
 
 def pack(dest, tokens, steps, groups):
@@ -143,11 +144,10 @@
         scratch_shapes=[
             pltpu.VMEM((1, rows), jnp.int32),
             pltpu.VMEM(steps.shape, BF),
-            pltpu.VMEM((rows, width), BF),
+            pltpu.VMEM((rows, width + LANES), BF),
             pltpu.VMEM((1, rows), jnp.int32),
             pltpu.VMEM((groups, LANES), F32),
             pltpu.VMEM((LANES, rows), F32),
-            pltpu.VMEM((rows, LANES), BF),
             pltpu.VMEM((rows, rows), BF),
             pltpu.SemaphoreType.DMA((3,)),
         ],
@@ -451,9 +451,9 @@
 def front_kernel(
     low_ref, high_ref, total_ref, w_ref, rel_ref, carry_ref, cx_ref, bx_ref, cb_ref, bb_ref,
     steps_hbm, tail_hbm,
-    conv_hbm, sent_ref, mid_hbm, in_hbm, outmap_hbm,
-    steps_ref, tail_ref, conv_ref, mid_ref, in_ref, outmap_ref, across_ref,
-    xe_ref, ext_ref, state_ref, gets, puts,
+    conv_hbm, mine_ref, mid_hbm, in_hbm, outmap_ref,
+    steps_ref, tail_ref, conv_ref, mid_ref, in_ref, across_ref,
+    xe_ref, ext_ref, gets, puts,
 ):
     half, width = low_ref.shape
     rows = 2 * half
@@ -465,28 +465,24 @@
         fetch(tail_hbm.at[tile], tail_ref.at[tile], gets.at[1, tile])
     assemble(xe_ref, low_ref, high_ref, slice(None))
 
-    def project(columns):
+    def project(tile):
+        columns = slice(tile * TILE, (tile + 1) * TILE)
         total = total_ref[:, columns] + mm(xe_ref[...], w_ref[:, columns])
-        ext_ref[...] = total.astype(BF).astype(F32)
+        ext_ref[tile] = total.astype(BF).astype(F32)
 
     rel = rel_ref[...]
-    project(slice(inner, inner + 2 * states))
-    both = conv_silu(ext_ref, cb_ref[...], bb_ref[...], rel, rows)
+    for tile in range(tiles + 1):
+        project(tile)
+    both = conv_silu(ext_ref.at[tiles], cb_ref[...], bb_ref[...], rel, rows)
     in_ref[...] = both[:, :states]
     outmap_ref[...] = both[:, states:]
-    put_maps = [
-        fetch(in_ref, in_hbm, puts.at[0]), fetch(outmap_ref, outmap_hbm, puts.at[1])
-    ]
+    put_map = fetch(in_ref, in_hbm, puts.at[0])
     across_ref[...] = both[:, :states].astype(F32).T.astype(BF)
-
-    def body(tile, _):
-        columns = pl.ds(pl.multiple_of(tile * TILE, TILE), TILE)
-        project(columns)
-        inner_rows = conv_silu(ext_ref, cx_ref[:, columns], bx_ref[:, columns], rel_ref[...], rows)
+    for tile in range(tiles):
+        columns = slice(tile * TILE, (tile + 1) * TILE)
+        inner_rows = conv_silu(ext_ref.at[tile], cx_ref[:, columns], bx_ref[:, columns], rel, rows)
         conv_ref[tile] = inner_rows
-        pltpu.make_async_copy(
-            conv_ref.at[tile], conv_hbm.at[:, columns], puts.at[2 + tile]
-        ).start()
+        fetch(conv_ref.at[tile], conv_hbm.at[:, pl.ds(tile * TILE, TILE)], puts.at[2 + tile])
         for at, (source, target) in enumerate(((steps_hbm, steps_ref), (tail_hbm, tail_ref))):
             pltpu.make_async_copy(source.at[tile], target.at[tile], gets.at[at, tile]).wait()
         inject = (inner_rows.astype(F32) * steps_ref[tile].astype(F32)).astype(BF)
@@ -500,42 +496,22 @@
                 mid_ref[:, columns] = carried.astype(BF)
             else:
                 carried = carry_ref[tile, block : block + 1] * carried + block_state
-        state_ref[:, columns] = carried
-        return 0
-
-    lax.fori_loop(0, tiles, body, 0)
+        mine_ref[:states, columns] = carried.astype(BF)
+        reach = carry_ref[tile, rows // BLK : rows // BLK + 1]
+        high = reach.astype(BF).astype(F32)
+        line = iota((HALO, TILE), 0)
+        codes = jnp.where(line == 0, high, jnp.where(line == 1, reach - high, 0.0))
+        mine_ref[states:, columns] = codes.astype(BF)
     put_mid = fetch(mid_ref, mid_hbm, puts.at[2 + tiles])
-    lines = states // 8
-
-    def tile_of(index):
-        column, line = index // lines, index % lines
-        return state_ref[line * 8 : line * 8 + 8, column * LANES : (column + 1) * LANES]
-
-    def codes_of(column):
-        per = TILE // LANES
-        at = rows // BLK
-        lanes = slice(column % per * LANES, (column % per + 1) * LANES)
-        gain = carry_ref[column // per, at : at + 1, lanes]
-        high = gain.astype(BF).astype(F32)
-        return high, gain - high
-
-    for dest in range(sent_ref.shape[0]):
-        first, second, shared = piece_tiles(dest)
-        columns = [index // lines for index in (first, second, shared)]
-        middle = tile_of(shared)[4 * (dest % 2) : 4 * (dest % 2) + 4]
-        piece = [tile_of(first), tile_of(second), middle]
-        piece += [*codes_of(min(columns)), *codes_of(max(columns))]
-        sent_ref[dest] = jnp.concatenate(piece, axis=0).astype(BF)
     put_mid.wait()
-    for copy in put_maps:
-        copy.wait()
+    put_map.wait()
     for tile in range(tiles):
         pltpu.make_async_copy(
             conv_ref.at[tile], conv_hbm.at[:, pl.ds(tile * TILE, TILE)], puts.at[2 + tile]
         ).wait()
 
 
-def front(piece, total, w_far, rel, carry, steps, tail, conv_x, bias_x, conv_bc, bias_bc, groups):
+def front(piece, total, w_far, rel, carry, steps, tail, conv_x, bias_x, conv_bc, bias_bc):
     half, width = piece[0].shape
     rows = 2 * half
     inner = conv_x.shape[1]
@@ -544,13 +520,13 @@
     return pl.pallas_call(
         front_kernel,
         in_specs=vmem(10) + hbm(2),
-        out_specs=hbm(1) + vmem(1) + hbm(3),
+        out_specs=hbm(1) + vmem(1) + hbm(2) + vmem(1),
         out_shape=[
             pltpu.HBM((rows, inner), BF),
-            jax.ShapeDtypeStruct((groups, PIECE, LANES), BF),
+            jax.ShapeDtypeStruct((states + HALO, inner), BF),
             pltpu.HBM((states, inner), BF),
             pltpu.HBM((rows, states), BF),
-            pltpu.HBM((rows, states), BF),
+            pltpu.VMEM((rows, states), BF),
         ],
         scratch_shapes=[
             pltpu.VMEM(steps.shape, BF),
@@ -558,11 +534,9 @@
             pltpu.VMEM((tiles, rows, TILE), BF),
             pltpu.VMEM((states, inner), BF),
             pltpu.VMEM((rows, states), BF),
-            pltpu.VMEM((rows, states), BF),
             pltpu.VMEM((states, rows), BF),
             pltpu.VMEM((rows + HALO, width), BF),
-            pltpu.VMEM((rows + HALO, TILE), F32),
-            pltpu.VMEM((states, inner), F32),
+            pltpu.VMEM((tiles + 1, rows + HALO, TILE), F32),
             pltpu.SemaphoreType.DMA((2, tiles)),
             pltpu.SemaphoreType.DMA((tiles + 3,)),
         ],
@@ -574,28 +548,143 @@
     )
 
 
+def combine_kernel(
+    core_ref, mine_ref, theirs_ref, sent_ref, kept_hbm, chip_ref, gain_ref, kept_ref, sem
+):
+    half, inner = chip_ref.shape
+    states = 2 * half
+    lines = half // 8
+    first = core_ref[0] == 0
+    span = pl.ds(pl.multiple_of(core_ref[0] * half, half), half)
+    own, other = mine_ref[span].astype(F32), theirs_ref[span].astype(F32)
+    own_codes, other_codes = mine_ref[states:].astype(F32), theirs_ref[states:].astype(F32)
+    early = jnp.where(first, own, other)
+    early_codes = jnp.where(first, own_codes, other_codes)
+    late_codes = jnp.where(first, other_codes, own_codes)
+    kept_ref[:half] = early.astype(BF)
+    kept_ref[half:] = early_codes.astype(BF)
+    put = fetch(kept_ref, kept_hbm, sem)
+    early_gain = early_codes[0:1] + early_codes[1:2]
+    late_gain = late_codes[0:1] + late_codes[1:2]
+    chip_ref[...] = late_gain * early + jnp.where(first, other, own)
+    gain_ref[...] = jnp.broadcast_to(early_gain * late_gain, gain_ref.shape)
+
+    def tile_of(index):
+        column, line = index // lines, index % lines
+        return chip_ref[line * 8 : line * 8 + 8, column * LANES : (column + 1) * LANES]
+
+    def codes_of(column):
+        gain = gain_ref[0:1, column * LANES : (column + 1) * LANES]
+        high = gain.astype(BF).astype(F32)
+        return high, gain - high
+
+    for dest in range(sent_ref.shape[0]):
+        one, two, shared = piece_tiles(dest)
+        columns = [index // lines for index in (one, two, shared)]
+        middle = tile_of(shared)[4 * (dest % 2) : 4 * (dest % 2) + 4]
+        piece = [tile_of(one), tile_of(two), middle]
+        piece += [*codes_of(min(columns)), *codes_of(max(columns))]
+        sent_ref[dest] = jnp.concatenate(piece, axis=0).astype(BF)
+    put.wait()
+
+
+def combine(core, mine, theirs, chips):
+    inner = mine.shape[1]
+    half = (mine.shape[0] - HALO) // 2
+    return pl.pallas_call(
+        combine_kernel,
+        in_specs=[pl.BlockSpec(memory_space=pltpu.SMEM)] + vmem(2),
+        out_specs=vmem(1) + hbm(1),
+        out_shape=[
+            jax.ShapeDtypeStruct((chips, PIECE, LANES), BF),
+            pltpu.HBM((half + HALO, inner), BF),
+        ],
+        scratch_shapes=[
+            pltpu.VMEM((half, inner), F32),
+            pltpu.VMEM((8, inner), F32),
+            pltpu.VMEM((half + HALO, inner), BF),
+            pltpu.SemaphoreType.DMA,
+        ],
+        name="combine",
+        **params(8, 1_000_000, 1_500_000),
+    )(core, near(mine), near(theirs))
+
+
+def entering_kernel(core_ref, recv_ref, kept_hbm, send_ref, keep_ref, kept_ref, enter_ref, sem):
+    get = fetch(kept_hbm, kept_ref, sem)
+    half, inner = enter_ref.shape
+    lines = half // 8
+    where = {}
+    for dest in range(recv_ref.shape[0]):
+        one, two, shared = piece_tiles(dest)
+        where[one] = (dest, 0)
+        where[two] = (dest, 1)
+        where.setdefault(shared, dest)
+
+    def tile_of(index):
+        if isinstance(where[index], tuple):
+            dest, at = where[index]
+            return recv_ref[dest].astype(F32)[8 * at : 8 * at + 8]
+        dest = where[index]
+        upper = recv_ref[dest].astype(F32)[16:20]
+        lower = recv_ref[dest + 1].astype(F32)[16:20]
+        return jnp.concatenate([upper, lower], axis=0)
+
+    for index in range(lines * inner // LANES):
+        column, line = index // lines, index % lines
+        enter_ref[line * 8 : line * 8 + 8, column * LANES : (column + 1) * LANES] = tile_of(index)
+    get.wait()
+    first = core_ref[0] == 0
+    codes = kept_ref[half:].astype(F32)
+    early = enter_ref[...]
+    late = (codes[0:1] + codes[1:2]) * early + kept_ref[:half].astype(F32)
+    send_ref[...] = jnp.where(first, late, early).astype(BF)
+    keep_ref[...] = jnp.where(first, early, late).astype(BF)
+
+
+def entering_halves(core, recv, kept):
+    rows, inner = kept.shape
+    half = rows - HALO
+    return pl.pallas_call(
+        entering_kernel,
+        in_specs=[pl.BlockSpec(memory_space=pltpu.SMEM)] + vmem(1) + hbm(1),
+        out_specs=vmem(2),
+        out_shape=[jax.ShapeDtypeStruct((half, inner), BF)] * 2,
+        scratch_shapes=[
+            pltpu.VMEM((rows, inner), BF),
+            pltpu.VMEM((half, inner), F32),
+            pltpu.SemaphoreType.DMA,
+        ],
+        name="entering_halves",
+        **params(8, 1_000_000, 1_500_000),
+    )(core, near(recv), far(kept))
+
+
 def inner_kernel(
-    rel_ref, skip_ref, low_hbm, high_hbm, in_hbm, outmap_hbm, conv_hbm, mid_hbm, part_hbm,
-    small_ref, in_ref, outmap_ref, conv_ref, mid_ref, part_ref,
+    rel_ref, skip_ref, outmap_ref, low_hbm, high_hbm, in_hbm, conv_hbm, mid_hbm, part_hbm,
+    small_ref, in_ref, conv_ref, mid_ref, part_ref,
     scores_ref, across_ref, gets, puts,
 ):
     half = low_hbm.shape[0]
-    gets = [
-        fetch(source, target, gets.at[at])
+    rows, inner = conv_ref.shape
+    tiles = inner // TILE
+    per = TILE // HD
+    first = [
+        fetch(source, target, gets.at[tiles + at])
         for at, (source, target) in enumerate(
             (
                 (low_hbm, small_ref.at[pl.ds(0, half)]),
                 (high_hbm, small_ref.at[pl.ds(half, half)]),
-                (in_hbm, in_ref), (outmap_hbm, outmap_ref),
-                (conv_hbm, conv_ref), (mid_hbm, mid_ref),
+                (in_hbm, in_ref),
             )
         )
     ]
-    for copy in gets:
+    get_mid = fetch(mid_hbm, mid_ref, gets.at[tiles + 3])
+    for tile in range(tiles):
+        columns = pl.ds(tile * TILE, TILE)
+        fetch(conv_hbm.at[:, columns], conv_ref.at[:, columns], gets.at[tile])
+    for copy in first:
         copy.wait()
-    rows, inner = conv_ref.shape
-    tiles = inner // TILE
-    per = TILE // HD
     ones = lower_ones(BLK)
     for block in range(rows // BLK):
         span = slice(block * BLK, (block + 1) * BLK)
@@ -607,6 +696,9 @@
 
     def body(tile, _):
         columns = pl.ds(pl.multiple_of(tile * TILE, TILE), TILE)
+        pltpu.make_async_copy(
+            conv_hbm.at[:, columns], conv_ref.at[:, columns], gets.at[tile]
+        ).wait()
         small = small_ref[...]
         steps = mm(small, head_spread(tile, 0))
         decays = mm(small, head_spread(tile, DECAY_AT)).astype(BF)
@@ -623,18 +715,25 @@
                     iota((BLK, 1), 0) < rel_ref[span], jnp.exp(cumulative), 0.0
                 )
                 total = total + enter * mm(outmap_ref[span], mid_ref[:, columns])
+            part = BLK // 2
+            pieces = [total[:part], total[part:]]
             for q in range(per):
                 down = cumulative[:, q * HD : q * HD + 1]
                 across = across_ref[block, pl.ds(DECAY_AT + per * tile + q, 1), :]
-                weights = (scores * jnp.exp(jnp.minimum(down - across, 0.0))).astype(BF)
                 mine = jnp.where(lane_head == q, inject[span], jnp.zeros((), BF))
-                total = total + mm(weights, mine)
+                for at, seen in ((0, part), (1, BLK)):
+                    lines = slice(at * part, (at + 1) * part)
+                    gap = jnp.minimum(down[lines] - across[:, :seen], 0.0)
+                    weights = (scores[lines, :seen] * jnp.exp(gap)).astype(BF)
+                    pieces[at] = pieces[at] + mm(weights, mine[:seen])
+            total = jnp.concatenate(pieces, axis=0)
             part_ref[span, columns] = total
         pltpu.make_async_copy(
             part_ref.at[:, columns], part_hbm.at[:, columns], puts.at[tile]
         ).start()
         return 0
 
+    get_mid.wait()
     lax.fori_loop(0, tiles, body, 0)
     for tile in range(tiles):
         columns = pl.ds(tile * TILE, TILE)
@@ -649,24 +748,23 @@
     tiles = inner // TILE
     return pl.pallas_call(
         inner_kernel,
-        in_specs=vmem(2) + hbm(6),
+        in_specs=vmem(3) + hbm(5),
         out_specs=hbm(1)[0],
         out_shape=pltpu.HBM((rows, inner), F32),
         scratch_shapes=[
             pltpu.VMEM((rows, LANES), BF),
             pltpu.VMEM(input_map.shape, BF),
-            pltpu.VMEM(output_map.shape, BF),
             pltpu.VMEM(conv.shape, BF),
             pltpu.VMEM(mid.shape, BF),
             pltpu.VMEM((rows, inner), F32),
             pltpu.VMEM((blocks, BLK, BLK), F32),
             pltpu.VMEM((blocks, 128, BLK), F32),
-            pltpu.SemaphoreType.DMA((6,)),
+            pltpu.SemaphoreType.DMA((tiles + 4,)),
             pltpu.SemaphoreType.DMA((tiles,)),
         ],
         name="inner_part",
         **params(24, 8 * rows * BLK * inner, 8_000_000),
-    )(rel, skip_wide, *[far(x) for x in (*small, input_map, output_map, conv, mid)])
+    )(rel, skip_wide, near(output_map), *[far(x) for x in (*small, input_map, conv, mid)])
 
 
 def scan_kernel(lines, me_ref, recv_ref, out_ref):
@@ -698,10 +796,10 @@
         functools.partial(scan_kernel, lines),
         in_specs=[pl.BlockSpec(memory_space=pltpu.SMEM)] + vmem(1),
         out_specs=pl.BlockSpec(memory_space=pltpu.VMEM),
-        out_shape=jax.ShapeDtypeStruct(recv.shape, BF),
+        out_shape=pltpu.VMEM(recv.shape, BF),
         name="scan_shards",
         **params(8, 10_000_000, 800_000),
-    )(me, recv)
+    )(me, near(recv))
 
 
 def prepare_kernel(rel_ref, low_hbm, high_hbm, gain_ref, small_ref, ones_ref, sems):
@@ -745,42 +843,20 @@
 
 
 def final_kernel(
-    recv_ref, gain_ref, outmap_hbm, part_hbm, out_hbm,
-    outmap_ref, part_ref, enter_ref, held_ref, gets, puts,
+    core_ref, keep_ref, got_ref, gain_ref, outmap_ref, part_hbm, out_hbm,
+    part_ref, enter_ref, held_ref, gets, puts,
 ):
     rows, inner = part_ref.shape
-    states = outmap_ref.shape[1]
-    lines = states // 8
+    half = keep_ref.shape[0]
     steps = rows // TAKEN
     spans = [pl.ds(step * TAKEN, TAKEN) for step in range(steps)]
-    get_map = fetch(outmap_hbm, outmap_ref, gets.at[steps])
     copies = [
         fetch(part_hbm.at[span], part_ref.at[span], gets.at[step])
         for step, span in enumerate(spans)
     ]
-    where = {}
-    for dest in range(recv_ref.shape[0]):
-        first, second, shared = piece_tiles(dest)
-        where[first] = (dest, 0)
-        where[second] = (dest, 1)
-        where.setdefault(shared, dest)
-
-    def tile_of(index):
-        if isinstance(where[index], tuple):
-            dest, at = where[index]
-            return recv_ref[dest].astype(F32)[8 * at : 8 * at + 8]
-        dest = where[index]
-        upper = recv_ref[dest].astype(F32)[16:20]
-        lower = recv_ref[dest + 1].astype(F32)[16:20]
-        return jnp.concatenate([upper, lower], axis=0)
-
-    def column_of(column):
-        parts = [tile_of(column * lines + line) for line in range(lines)]
-        return jnp.concatenate(parts, axis=0).astype(BF)
-
-    for column in range(inner // LANES):
-        enter_ref[:, column * LANES : (column + 1) * LANES] = column_of(column)
-    get_map.wait()
+    core = core_ref[0]
+    enter_ref[pl.ds(pl.multiple_of(core * half, half), half)] = keep_ref[...]
+    enter_ref[pl.ds(pl.multiple_of((1 - core) * half, half), half)] = got_ref[...]
     puts_made = []
     for step, span in enumerate(spans):
         outer = mm(outmap_ref[span], enter_ref[...])
@@ -791,25 +867,24 @@
         copy.wait()
 
 
-def final(output_map, part, gain, recv):
+def final(core, output_map, part, gain, keep, got):
     rows, inner = part.shape
     states = output_map.shape[1]
     return pl.pallas_call(
         final_kernel,
-        in_specs=vmem(2) + hbm(2),
+        in_specs=[pl.BlockSpec(memory_space=pltpu.SMEM)] + vmem(4) + hbm(1),
         out_specs=hbm(1)[0],
         out_shape=jax.ShapeDtypeStruct((rows, inner), BF),
         scratch_shapes=[
-            pltpu.VMEM((rows, states), BF),
             pltpu.VMEM((rows, inner), F32),
             pltpu.VMEM((states, inner), BF),
             pltpu.VMEM((rows, inner), BF),
-            pltpu.SemaphoreType.DMA((rows // TAKEN + 1,)),
+            pltpu.SemaphoreType.DMA((rows // TAKEN,)),
             pltpu.SemaphoreType.DMA((rows // TAKEN,)),
         ],
         name="final",
         **params(16, 2 * rows * states * inner, 7_000_000),
-    )(near(recv), near(gain), far(output_map), far(part))
+    )(core, near(keep), near(got), near(gain), near(output_map), far(part))
 
 
 def on_device(tokens, dt_decay, dest, lengths, w_x, w_bc, conv_x, conv_bc, bias_x, bias_bc, skip):
@@ -846,21 +921,36 @@
     total = project_near(
         (low_left, high_left), (low_right, high_right), w_left, w_right, total
     )
-    conv, state, mid, input_map, output_map = front(
+    conv, mine, mid, input_map, output_map = front(
         (low_far, high_far), total, w_far, rel, carry, steps, tail,
-        conv_x, bias_x[None, :], conv_bc, bias_bc[None, :], groups,
+        conv_x, bias_x[None, :], conv_bc, bias_bc[None, :],
     )
-    gathered = lax.all_to_all(state, "ctx", split_axis=0, concat_axis=0, tiled=True)
+    place = lax.axis_index("ctx").astype(jnp.int32)
+    core, chip = (place % 2)[None], (place // 2)[None]
+    chips = groups // 2
+    peers = [[2 * at + half for at in range(chips)] for half in range(2)]
+    swap = [(i, i ^ 1) for i in range(groups)]
+
+    def exchange(x):
+        return lax.all_to_all(
+            x, "ctx", split_axis=0, concat_axis=0, tiled=True, axis_index_groups=peers
+        )
+
+    theirs = lax.ppermute(mine, "ctx", swap)
+    sent, kept = combine(core, mine, theirs, chips)
+    sent, conv = lax.optimization_barrier((sent, conv))
+    gathered = exchange(sent)
     part = inner_part(
         small, rel, input_map, output_map, conv, mid, jnp.repeat(skip, HD)[None, :]
     )
     gathered, part = lax.optimization_barrier((gathered, part))
-    spot = lax.axis_index("ctx").astype(jnp.int32)[None]
-    entering = scan_shards(spot, gathered, input_map.shape[1] // 8)
+    entering = scan_shards(chip, gathered, input_map.shape[1] // 16)
     entering, rel = lax.optimization_barrier((entering, rel))
     gain = prepare(rel, small, inner)
-    enter = lax.all_to_all(entering, "ctx", split_axis=0, concat_axis=0, tiled=True)
-    return final(output_map, part, gain, enter)
+    arrived, gain = lax.optimization_barrier((exchange(entering), gain))
+    send, keep = entering_halves(core, arrived, kept)
+    got = lax.ppermute(send, "ctx", swap)
+    return final(core, output_map, part, gain, keep, got)
 
 
 def solution(mesh):

time: 140 us -> 137 us (0.979)
  waiting for transfers between devices: 58.8 us -> 51.6 us
  starting transfers between devices: 37 us -> 41 us
    all_to_all x2, waiting for transfers between devices: 16.8 us -> 7.3 us  [exchange(): lax.all_to_all(x, 'ctx', split_axis=0, concat_axis=0, tiled=True, axis_in...]
    ppermute x0 -> x2, starting transfers between devices: none -> 3.61 us  [the longest x1 2.94 us: on_device(): got = lax.ppermute(send, 'ctx', swap)]
    ppermute x0 -> x2, waiting for transfers between devices: none -> 2.34 us  [the longest x1 1.31 us: on_device(): theirs = lax.ppermute(mine, 'ctx', swap)]
    pallas_call x2 -> x4, Pallas kernels: 11.6 us -> 13.1 us  [the longest x1 7.65 us: inner_part(): pl.pallas_call(inner_kernel, in_specs=vmem(3) + hbm(5), out_specs=hbm(1)[...]
  transfers between devices with their start and end apart: 10 -> 12, of which waited for: 8 -> 10; matrix products, arithmetic and copies ran while one was open for 1% -> 1% of each run, Pallas kernels for 17% -> 17%
where the time goes in v5:
time: 137 us
  waiting for transfers between devices  51.6 us (38%)
  Pallas kernels  42.5 us (31%)
  starting transfers between devices  41 us (30%)
    all_to_all x1, waiting for transfers between devices, on_device(): lax.all_to_all(sent, 'ctx', split_axis=0, concat_axis=0, tiled=True)  36.6 us
    all_to_all x1, starting transfers between devices, on_device(): lax.all_to_all(sent, 'ctx', split_axis=0, concat_axis=0, tiled=True)  13.2 us
    all_to_all x2, starting transfers between devices, exchange(): lax.all_to_all(x, 'ctx', split_axis=0, concat_axis=0, tiled=True, axis_in...  12.6 us
    ppermute x6, starting transfers between devices, turned(): return lax.ppermute(x, 'head', [(i, (i + by) % ring) for i in range(ring)])  8.73 us
    pallas_call x1, Pallas kernels, front(): pl.pallas_call(front_kernel, in_specs=vmem(10) + hbm(2), out_specs=hbm(1)...  7.72 us
    pallas_call x1, Pallas kernels, inner_part(): pl.pallas_call(inner_kernel, in_specs=vmem(3) + hbm(5), out_specs=hbm(1)[...  7.65 us
    all_to_all x2, waiting for transfers between devices, exchange(): lax.all_to_all(x, 'ctx', split_axis=0, concat_axis=0, tiled=True, axis_in...  7.3 us
    ppermute x6, waiting for transfers between devices, turned(): return lax.ppermute(x, 'head', [(i, (i + by) % ring) for i in range(ring)])  5.42 us
  transfers between devices with their start and end apart: 12, of which 10 were waited for; matrix products, arithmetic and copies ran while one was open for 1% of the time, Pallas kernels for 17%

profile of v5, /device:TPU:1, one launch (start us, length us, event | category | flops | bytes accessed | tf_op | source)
XLA Modules:
  0.0 136.6 jit_solution(612282919897260990)
XLA Ops:
  0.0 3.4 %pack.1 = bf16[64,88,128]{2,1,0:T(8,128)(2,1)} custom-call(s32[1,512]{1,0:T(1,128)} %bitcast.12, bf16[20,2,512]{2,1,0:T(2,128)(2,1)} %bitcast.11, bf16[512,640]{1,0:T(8,128)(2,1)} %tok_hbm.1), custom_call_target="tpu_custom_call" | custom-call | flops 805306368 | bytes 1310720 | tf_op jit(solution)/shard_map/pack/pallas_call | solution.py:139
  3.5 13.2 %all-to-all-start = ((bf16[64,88,128]{2,1,0:T(8,128)(2,1)}), bf16[64,88,128]{2,1,0:T(8,128)(2,1)S(1)}, u32[]{:S(2)}, u32[]{:S(2)}) async-start(bf16[64,88,128]{2,1,0:T(8,128)(2,1)} %pack.1), calls=%async_computation | async-start | bytes 2883584 | tf_op jit(solution)/shard_map/all_to_all | solution.py:897
  17.1 36.6 %all-to-all-done.recv_ref = bf16[64,88,128]{2,1,0:T(8,128)(2,1)S(1)} async-done(((bf16[64,88,128]{2,1,0:T(8,128)(2,1)}), bf16[64,88,128]{2,1,0:T(8,128)(2,1)S(1)}, u32[]{:S(2)}, u32[]{:S(2)}) %all-to-all-start) | async-done | bytes 1441824 | tf_op jit(solution)/shard_map/all_to_all | solution.py:897
  53.6 1.2 unpack_low.1
  55.9 3.0 %collective-permute-start.2 = (bf16[16,640]{1,0:T(8,128)(2,1)S(1)}, bf16[16,640]{1,0:T(8,128)(2,1)S(1)}, u32[]{:S(2)}, u32[]{:S(2)}) collective-permute-start(bf16[16,640]{1,0:T(8,128)(2,1)S(1)} %get-tuple-element.40), channel_id=1, source_target_pairs={{0,4},{4,8},{8,12},{12,16},{16,20},{20,24},{24,28},{28,32},{32,36}... | collective-permute-start | bytes 61448 | tf_op jit(solution)/shard_map/ppermute | solution.py:904
  59.3 1.3 collective-permute-start
  60.6 1.7 %collective-permute-start.3 = (bf16[272,640]{1,0:T(8,128)(2,1)S(1)}, bf16[272,640]{1,0:T(8,128)(2,1)S(1)}, u32[]{:S(2)}, u32[]{:S(2)}) collective-permute-start(bf16[272,640]{1,0:T(8,128)(2,1)S(1)} %constant_dynamic-update-slice_fusion.high_ref), channel_id=1, source_target_pairs={{0,3},{1,0},{2,1},{3,2},{4,7},{5,4},{6,5},{7,6},{8,11},{9,8},{10,9... | collective-permute-start | bytes 1044488 | tf_op jit(solution)/shard_map/ppermute | solution.py:901
  62.3 4.4 %decay_factors.1 = (bf16[5,512,256]{2,1,0:T(8,128)(2,1)}, f32[5,512,256]{2,1,0:T(8,128)}, f32[5,8,256]{2,1,0:T(8,128)S(1)}) custom-call(s32[512,1]{1,0:T(8,128)S(1)} %add_subtract_fusion.rel_ref, bf16[256,128]{1,0:T(8,128)(2,1)} %get-tuple-element.41.low_hbm, bf16[256,128]{1,0:T(8,128)(2,1)} %get-tuple-element.42.high_hbm), custom_call_target="tpu_custom_call" | custom-call | flops 671088640 | bytes 7000000 | tf_op jit(solution)/shard_map/decay_factors/pallas_call | solution.py:337
  66.8 2.7 %collective-permute-start.6 = (bf16[256,640]{1,0:T(8,128)(2,1)S(1)}, bf16[256,640]{1,0:T(8,128)(2,1)S(1)}, u32[]{:S(2)}, u32[]{:S(2)}) collective-permute-start(bf16[256,640]{1,0:T(8,128)(2,1)S(1)} %get-tuple-element.37.low_ref), channel_id=1, source_target_pairs={{0,3},{1,0},{2,1},{3,2},{4,7},{5,4},{6,5},{7,6},{8,11},{9,8},{10,9... | collective-permute-start | bytes 983048 | tf_op jit(solution)/shard_map/ppermute | solution.py:901
  70.6 3.0 %collective-permute-start.4 = (bf16[272,640]{1,0:T(8,128)(2,1)S(1)}, bf16[272,640]{1,0:T(8,128)(2,1)S(1)}, u32[]{:S(2)}, u32[]{:S(2)}) collective-permute-start(bf16[272,640]{1,0:T(8,128)(2,1)S(1)} %collective-permute-done.3.high3), channel_id=1, source_target_pairs={{0,3},{1,0},{2,1},{3,2},{4,7},{5,4},{6,5},{7,6},{8,11},{9,8},{10,9... | collective-permute-start | bytes 1044488 | tf_op jit(solution)/shard_map/ppermute | solution.py:901
  73.6 3.9 %project_own.1 = (f32[528,1536]{1,0:T(8,128)S(1)}, bf16[640,1536]{1,0:T(8,128)(2,1)S(1)}, bf16[640,1536]{1,0:T(8,128)(2,1)S(1)}, bf16[640,1536]{1,0:T(8,128)(2,1)S(1)}) custom-call(s32[1]{0:T(128)} %bitcast.6.me_ref, bf16[256,640]{1,0:T(8,128)(2,1)S(1)} %get-tuple-element.37.low_ref, bf16[272,640]{1,0:T(8,128)(2,1)S(1)} %constant_dynamic-update-slice_fusion.high_ref, ...), custom_call_target="tpu_custom_call" | custom-call | flops 1038090240 | bytes 8000000 | tf_op jit(solution)/shard_map/project_own/pallas_call | solution.py:400
  77.9 3.2 %project_near.1.total_ref = f32[528,1536]{1,0:T(8,128)S(1)} custom-call(bf16[256,640]{1,0:T(8,128)(2,1)S(1)} %collective-permute-done.low1, bf16[272,640]{1,0:T(8,128)(2,1)S(1)} %collective-permute-done.5.high1, bf16[256,640]{1,0:T(8,128)(2,1)S(1)} %collective-permute-done.6.low3, bf16[272,640]{1,0:T(8,128)(2,1)S(1)} %collective-permute-done.3.high3, ...), custom_call_target="tpu_custom_call" | custom-call | flops 2076180480 | bytes 8000000 | tf_op jit(solution)/shard_map/project_near/pallas_call | solution.py:434
  81.2 3.5 %collective-permute-done.1.low_ref = bf16[256,640]{1,0:T(8,128)(2,1)S(1)} collective-permute-done((bf16[256,640]{1,0:T(8,128)(2,1)S(1)}, bf16[256,640]{1,0:T(8,128)(2,1)S(1)}, u32[]{:S(2)}, u32[]{:S(2)}) %collective-permute-start.1) | collective-permute-done | bytes 327712 | tf_op jit(solution)/shard_map/ppermute | solution.py:901
  85.1 7.7 %front.1 = (bf16[512,1280]{1,0:T(8,128)(2,1)}, bf16[144,1280]{1,0:T(8,128)(2,1)S(1)}, bf16[128,1280]{1,0:T(8,128)(2,1)}, bf16[512,128]{1,0:T(8,128)(2,1)}, bf16[512,128]{1,0:T(8,128)(2,1)S(1)}) custom-call(bf16[256,640]{1,0:T(8,128)(2,1)S(1)} %collective-permute-done.1.low_ref, bf16[272,640]{1,0:T(8,128)(2,1)S(1)} %collective-permute-done.4.high_ref, ...), custom_call_target="tpu_custom_call" | custom-call | flops 1006632960 | bytes 12000000 | tf_op jit(solution)/shard_map/front/pallas_call | solution.py:520
  93.5 1.3 collective-permute-done.7.theirs_ref
  94.8 1.5 %combine.1 = (bf16[32,24,128]{2,1,0:T(8,128)(2,1)}, bf16[80,1280]{1,0:T(8,128)(2,1)}) custom-call(s32[1]{0:T(128)} %bitcast.core_ref, bf16[144,1280]{1,0:T(8,128)(2,1)S(1)} %get-tuple-element.52.mine_ref, bf16[144,1280]{1,0:T(8,128)(2,1)S(1)} %collective-permute-done.7.theirs_ref), custom_call_target="tpu_custom_call" | custom-call | flops 1000000 | bytes 1500000 | tf_op jit(solution)/shard_map/combine/pallas_call | solution.py:594
  96.3 4.9 %all-to-all-start.1 = ((bf16[32,24,128]{2,1,0:T(8,128)(2,1)}), bf16[32,24,128]{2,1,0:T(8,128)(2,1)S(1)}, u32[]{:S(2)}, u32[]{:S(2)}) async-start(bf16[32,24,128]{2,1,0:T(8,128)(2,1)} %get-tuple-element.55), calls=%async_computation.1 | async-start | bytes 393216 | tf_op jit(solution)/shard_map/all_to_all | solution.py:935
  101.3 7.6 %inner_part.1.part_hbm = f32[512,1280]{1,0:T(8,128)} custom-call(s32[512,1]{1,0:T(8,128)S(1)} %add_subtract_fusion.rel_ref, f32[1,1280]{1,0:T(1,128)S(1)} %broadcast_in_dim_reshape.3.skip_ref, bf16[512,128]{1,0:T(8,128)(2,1)S(1)} %get-tuple-element.56.outmap_ref, bf16[256,128]{1,0:T(8,128)(2,1)} %get-tuple-element.41.low_hbm, ...), custom_call_target="tpu_custom_call" | custom-call | flops 1342177280 | bytes 8000000 | tf_op jit(solution)/shard_map/inner_part/pallas_call | solution.py:749
  108.9 1.6 %all-to-all-done.1.recv_ref = bf16[32,24,128]{2,1,0:T(8,128)(2,1)S(1)} async-done(((bf16[32,24,128]{2,1,0:T(8,128)(2,1)}), bf16[32,24,128]{2,1,0:T(8,128)(2,1)S(1)}, u32[]{:S(2)}, u32[]{:S(2)}) %all-to-all-start.1) | async-done | bytes 196640 | tf_op jit(solution)/shard_map/all_to_all | solution.py:935
  111.3 7.7 %all-to-all-start.2 = ((bf16[32,24,128]{2,1,0:T(8,128)(2,1)}), bf16[32,24,128]{2,1,0:T(8,128)(2,1)S(1)}, u32[]{:S(2)}, u32[]{:S(2)}) async-start(bf16[32,24,128]{2,1,0:T(8,128)(2,1)} %scan_shards.1), calls=%async_computation.2 | async-start | bytes 393216 | tf_op jit(solution)/shard_map/all_to_all | solution.py:935
  119.0 3.7 %prepare.1.gain_ref = f32[512,1280]{1,0:T(8,128)S(1)} custom-call(s32[512,1]{1,0:T(8,128)S(1)} %add_subtract_fusion.rel_ref, bf16[256,128]{1,0:T(8,128)(2,1)} %get-tuple-element.41.low_hbm, bf16[256,128]{1,0:T(8,128)(2,1)} %get-tuple-element.42.high_hbm), custom_call_target="tpu_custom_call" | custom-call | flops 671088640 | bytes 8000000 | tf_op jit(solution)/shard_map/prepare/pallas_call | solution.py:830
  122.7 5.7 %all-to-all-done.2.recv_ref = bf16[32,24,128]{2,1,0:T(8,128)(2,1)S(1)} async-done(((bf16[32,24,128]{2,1,0:T(8,128)(2,1)}), bf16[32,24,128]{2,1,0:T(8,128)(2,1)S(1)}, u32[]{:S(2)}, u32[]{:S(2)}) %all-to-all-start.2) | async-done | bytes 196640 | tf_op jit(solution)/shard_map/all_to_all | solution.py:935
  129.5 2.9 %collective-permute-start.8 = (bf16[64,1280]{1,0:T(8,128)(2,1)S(1)}, bf16[64,1280]{1,0:T(8,128)(2,1)S(1)}, u32[]{:S(2)}, u32[]{:S(2)}) collective-permute-start(bf16[64,1280]{1,0:T(8,128)(2,1)S(1)} %get-tuple-element.66), channel_id=1, source_target_pairs={{0,4},{4,0},{8,12},{12,8},{16,20},{20,16},{24,28},{28,24},{32,36},... | collective-permute-start | bytes 491528 | tf_op jit(solution)/shard_map/ppermute | solution.py:952
  133.4 3.0 %final.1 = bf16[512,1280]{1,0:T(8,128)(2,1)} custom-call(s32[1]{0:T(128)} %bitcast.core_ref, bf16[64,1280]{1,0:T(8,128)(2,1)S(1)} %get-tuple-element.65.keep_ref, bf16[64,1280]{1,0:T(8,128)(2,1)S(1)} %collective-permute-done.8.got_ref, f32[512,1280]{1,0:T(8,128)S(1)} %prepare.1.gain_ref, bf16[512,128]{1,0:T(8,128)(2,1)S(1)} %get-tuple-element.56.outmap_ref, ...), custom_call_target="tpu_custom_call" | custom-call | flops 167772160 | bytes 7000000 | tf_op jit(solution)/shard_map/final/pallas_call | solution.py:873
  (37 shorter events, 7.7 us)
Async XLA Ops:
  3.5 13.2 %copy-start.4 = (s32[128]{0:T(128)S(1)}, s32[128]{0:T(128)}, u32[]{:S(2)}) copy-start(s32[128]{0:T(128)} %param.14) | copy-start | bytes 1540
  3.5 50.2 %all-to-all-start = ((bf16[64,88,128]{2,1,0:T(8,128)(2,1)}), bf16[64,88,128]{2,1,0:T(8,128)(2,1)S(1)}, u32[]{:S(2)}, u32[]{:S(2)}) async-start(bf16[64,88,128]{2,1,0:T(8,128)(2,1)} %pack.1), calls=%async_computation | async-start | bytes 2883584 | tf_op jit(solution)/shard_map/all_to_all | solution.py:897
  55.9 17.7 %copy-start.3 = (f32[1280]{0:T(1024)S(1)}, f32[1280]{0:T(1024)}, u32[]{:S(2)}) copy-start(f32[1280]{0:T(1024)} %param.19) | copy-start | bytes 15364
  55.9 4.7 %collective-permute-start.2 = (bf16[16,640]{1,0:T(8,128)(2,1)S(1)}, bf16[16,640]{1,0:T(8,128)(2,1)S(1)}, u32[]{:S(2)}, u32[]{:S(2)}) collective-permute-start(bf16[16,640]{1,0:T(8,128)(2,1)S(1)} %get-tuple-element.40), channel_id=1, source_target_pairs={{0,4},{4,8},{8,12},{12,16},{16,20},{20,24},{24,28},{28,32},{32,36}... | collective-permute-start | bytes 61448 | tf_op jit(solution)/shard_map/ppermute | solution.py:904
  59.3 14.3 %collective-permute-start = (bf16[256,640]{1,0:T(8,128)(2,1)S(1)}, bf16[256,640]{1,0:T(8,128)(2,1)S(1)}, u32[]{:S(2)}, u32[]{:S(2)}) collective-permute-start(bf16[256,640]{1,0:T(8,128)(2,1)S(1)} %get-tuple-element.37.low_ref), channel_id=1, source_target_pairs={{0,1},{1,2},{2,3},{3,0},{4,5},{5,6},{6,7},{7,4},{8,9},{9,10},{10,1... | collective-permute-start | bytes 983048 | tf_op jit(solution)/shard_map/ppermute | solution.py:901
  60.6 10.0 %collective-permute-start.3 = (bf16[272,640]{1,0:T(8,128)(2,1)S(1)}, bf16[272,640]{1,0:T(8,128)(2,1)S(1)}, u32[]{:S(2)}, u32[]{:S(2)}) collective-permute-start(bf16[272,640]{1,0:T(8,128)(2,1)S(1)} %constant_dynamic-update-slice_fusion.high_ref), channel_id=1, source_target_pairs={{0,3},{1,0},{2,1},{3,2},{4,7},{5,4},{6,5},{7,6},{8,11},{9,8},{10,9... | collective-permute-start | bytes 1044488 | tf_op jit(solution)/shard_map/ppermute | solution.py:901
  66.7 11.2 %collective-permute-start.5 = (bf16[272,640]{1,0:T(8,128)(2,1)S(1)}, bf16[272,640]{1,0:T(8,128)(2,1)S(1)}, u32[]{:S(2)}, u32[]{:S(2)}) collective-permute-start(bf16[272,640]{1,0:T(8,128)(2,1)S(1)} %constant_dynamic-update-slice_fusion.high_ref), channel_id=1, source_target_pairs={{0,1},{1,2},{2,3},{3,0},{4,5},{5,6},{6,7},{7,4},{8,9},{9,10},{10,1... | collective-permute-start | bytes 1044488 | tf_op jit(solution)/shard_map/ppermute | solution.py:901
  66.8 10.8 %collective-permute-start.6 = (bf16[256,640]{1,0:T(8,128)(2,1)S(1)}, bf16[256,640]{1,0:T(8,128)(2,1)S(1)}, u32[]{:S(2)}, u32[]{:S(2)}) collective-permute-start(bf16[256,640]{1,0:T(8,128)(2,1)S(1)} %get-tuple-element.37.low_ref), channel_id=1, source_target_pairs={{0,3},{1,0},{2,1},{3,2},{4,7},{5,4},{6,5},{7,6},{8,11},{9,8},{10,9... | collective-permute-start | bytes 983048 | tf_op jit(solution)/shard_map/ppermute | solution.py:901
  70.6 14.5 %collective-permute-start.4 = (bf16[272,640]{1,0:T(8,128)(2,1)S(1)}, bf16[272,640]{1,0:T(8,128)(2,1)S(1)}, u32[]{:S(2)}, u32[]{:S(2)}) collective-permute-start(bf16[272,640]{1,0:T(8,128)(2,1)S(1)} %collective-permute-done.3.high3), channel_id=1, source_target_pairs={{0,3},{1,0},{2,1},{3,2},{4,7},{5,4},{6,5},{7,6},{8,11},{9,8},{10,9... | collective-permute-start | bytes 1044488 | tf_op jit(solution)/shard_map/ppermute | solution.py:901
  73.6 11.1 %collective-permute-start.1 = (bf16[256,640]{1,0:T(8,128)(2,1)S(1)}, bf16[256,640]{1,0:T(8,128)(2,1)S(1)}, u32[]{:S(2)}, u32[]{:S(2)}) collective-permute-start(bf16[256,640]{1,0:T(8,128)(2,1)S(1)} %collective-permute-done.low1), channel_id=1, source_target_pairs={{0,1},{1,2},{2,3},{3,0},{4,5},{5,6},{6,7},{7,4},{8,9},{9,10},{10,1... | collective-permute-start | bytes 983048 | tf_op jit(solution)/shard_map/ppermute | solution.py:901
  77.9 7.1 %copy-start = (f32[4,1280]{1,0:T(4,128)S(1)}, f32[4,1280]{1,0:T(4,128)}, u32[]{:S(2)}) copy-start(f32[4,1280]{1,0:T(4,128)} %cx_ref.1) | copy-start | bytes 61444
  77.9 7.1 %copy-start.1 = (f32[4,256]{1,0:T(4,128)S(1)}, f32[4,256]{1,0:T(4,128)}, u32[]{:S(2)}) copy-start(f32[4,256]{1,0:T(4,128)} %cb_ref.1) | copy-start | bytes 12292
  77.9 7.1 %copy-start.2 = (f32[256]{0:T(256)S(1)}, f32[256]{0:T(256)}, u32[]{:S(2)}) copy-start(f32[256]{0:T(256)} %param.20) | copy-start | bytes 3076
  85.1 16.1 %copy-start.5 = (f32[20]{0:T(128)S(1)}, f32[20]{0:T(128)}, u32[]{:S(2)}) copy-start(f32[20]{0:T(128)} %param.21) | copy-start | bytes 244
  92.8 2.0 %collective-permute-start.7 = (bf16[144,1280]{1,0:T(8,128)(2,1)S(1)}, bf16[144,1280]{1,0:T(8,128)(2,1)S(1)}, u32[]{:S(2)}, u32[]{:S(2)}) collective-permute-start(bf16[144,1280]{1,0:T(8,128)(2,1)S(1)} %get-tuple-element.52.mine_ref), channel_id=1, source_target_pairs={{0,4},{4,0},{8,12},{12,8},{16,20},{20,16},{24,28},{28,24},{32,36},... | collective-permute-start | bytes 1105928 | tf_op jit(solution)/shard_map/ppermute | solution.py:939
  96.3 14.3 %all-to-all-start.1 = ((bf16[32,24,128]{2,1,0:T(8,128)(2,1)}), bf16[32,24,128]{2,1,0:T(8,128)(2,1)S(1)}, u32[]{:S(2)}, u32[]{:S(2)}) async-start(bf16[32,24,128]{2,1,0:T(8,128)(2,1)} %get-tuple-element.55), calls=%async_computation.1 | async-start | bytes 393216 | tf_op jit(solution)/shard_map/all_to_all | solution.py:935
  111.3 17.1 %all-to-all-start.2 = ((bf16[32,24,128]{2,1,0:T(8,128)(2,1)}), bf16[32,24,128]{2,1,0:T(8,128)(2,1)S(1)}, u32[]{:S(2)}, u32[]{:S(2)}) async-start(bf16[32,24,128]{2,1,0:T(8,128)(2,1)} %scan_shards.1), calls=%async_computation.2 | async-start | bytes 393216 | tf_op jit(solution)/shard_map/all_to_all | solution.py:935
  129.5 4.0 %collective-permute-start.8 = (bf16[64,1280]{1,0:T(8,128)(2,1)S(1)}, bf16[64,1280]{1,0:T(8,128)(2,1)S(1)}, u32[]{:S(2)}, u32[]{:S(2)}) collective-permute-start(bf16[64,1280]{1,0:T(8,128)(2,1)S(1)} %get-tuple-element.66), channel_id=1, source_target_pairs={{0,4},{4,0},{8,12},{12,8},{16,20},{20,16},{24,28},{28,24},{32,36},... | collective-permute-start | bytes 491528 | tf_op jit(solution)/shard_map/ppermute | solution.py:952

commit v6 on v5

--- a/solution.py
+++ b/solution.py
@@ -451,8 +451,8 @@
 def front_kernel(
     low_ref, high_ref, total_ref, w_ref, rel_ref, carry_ref, cx_ref, bx_ref, cb_ref, bb_ref,
     steps_hbm, tail_hbm,
-    conv_hbm, mine_ref, mid_hbm, in_hbm, outmap_ref,
-    steps_ref, tail_ref, conv_ref, mid_ref, in_ref, across_ref,
+    conv_hbm, mine_ref, in_hbm, outmap_ref,
+    steps_ref, tail_ref, conv_ref, in_ref, across_ref,
     xe_ref, ext_ref, gets, puts,
 ):
     half, width = low_ref.shape
@@ -493,7 +493,6 @@
             block_state = mm(across_ref[:, span], decayed[span])
             if carried is None:
                 carried = block_state
-                mid_ref[:, columns] = carried.astype(BF)
             else:
                 carried = carry_ref[tile, block : block + 1] * carried + block_state
         mine_ref[:states, columns] = carried.astype(BF)
@@ -502,8 +501,6 @@
         line = iota((HALO, TILE), 0)
         codes = jnp.where(line == 0, high, jnp.where(line == 1, reach - high, 0.0))
         mine_ref[states:, columns] = codes.astype(BF)
-    put_mid = fetch(mid_ref, mid_hbm, puts.at[2 + tiles])
-    put_mid.wait()
     put_map.wait()
     for tile in range(tiles):
         pltpu.make_async_copy(
@@ -520,11 +517,10 @@
     return pl.pallas_call(
         front_kernel,
         in_specs=vmem(10) + hbm(2),
-        out_specs=hbm(1) + vmem(1) + hbm(2) + vmem(1),
+        out_specs=hbm(1) + vmem(1) + hbm(1) + vmem(1),
         out_shape=[
             pltpu.HBM((rows, inner), BF),
             jax.ShapeDtypeStruct((states + HALO, inner), BF),
-            pltpu.HBM((states, inner), BF),
             pltpu.HBM((rows, states), BF),
             pltpu.VMEM((rows, states), BF),
         ],
@@ -532,13 +528,12 @@
             pltpu.VMEM(steps.shape, BF),
             pltpu.VMEM(tail.shape, F32),
             pltpu.VMEM((tiles, rows, TILE), BF),
-            pltpu.VMEM((states, inner), BF),
             pltpu.VMEM((rows, states), BF),
             pltpu.VMEM((states, rows), BF),
             pltpu.VMEM((rows + HALO, width), BF),
             pltpu.VMEM((tiles + 1, rows + HALO, TILE), F32),
             pltpu.SemaphoreType.DMA((2, tiles)),
-            pltpu.SemaphoreType.DMA((tiles + 3,)),
+            pltpu.SemaphoreType.DMA((tiles + 2,)),
         ],
         name="front",
         **params(20, 2 * rows * width * (inner + 2 * states), 12_000_000),
@@ -610,8 +605,7 @@
     )(core, near(mine), near(theirs))
 
 
-def entering_kernel(core_ref, recv_ref, kept_hbm, send_ref, keep_ref, kept_ref, enter_ref, sem):
-    get = fetch(kept_hbm, kept_ref, sem)
+def entering_kernel(core_ref, recv_ref, kept_ref, send_ref, keep_ref, enter_ref):
     half, inner = enter_ref.shape
     lines = half // 8
     where = {}
@@ -633,7 +627,6 @@
     for index in range(lines * inner // LANES):
         column, line = index // lines, index % lines
         enter_ref[line * 8 : line * 8 + 8, column * LANES : (column + 1) * LANES] = tile_of(index)
-    get.wait()
     first = core_ref[0] == 0
     codes = kept_ref[half:].astype(F32)
     early = enter_ref[...]
@@ -647,23 +640,19 @@
     half = rows - HALO
     return pl.pallas_call(
         entering_kernel,
-        in_specs=[pl.BlockSpec(memory_space=pltpu.SMEM)] + vmem(1) + hbm(1),
+        in_specs=[pl.BlockSpec(memory_space=pltpu.SMEM)] + vmem(2),
         out_specs=vmem(2),
         out_shape=[jax.ShapeDtypeStruct((half, inner), BF)] * 2,
-        scratch_shapes=[
-            pltpu.VMEM((rows, inner), BF),
-            pltpu.VMEM((half, inner), F32),
-            pltpu.SemaphoreType.DMA,
-        ],
+        scratch_shapes=[pltpu.VMEM((half, inner), F32)],
         name="entering_halves",
         **params(8, 1_000_000, 1_500_000),
-    )(core, near(recv), far(kept))
+    )(core, near(recv), near(kept))
 
 
 def inner_kernel(
-    rel_ref, skip_ref, outmap_ref, low_hbm, high_hbm, in_hbm, conv_hbm, mid_hbm, part_hbm,
-    small_ref, in_ref, conv_ref, mid_ref, part_ref,
-    scores_ref, across_ref, gets, puts,
+    rel_ref, skip_ref, outmap_ref, low_hbm, high_hbm, in_hbm, conv_hbm, part_hbm,
+    small_ref, in_ref, conv_ref, part_ref,
+    scores_ref, across_ref, turned_ref, gets, puts,
 ):
     half = low_hbm.shape[0]
     rows, inner = conv_ref.shape
@@ -679,7 +668,6 @@
             )
         )
     ]
-    get_mid = fetch(mid_hbm, mid_ref, gets.at[tiles + 3])
     for tile in range(tiles):
         columns = pl.ds(tile * TILE, TILE)
         fetch(conv_hbm.at[:, columns], conv_ref.at[:, columns], gets.at[tile])
@@ -693,6 +681,7 @@
         keep = (gap >= 0) & (gap <= rel_ref[span])
         scores_ref[block] = jnp.where(keep, scores, 0.0)
         across_ref[block] = mm(ones, small_ref[span]).T
+    turned_ref[...] = in_ref[...].astype(F32).T.astype(BF)
 
     def body(tile, _):
         columns = pl.ds(pl.multiple_of(tile * TILE, TILE), TILE)
@@ -705,6 +694,7 @@
         conv = conv_ref[:, columns].astype(F32)
         inject = (conv * steps).astype(BF)
         lane_head = iota((BLK, TILE), 1) // HD
+        state = None
         for block in range(rows // BLK):
             span = slice(block * BLK, (block + 1) * BLK)
             cumulative = mm(ones, decays[span])
@@ -714,7 +704,16 @@
                 enter = jnp.where(
                     iota((BLK, 1), 0) < rel_ref[span], jnp.exp(cumulative), 0.0
                 )
-                total = total + enter * mm(outmap_ref[span], mid_ref[:, columns])
+                total = total + enter * mm(outmap_ref[span], state.astype(BF))
+            if (block + 1) * BLK < rows:
+                last = rel_ref[(block + 1) * BLK - 1 : (block + 1) * BLK]
+                end = cumulative[BLK - 1 : BLK]
+                behind = BLK - 1 - iota((BLK, 1), 0)
+                tail = jnp.where(behind <= last, jnp.exp(end - cumulative), 0.0)
+                decayed = (tail * inject[span].astype(F32)).astype(BF)
+                block_state = mm(turned_ref[:, span], decayed)
+                carry = jnp.where(last > BLK - 1, jnp.exp(end), 0.0)
+                state = block_state if state is None else carry * state + block_state
             part = BLK // 2
             pieces = [total[:part], total[part:]]
             for q in range(per):
@@ -733,7 +732,6 @@
         ).start()
         return 0
 
-    get_mid.wait()
     lax.fori_loop(0, tiles, body, 0)
     for tile in range(tiles):
         columns = pl.ds(tile * TILE, TILE)
@@ -742,29 +740,29 @@
         ).wait()
 
 
-def inner_part(small, rel, input_map, output_map, conv, mid, skip_wide):
+def inner_part(small, rel, input_map, output_map, conv, skip_wide):
     rows, inner = conv.shape
     blocks = rows // BLK
     tiles = inner // TILE
     return pl.pallas_call(
         inner_kernel,
-        in_specs=vmem(3) + hbm(5),
+        in_specs=vmem(3) + hbm(4),
         out_specs=hbm(1)[0],
         out_shape=pltpu.HBM((rows, inner), F32),
         scratch_shapes=[
             pltpu.VMEM((rows, LANES), BF),
             pltpu.VMEM(input_map.shape, BF),
             pltpu.VMEM(conv.shape, BF),
-            pltpu.VMEM(mid.shape, BF),
             pltpu.VMEM((rows, inner), F32),
             pltpu.VMEM((blocks, BLK, BLK), F32),
             pltpu.VMEM((blocks, 128, BLK), F32),
-            pltpu.SemaphoreType.DMA((tiles + 4,)),
+            pltpu.VMEM((input_map.shape[1], rows), BF),
+            pltpu.SemaphoreType.DMA((tiles + 3,)),
             pltpu.SemaphoreType.DMA((tiles,)),
         ],
         name="inner_part",
         **params(24, 8 * rows * BLK * inner, 8_000_000),
-    )(rel, skip_wide, near(output_map), *[far(x) for x in (*small, input_map, conv, mid)])
+    )(rel, skip_wide, near(output_map), *[far(x) for x in (*small, input_map, conv)])
 
 
 def scan_kernel(lines, me_ref, recv_ref, out_ref):
@@ -802,9 +800,13 @@
     )(me, near(recv))
 
 
-def prepare_kernel(rel_ref, low_hbm, high_hbm, gain_ref, small_ref, ones_ref, sems):
+def prepare_kernel(
+    rel_ref, low_hbm, high_hbm, kept_hbm, gain_ref, kept_ref,
+    small_ref, ones_ref, sems,
+):
     rows, inner = gain_ref.shape
     half = rows // 2
+    get_kept = fetch(kept_hbm, kept_ref, sems.at[2])
     get_small = [
         fetch(low_hbm, small_ref.at[pl.ds(0, half)], sems.at[0]),
         fetch(high_hbm, small_ref.at[pl.ds(half, half)], sems.at[1]),
@@ -823,23 +825,27 @@
         return 0
 
     lax.fori_loop(0, inner // TILE, body, 0)
-
-
-def prepare(rel, small, inner):
-    rows = rel.shape[0]
+    get_kept.wait()
+
+
+def prepare(rel, small, kept):
+    rows, inner = rel.shape[0], kept.shape[1]
     return pl.pallas_call(
         prepare_kernel,
-        in_specs=vmem(1) + hbm(2),
-        out_specs=vmem(1)[0],
-        out_shape=pltpu.VMEM((rows, inner), F32),
+        in_specs=vmem(1) + hbm(3),
+        out_specs=vmem(2),
+        out_shape=[
+            pltpu.VMEM((rows, inner), F32),
+            pltpu.VMEM(kept.shape, BF),
+        ],
         scratch_shapes=[
             pltpu.VMEM((rows, LANES), BF),
             pltpu.VMEM((rows, rows), BF),
-            pltpu.SemaphoreType.DMA((2,)),
+            pltpu.SemaphoreType.DMA((3,)),
         ],
         name="prepare",
         **params(8, 2 * rows * rows * inner, 8_000_000),
-    )(rel, *[far(x) for x in small])
+    )(rel, *[far(x) for x in (*small, kept)])
 
 
 def final_kernel(
@@ -921,7 +927,7 @@
     total = project_near(
         (low_left, high_left), (low_right, high_right), w_left, w_right, total
     )
-    conv, mine, mid, input_map, output_map = front(
+    conv, mine, input_map, output_map = front(
         (low_far, high_far), total, w_far, rel, carry, steps, tail,
         conv_x, bias_x[None, :], conv_bc, bias_bc[None, :],
     )
@@ -941,12 +947,12 @@
     sent, conv = lax.optimization_barrier((sent, conv))
     gathered = exchange(sent)
     part = inner_part(
-        small, rel, input_map, output_map, conv, mid, jnp.repeat(skip, HD)[None, :]
+        small, rel, input_map, output_map, conv, jnp.repeat(skip, HD)[None, :]
     )
     gathered, part = lax.optimization_barrier((gathered, part))
     entering = scan_shards(chip, gathered, input_map.shape[1] // 16)
     entering, rel = lax.optimization_barrier((entering, rel))
-    gain = prepare(rel, small, inner)
+    gain, kept = prepare(rel, small, kept)
     arrived, gain = lax.optimization_barrier((exchange(entering), gain))
     send, keep = entering_halves(core, arrived, kept)
     got = lax.ppermute(send, "ctx", swap)

time: 137 us -> 137 us (level)
  no operation moved by 1% of the time
where the time goes in v6:
time: 137 us; the launch traced here: 136 us
  waiting for transfers between devices  50.7 us (37%)
  Pallas kernels  42.2 us (31%)
  starting transfers between devices  41.8 us (31%)
    all_to_all x1, waiting for transfers between devices, on_device(): lax.all_to_all(sent, 'ctx', split_axis=0, concat_axis=0, tiled=True)  36.6 us
    all_to_all x2, starting transfers between devices, exchange(): lax.all_to_all(x, 'ctx', split_axis=0, concat_axis=0, tiled=True, axis_in...  13.4 us
    all_to_all x1, starting transfers between devices, on_device(): lax.all_to_all(sent, 'ctx', split_axis=0, concat_axis=0, tiled=True)  13.2 us
    ppermute x6, starting transfers between devices, turned(): return lax.ppermute(x, 'head', [(i, (i + by) % ring) for i in range(ring)])  8.7 us
    pallas_call x1, Pallas kernels, inner_part(): pl.pallas_call(inner_kernel, in_specs=vmem(3) + hbm(4), out_specs=hbm(1)[...  8.48 us
    pallas_call x1, Pallas kernels, front(): pl.pallas_call(front_kernel, in_specs=vmem(10) + hbm(2), out_specs=hbm(1)...  7.4 us
    all_to_all x2, waiting for transfers between devices, exchange(): lax.all_to_all(x, 'ctx', split_axis=0, concat_axis=0, tiled=True, axis_in...  6.35 us
    ppermute x6, waiting for transfers between devices, turned(): return lax.ppermute(x, 'head', [(i, (i + by) % ring) for i in range(ring)])  5.45 us
  transfers between devices with their start and end apart: 12, of which 10 were waited for; matrix products, arithmetic and copies ran while one was open for 1% of the time, Pallas kernels for 17%

profile of v6, /device:TPU:1, one launch (start us, length us, event | category | flops | bytes accessed | tf_op | source)
XLA Modules:
  0.0 136.2 jit_solution(4756258723914565402)
XLA Ops:
  0.0 3.5 %pack.1 = bf16[64,88,128]{2,1,0:T(8,128)(2,1)} custom-call(s32[1,512]{1,0:T(1,128)} %bitcast.12, bf16[20,2,512]{2,1,0:T(2,128)(2,1)} %bitcast.11, bf16[512,640]{1,0:T(8,128)(2,1)} %tok_hbm.1), custom_call_target="tpu_custom_call" | custom-call | flops 805306368 | bytes 1310720 | tf_op jit(solution)/shard_map/pack/pallas_call | solution.py:139
  3.5 13.2 %all-to-all-start = ((bf16[64,88,128]{2,1,0:T(8,128)(2,1)}), bf16[64,88,128]{2,1,0:T(8,128)(2,1)S(1)}, u32[]{:S(2)}, u32[]{:S(2)}) async-start(bf16[64,88,128]{2,1,0:T(8,128)(2,1)} %pack.1), calls=%async_computation | async-start | bytes 2883584 | tf_op jit(solution)/shard_map/all_to_all | solution.py:903
  17.1 36.6 %all-to-all-done.recv_ref = bf16[64,88,128]{2,1,0:T(8,128)(2,1)S(1)} async-done(((bf16[64,88,128]{2,1,0:T(8,128)(2,1)}), bf16[64,88,128]{2,1,0:T(8,128)(2,1)S(1)}, u32[]{:S(2)}, u32[]{:S(2)}) %all-to-all-start) | async-done | bytes 1441824 | tf_op jit(solution)/shard_map/all_to_all | solution.py:903
  53.6 1.2 unpack_low.1
  55.9 3.0 %collective-permute-start.2 = (bf16[16,640]{1,0:T(8,128)(2,1)S(1)}, bf16[16,640]{1,0:T(8,128)(2,1)S(1)}, u32[]{:S(2)}, u32[]{:S(2)}) collective-permute-start(bf16[16,640]{1,0:T(8,128)(2,1)S(1)} %get-tuple-element.41), channel_id=1, source_target_pairs={{0,4},{4,8},{8,12},{12,16},{16,20},{20,24},{24,28},{28,32},{32,36}... | collective-permute-start | bytes 61448 | tf_op jit(solution)/shard_map/ppermute | solution.py:910
  59.3 1.3 collective-permute-start
  60.6 1.7 %collective-permute-start.3 = (bf16[272,640]{1,0:T(8,128)(2,1)S(1)}, bf16[272,640]{1,0:T(8,128)(2,1)S(1)}, u32[]{:S(2)}, u32[]{:S(2)}) collective-permute-start(bf16[272,640]{1,0:T(8,128)(2,1)S(1)} %constant_dynamic-update-slice_fusion.high_ref), channel_id=1, source_target_pairs={{0,3},{1,0},{2,1},{3,2},{4,7},{5,4},{6,5},{7,6},{8,11},{9,8},{10,9... | collective-permute-start | bytes 1044488 | tf_op jit(solution)/shard_map/ppermute | solution.py:907
  62.3 4.4 %decay_factors.1 = (bf16[5,512,256]{2,1,0:T(8,128)(2,1)}, f32[5,512,256]{2,1,0:T(8,128)}, f32[5,8,256]{2,1,0:T(8,128)S(1)}) custom-call(s32[512,1]{1,0:T(8,128)S(1)} %add_subtract_fusion.rel_ref, bf16[256,128]{1,0:T(8,128)(2,1)} %get-tuple-element.42.low_hbm, bf16[256,128]{1,0:T(8,128)(2,1)} %get-tuple-element.43.high_hbm), custom_call_target="tpu_custom_call" | custom-call | flops 671088640 | bytes 7000000 | tf_op jit(solution)/shard_map/decay_factors/pallas_call | solution.py:337
  66.8 2.7 %collective-permute-start.6 = (bf16[256,640]{1,0:T(8,128)(2,1)S(1)}, bf16[256,640]{1,0:T(8,128)(2,1)S(1)}, u32[]{:S(2)}, u32[]{:S(2)}) collective-permute-start(bf16[256,640]{1,0:T(8,128)(2,1)S(1)} %get-tuple-element.38.low_ref), channel_id=1, source_target_pairs={{0,3},{1,0},{2,1},{3,2},{4,7},{5,4},{6,5},{7,6},{8,11},{9,8},{10,9... | collective-permute-start | bytes 983048 | tf_op jit(solution)/shard_map/ppermute | solution.py:907
  69.5 1.1 collective-permute-done.3.high3
  70.6 3.0 %collective-permute-start.4 = (bf16[272,640]{1,0:T(8,128)(2,1)S(1)}, bf16[272,640]{1,0:T(8,128)(2,1)S(1)}, u32[]{:S(2)}, u32[]{:S(2)}) collective-permute-start(bf16[272,640]{1,0:T(8,128)(2,1)S(1)} %collective-permute-done.3.high3), channel_id=1, source_target_pairs={{0,3},{1,0},{2,1},{3,2},{4,7},{5,4},{6,5},{7,6},{8,11},{9,8},{10,9... | collective-permute-start | bytes 1044488 | tf_op jit(solution)/shard_map/ppermute | solution.py:907
  73.6 3.9 %project_own.1 = (f32[528,1536]{1,0:T(8,128)S(1)}, bf16[640,1536]{1,0:T(8,128)(2,1)S(1)}, bf16[640,1536]{1,0:T(8,128)(2,1)S(1)}, bf16[640,1536]{1,0:T(8,128)(2,1)S(1)}) custom-call(s32[1]{0:T(128)} %bitcast.6.me_ref, bf16[256,640]{1,0:T(8,128)(2,1)S(1)} %get-tuple-element.38.low_ref, bf16[272,640]{1,0:T(8,128)(2,1)S(1)} %constant_dynamic-update-slice_fusion.high_ref, ...), custom_call_target="tpu_custom_call" | custom-call | flops 1038090240 | bytes 8000000 | tf_op jit(solution)/shard_map/project_own/pallas_call | solution.py:400
  77.9 3.2 %project_near.1.total_ref = f32[528,1536]{1,0:T(8,128)S(1)} custom-call(bf16[256,640]{1,0:T(8,128)(2,1)S(1)} %collective-permute-done.low1, bf16[272,640]{1,0:T(8,128)(2,1)S(1)} %collective-permute-done.5.high1, bf16[256,640]{1,0:T(8,128)(2,1)S(1)} %collective-permute-done.6.low3, bf16[272,640]{1,0:T(8,128)(2,1)S(1)} %collective-permute-done.3.high3, ...), custom_call_target="tpu_custom_call" | custom-call | flops 2076180480 | bytes 8000000 | tf_op jit(solution)/shard_map/project_near/pallas_call | solution.py:434
  81.2 3.5 %collective-permute-done.1.low_ref = bf16[256,640]{1,0:T(8,128)(2,1)S(1)} collective-permute-done((bf16[256,640]{1,0:T(8,128)(2,1)S(1)}, bf16[256,640]{1,0:T(8,128)(2,1)S(1)}, u32[]{:S(2)}, u32[]{:S(2)}) %collective-permute-start.1) | collective-permute-done | bytes 327712 | tf_op jit(solution)/shard_map/ppermute | solution.py:907
  85.1 7.4 %front.1 = (bf16[512,1280]{1,0:T(8,128)(2,1)}, bf16[144,1280]{1,0:T(8,128)(2,1)S(1)}, bf16[512,128]{1,0:T(8,128)(2,1)}, bf16[512,128]{1,0:T(8,128)(2,1)S(1)}) custom-call(bf16[256,640]{1,0:T(8,128)(2,1)S(1)} %collective-permute-done.1.low_ref, bf16[272,640]{1,0:T(8,128)(2,1)S(1)} %collective-permute-done.4.high_ref, f32[528,1536]{1,0:T(8,128)S(1)} %project_near.1.total_ref, ...), custom_call_target="tpu_custom_call" | custom-call | flops 1006632960 | bytes 12000000 | tf_op jit(solution)/shard_map/front/pallas_call | solution.py:517
  93.2 1.3 collective-permute-done.7.theirs_ref
  94.5 1.4 %combine.1 = (bf16[32,24,128]{2,1,0:T(8,128)(2,1)}, bf16[80,1280]{1,0:T(8,128)(2,1)}) custom-call(s32[1]{0:T(128)} %bitcast.core_ref, bf16[144,1280]{1,0:T(8,128)(2,1)S(1)} %get-tuple-element.53.mine_ref, bf16[144,1280]{1,0:T(8,128)(2,1)S(1)} %collective-permute-done.7.theirs_ref), custom_call_target="tpu_custom_call" | custom-call | flops 1000000 | bytes 1500000 | tf_op jit(solution)/shard_map/combine/pallas_call | solution.py:589
  95.9 4.9 %all-to-all-start.1 = ((bf16[32,24,128]{2,1,0:T(8,128)(2,1)}), bf16[32,24,128]{2,1,0:T(8,128)(2,1)S(1)}, u32[]{:S(2)}, u32[]{:S(2)}) async-start(bf16[32,24,128]{2,1,0:T(8,128)(2,1)} %get-tuple-element.56), calls=%async_computation.1 | async-start | bytes 393216 | tf_op jit(solution)/shard_map/all_to_all | solution.py:941
  101.0 8.5 %inner_part.1.part_hbm = f32[512,1280]{1,0:T(8,128)} custom-call(s32[512,1]{1,0:T(8,128)S(1)} %add_subtract_fusion.rel_ref, f32[1,1280]{1,0:T(1,128)S(1)} %broadcast_in_dim_reshape.3.skip_ref, bf16[512,128]{1,0:T(8,128)(2,1)S(1)} %get-tuple-element.57.outmap_ref, bf16[256,128]{1,0:T(8,128)(2,1)} %get-tuple-element.42.low_hbm, ...), custom_call_target="tpu_custom_call" | custom-call | flops 1342177280 | bytes 8000000 | tf_op jit(solution)/shard_map/inner_part/pallas_call | solution.py:747
  111.0 8.5 %all-to-all-start.2 = ((bf16[32,24,128]{2,1,0:T(8,128)(2,1)}), bf16[32,24,128]{2,1,0:T(8,128)(2,1)S(1)}, u32[]{:S(2)}, u32[]{:S(2)}) async-start(bf16[32,24,128]{2,1,0:T(8,128)(2,1)} %scan_shards.1), calls=%async_computation.2 | async-start | bytes 393216 | tf_op jit(solution)/shard_map/all_to_all | solution.py:941
  119.6 3.8 %prepare.1 = (f32[512,1280]{1,0:T(8,128)S(1)}, bf16[80,1280]{1,0:T(8,128)(2,1)S(1)}) custom-call(s32[512,1]{1,0:T(8,128)S(1)} %add_subtract_fusion.rel_ref, bf16[256,128]{1,0:T(8,128)(2,1)} %get-tuple-element.42.low_hbm, bf16[256,128]{1,0:T(8,128)(2,1)} %get-tuple-element.43.high_hbm, bf16[80,1280]{1,0:T(8,128)(2,1)} %get-tuple-element.63.kept_hbm), custom_call_target="tpu_custom_call" | custom-call | flops 671088640 | bytes 8000000 | tf_op jit(solution)/shard_map/prepare/pallas_call | solution.py:833
  123.3 5.6 %all-to-all-done.2.recv_ref = bf16[32,24,128]{2,1,0:T(8,128)(2,1)S(1)} async-done(((bf16[32,24,128]{2,1,0:T(8,128)(2,1)}), bf16[32,24,128]{2,1,0:T(8,128)(2,1)S(1)}, u32[]{:S(2)}, u32[]{:S(2)}) %all-to-all-start.2) | async-done | bytes 196640 | tf_op jit(solution)/shard_map/all_to_all | solution.py:941
  129.1 2.9 %collective-permute-start.8 = (bf16[64,1280]{1,0:T(8,128)(2,1)S(1)}, bf16[64,1280]{1,0:T(8,128)(2,1)S(1)}, u32[]{:S(2)}, u32[]{:S(2)}) collective-permute-start(bf16[64,1280]{1,0:T(8,128)(2,1)S(1)} %get-tuple-element.68), channel_id=1, source_target_pairs={{0,4},{4,0},{8,12},{12,8},{16,20},{20,16},{24,28},{28,24},{32,36},... | collective-permute-start | bytes 491528 | tf_op jit(solution)/shard_map/ppermute | solution.py:958
  133.0 3.0 %final.1 = bf16[512,1280]{1,0:T(8,128)(2,1)} custom-call(s32[1]{0:T(128)} %bitcast.core_ref, bf16[64,1280]{1,0:T(8,128)(2,1)S(1)} %get-tuple-element.67.keep_ref, bf16[64,1280]{1,0:T(8,128)(2,1)S(1)} %collective-permute-done.8.got_ref, f32[512,1280]{1,0:T(8,128)S(1)} %get-tuple-element.69.gain_ref, bf16[512,128]{1,0:T(8,128)(2,1)S(1)} %get-tuple-element.57.outmap_ref, ...), custom_call_target="tpu_custom_call" | custom-call | flops 167772160 | bytes 7000000 | tf_op jit(solution)/shard_map/final/pallas_call | solution.py:879
  (37 shorter events, 6.4 us)
Async XLA Ops:
  3.5 13.2 %copy-start.4 = (s32[128]{0:T(128)S(1)}, s32[128]{0:T(128)}, u32[]{:S(2)}) copy-start(s32[128]{0:T(128)} %param.14) | copy-start | bytes 1540
  3.5 50.2 %all-to-all-start = ((bf16[64,88,128]{2,1,0:T(8,128)(2,1)}), bf16[64,88,128]{2,1,0:T(8,128)(2,1)S(1)}, u32[]{:S(2)}, u32[]{:S(2)}) async-start(bf16[64,88,128]{2,1,0:T(8,128)(2,1)} %pack.1), calls=%async_computation | async-start | bytes 2883584 | tf_op jit(solution)/shard_map/all_to_all | solution.py:903
  55.9 17.7 %copy-start.3 = (f32[1280]{0:T(1024)S(1)}, f32[1280]{0:T(1024)}, u32[]{:S(2)}) copy-start(f32[1280]{0:T(1024)} %param.19) | copy-start | bytes 15364
  55.9 4.7 %collective-permute-start.2 = (bf16[16,640]{1,0:T(8,128)(2,1)S(1)}, bf16[16,640]{1,0:T(8,128)(2,1)S(1)}, u32[]{:S(2)}, u32[]{:S(2)}) collective-permute-start(bf16[16,640]{1,0:T(8,128)(2,1)S(1)} %get-tuple-element.41), channel_id=1, source_target_pairs={{0,4},{4,8},{8,12},{12,16},{16,20},{20,24},{24,28},{28,32},{32,36}... | collective-permute-start | bytes 61448 | tf_op jit(solution)/shard_map/ppermute | solution.py:910
  59.3 14.3 %collective-permute-start = (bf16[256,640]{1,0:T(8,128)(2,1)S(1)}, bf16[256,640]{1,0:T(8,128)(2,1)S(1)}, u32[]{:S(2)}, u32[]{:S(2)}) collective-permute-start(bf16[256,640]{1,0:T(8,128)(2,1)S(1)} %get-tuple-element.38.low_ref), channel_id=1, source_target_pairs={{0,1},{1,2},{2,3},{3,0},{4,5},{5,6},{6,7},{7,4},{8,9},{9,10},{10,1... | collective-permute-start | bytes 983048 | tf_op jit(solution)/shard_map/ppermute | solution.py:907
  60.6 10.0 %collective-permute-start.3 = (bf16[272,640]{1,0:T(8,128)(2,1)S(1)}, bf16[272,640]{1,0:T(8,128)(2,1)S(1)}, u32[]{:S(2)}, u32[]{:S(2)}) collective-permute-start(bf16[272,640]{1,0:T(8,128)(2,1)S(1)} %constant_dynamic-update-slice_fusion.high_ref), channel_id=1, source_target_pairs={{0,3},{1,0},{2,1},{3,2},{4,7},{5,4},{6,5},{7,6},{8,11},{9,8},{10,9... | collective-permute-start | bytes 1044488 | tf_op jit(solution)/shard_map/ppermute | solution.py:907
  66.7 11.2 %collective-permute-start.5 = (bf16[272,640]{1,0:T(8,128)(2,1)S(1)}, bf16[272,640]{1,0:T(8,128)(2,1)S(1)}, u32[]{:S(2)}, u32[]{:S(2)}) collective-permute-start(bf16[272,640]{1,0:T(8,128)(2,1)S(1)} %constant_dynamic-update-slice_fusion.high_ref), channel_id=1, source_target_pairs={{0,1},{1,2},{2,3},{3,0},{4,5},{5,6},{6,7},{7,4},{8,9},{9,10},{10,1... | collective-permute-start | bytes 1044488 | tf_op jit(solution)/shard_map/ppermute | solution.py:907
  66.8 10.8 %collective-permute-start.6 = (bf16[256,640]{1,0:T(8,128)(2,1)S(1)}, bf16[256,640]{1,0:T(8,128)(2,1)S(1)}, u32[]{:S(2)}, u32[]{:S(2)}) collective-permute-start(bf16[256,640]{1,0:T(8,128)(2,1)S(1)} %get-tuple-element.38.low_ref), channel_id=1, source_target_pairs={{0,3},{1,0},{2,1},{3,2},{4,7},{5,4},{6,5},{7,6},{8,11},{9,8},{10,9... | collective-permute-start | bytes 983048 | tf_op jit(solution)/shard_map/ppermute | solution.py:907
  70.6 14.5 %collective-permute-start.4 = (bf16[272,640]{1,0:T(8,128)(2,1)S(1)}, bf16[272,640]{1,0:T(8,128)(2,1)S(1)}, u32[]{:S(2)}, u32[]{:S(2)}) collective-permute-start(bf16[272,640]{1,0:T(8,128)(2,1)S(1)} %collective-permute-done.3.high3), channel_id=1, source_target_pairs={{0,3},{1,0},{2,1},{3,2},{4,7},{5,4},{6,5},{7,6},{8,11},{9,8},{10,9... | collective-permute-start | bytes 1044488 | tf_op jit(solution)/shard_map/ppermute | solution.py:907
  73.6 11.1 %collective-permute-start.1 = (bf16[256,640]{1,0:T(8,128)(2,1)S(1)}, bf16[256,640]{1,0:T(8,128)(2,1)S(1)}, u32[]{:S(2)}, u32[]{:S(2)}) collective-permute-start(bf16[256,640]{1,0:T(8,128)(2,1)S(1)} %collective-permute-done.low1), channel_id=1, source_target_pairs={{0,1},{1,2},{2,3},{3,0},{4,5},{5,6},{6,7},{7,4},{8,9},{9,10},{10,1... | collective-permute-start | bytes 983048 | tf_op jit(solution)/shard_map/ppermute | solution.py:907
  77.9 7.1 %copy-start = (f32[4,1280]{1,0:T(4,128)S(1)}, f32[4,1280]{1,0:T(4,128)}, u32[]{:S(2)}) copy-start(f32[4,1280]{1,0:T(4,128)} %cx_ref.1) | copy-start | bytes 61444
  77.9 7.1 %copy-start.1 = (f32[4,256]{1,0:T(4,128)S(1)}, f32[4,256]{1,0:T(4,128)}, u32[]{:S(2)}) copy-start(f32[4,256]{1,0:T(4,128)} %cb_ref.1) | copy-start | bytes 12292
  77.9 7.1 %copy-start.2 = (f32[256]{0:T(256)S(1)}, f32[256]{0:T(256)}, u32[]{:S(2)}) copy-start(f32[256]{0:T(256)} %param.20) | copy-start | bytes 3076
  85.1 15.7 %copy-start.5 = (f32[20]{0:T(128)S(1)}, f32[20]{0:T(128)}, u32[]{:S(2)}) copy-start(f32[20]{0:T(128)} %param.21) | copy-start | bytes 244
  92.5 2.0 %collective-permute-start.7 = (bf16[144,1280]{1,0:T(8,128)(2,1)S(1)}, bf16[144,1280]{1,0:T(8,128)(2,1)S(1)}, u32[]{:S(2)}, u32[]{:S(2)}) collective-permute-start(bf16[144,1280]{1,0:T(8,128)(2,1)S(1)} %get-tuple-element.53.mine_ref), channel_id=1, source_target_pairs={{0,4},{4,0},{8,12},{12,8},{16,20},{20,16},{24,28},{28,24},{32,36},... | collective-permute-start | bytes 1105928 | tf_op jit(solution)/shard_map/ppermute | solution.py:945
  95.9 14.3 %all-to-all-start.1 = ((bf16[32,24,128]{2,1,0:T(8,128)(2,1)}), bf16[32,24,128]{2,1,0:T(8,128)(2,1)S(1)}, u32[]{:S(2)}, u32[]{:S(2)}) async-start(bf16[32,24,128]{2,1,0:T(8,128)(2,1)} %get-tuple-element.56), calls=%async_computation.1 | async-start | bytes 393216 | tf_op jit(solution)/shard_map/all_to_all | solution.py:941
  111.0 17.9 %all-to-all-start.2 = ((bf16[32,24,128]{2,1,0:T(8,128)(2,1)}), bf16[32,24,128]{2,1,0:T(8,128)(2,1)S(1)}, u32[]{:S(2)}, u32[]{:S(2)}) async-start(bf16[32,24,128]{2,1,0:T(8,128)(2,1)} %scan_shards.1), calls=%async_computation.2 | async-start | bytes 393216 | tf_op jit(solution)/shard_map/all_to_all | solution.py:941
  129.1 4.0 %collective-permute-start.8 = (bf16[64,1280]{1,0:T(8,128)(2,1)S(1)}, bf16[64,1280]{1,0:T(8,128)(2,1)S(1)}, u32[]{:S(2)}, u32[]{:S(2)}) collective-permute-start(bf16[64,1280]{1,0:T(8,128)(2,1)S(1)} %get-tuple-element.68), channel_id=1, source_target_pairs={{0,4},{4,0},{8,12},{12,8},{16,20},{20,16},{24,28},{28,24},{32,36},... | collective-permute-start | bytes 491528 | tf_op jit(solution)/shard_map/ppermute | solution.py:958

commit v7 on v6

--- a/solution.py
+++ b/solution.py
@@ -544,7 +544,7 @@
 
 
 def combine_kernel(
-    core_ref, mine_ref, theirs_ref, sent_ref, kept_hbm, chip_ref, gain_ref, kept_ref, sem
+    core_ref, mine_ref, theirs_ref, sent_ref, kept_ref, chip_ref, gain_ref
 ):
     half, inner = chip_ref.shape
     states = 2 * half
@@ -558,7 +558,6 @@
     late_codes = jnp.where(first, other_codes, own_codes)
     kept_ref[:half] = early.astype(BF)
     kept_ref[half:] = early_codes.astype(BF)
-    put = fetch(kept_ref, kept_hbm, sem)
     early_gain = early_codes[0:1] + early_codes[1:2]
     late_gain = late_codes[0:1] + late_codes[1:2]
     chip_ref[...] = late_gain * early + jnp.where(first, other, own)
@@ -580,7 +579,6 @@
         piece = [tile_of(one), tile_of(two), middle]
         piece += [*codes_of(min(columns)), *codes_of(max(columns))]
         sent_ref[dest] = jnp.concatenate(piece, axis=0).astype(BF)
-    put.wait()
 
 
 def combine(core, mine, theirs, chips):
@@ -589,16 +587,14 @@
     return pl.pallas_call(
         combine_kernel,
         in_specs=[pl.BlockSpec(memory_space=pltpu.SMEM)] + vmem(2),
-        out_specs=vmem(1) + hbm(1),
+        out_specs=vmem(2),
         out_shape=[
             jax.ShapeDtypeStruct((chips, PIECE, LANES), BF),
-            pltpu.HBM((half + HALO, inner), BF),
+            pltpu.VMEM((half + HALO, inner), BF),
         ],
         scratch_shapes=[
             pltpu.VMEM((half, inner), F32),
             pltpu.VMEM((8, inner), F32),
-            pltpu.VMEM((half + HALO, inner), BF),
-            pltpu.SemaphoreType.DMA,
         ],
         name="combine",
         **params(8, 1_000_000, 1_500_000),
@@ -801,12 +797,11 @@
 
 
 def prepare_kernel(
-    rel_ref, low_hbm, high_hbm, kept_hbm, gain_ref, kept_ref,
+    rel_ref, low_hbm, high_hbm, gain_ref,
     small_ref, ones_ref, sems,
 ):
     rows, inner = gain_ref.shape
     half = rows // 2
-    get_kept = fetch(kept_hbm, kept_ref, sems.at[2])
     get_small = [
         fetch(low_hbm, small_ref.at[pl.ds(0, half)], sems.at[0]),
         fetch(high_hbm, small_ref.at[pl.ds(half, half)], sems.at[1]),
@@ -825,27 +820,23 @@
         return 0
 
     lax.fori_loop(0, inner // TILE, body, 0)
-    get_kept.wait()
-
-
-def prepare(rel, small, kept):
-    rows, inner = rel.shape[0], kept.shape[1]
+
+
+def prepare(rel, small, inner):
+    rows = rel.shape[0]
     return pl.pallas_call(
         prepare_kernel,
-        in_specs=vmem(1) + hbm(3),
-        out_specs=vmem(2),
-        out_shape=[
-            pltpu.VMEM((rows, inner), F32),
-            pltpu.VMEM(kept.shape, BF),
-        ],
+        in_specs=vmem(1) + hbm(2),
+        out_specs=vmem(1)[0],
+        out_shape=pltpu.VMEM((rows, inner), F32),
         scratch_shapes=[
             pltpu.VMEM((rows, LANES), BF),
             pltpu.VMEM((rows, rows), BF),
-            pltpu.SemaphoreType.DMA((3,)),
+            pltpu.SemaphoreType.DMA((2,)),
         ],
         name="prepare",
         **params(8, 2 * rows * rows * inner, 8_000_000),
-    )(rel, *[far(x) for x in (*small, kept)])
+    )(rel, *[far(x) for x in small])
 
 
 def final_kernel(
@@ -952,7 +943,7 @@
     gathered, part = lax.optimization_barrier((gathered, part))
     entering = scan_shards(chip, gathered, input_map.shape[1] // 16)
     entering, rel = lax.optimization_barrier((entering, rel))
-    gain, kept = prepare(rel, small, kept)
+    gain = prepare(rel, small, inner)
     arrived, gain = lax.optimization_barrier((exchange(entering), gain))
     send, keep = entering_halves(core, arrived, kept)
     got = lax.ppermute(send, "ctx", swap)

time: 137 us -> 136 us (level)
  no operation moved by 1% of the time
where the time goes in v7:
time: 136 us
  waiting for transfers between devices  50.8 us (37%)
  starting transfers between devices  41.9 us (31%)
  Pallas kernels  41.6 us (31%)
    all_to_all x1, waiting for transfers between devices, on_device(): lax.all_to_all(sent, 'ctx', split_axis=0, concat_axis=0, tiled=True)  36.6 us
    all_to_all x2, starting transfers between devices, exchange(): lax.all_to_all(x, 'ctx', split_axis=0, concat_axis=0, tiled=True, axis_in...  13.4 us
    all_to_all x1, starting transfers between devices, on_device(): lax.all_to_all(sent, 'ctx', split_axis=0, concat_axis=0, tiled=True)  13.2 us
    ppermute x6, starting transfers between devices, turned(): return lax.ppermute(x, 'head', [(i, (i + by) % ring) for i in range(ring)])  8.73 us
    pallas_call x1, Pallas kernels, inner_part(): pl.pallas_call(inner_kernel, in_specs=vmem(3) + hbm(4), out_specs=hbm(1)[...  8.48 us
    pallas_call x1, Pallas kernels, front(): pl.pallas_call(front_kernel, in_specs=vmem(10) + hbm(2), out_specs=hbm(1)...  7.4 us
    all_to_all x2, waiting for transfers between devices, exchange(): lax.all_to_all(x, 'ctx', split_axis=0, concat_axis=0, tiled=True, axis_in...  6.46 us
    ppermute x6, waiting for transfers between devices, turned(): return lax.ppermute(x, 'head', [(i, (i + by) % ring) for i in range(ring)])  5.42 us
  transfers between devices with their start and end apart: 12, of which 10 were waited for; matrix products, arithmetic and copies ran while one was open for 1% of the time, Pallas kernels for 17%

profile of v7, /device:TPU:1, one launch (start us, length us, event | category | flops | bytes accessed | tf_op | source)
XLA Modules:
  0.0 135.6 jit_solution(5331418998939849941)
XLA Ops:
  0.0 3.4 %pack.1 = bf16[64,88,128]{2,1,0:T(8,128)(2,1)} custom-call(s32[1,512]{1,0:T(1,128)} %bitcast.12, bf16[20,2,512]{2,1,0:T(2,128)(2,1)} %bitcast.11, bf16[512,640]{1,0:T(8,128)(2,1)} %tok_hbm.1), custom_call_target="tpu_custom_call" | custom-call | flops 805306368 | bytes 1310720 | tf_op jit(solution)/shard_map/pack/pallas_call | solution.py:139
  3.5 13.2 %all-to-all-start = ((bf16[64,88,128]{2,1,0:T(8,128)(2,1)}), bf16[64,88,128]{2,1,0:T(8,128)(2,1)S(1)}, u32[]{:S(2)}, u32[]{:S(2)}) async-start(bf16[64,88,128]{2,1,0:T(8,128)(2,1)} %pack.1), calls=%async_computation | async-start | bytes 2883584 | tf_op jit(solution)/shard_map/all_to_all | solution.py:894
  17.1 36.6 %all-to-all-done.recv_ref = bf16[64,88,128]{2,1,0:T(8,128)(2,1)S(1)} async-done(((bf16[64,88,128]{2,1,0:T(8,128)(2,1)}), bf16[64,88,128]{2,1,0:T(8,128)(2,1)S(1)}, u32[]{:S(2)}, u32[]{:S(2)}) %all-to-all-start) | async-done | bytes 1441824 | tf_op jit(solution)/shard_map/all_to_all | solution.py:894
  53.6 1.2 unpack_low.1
  54.8 1.1 unpack_high.1
  55.9 3.0 %collective-permute-start.2 = (bf16[16,640]{1,0:T(8,128)(2,1)S(1)}, bf16[16,640]{1,0:T(8,128)(2,1)S(1)}, u32[]{:S(2)}, u32[]{:S(2)}) collective-permute-start(bf16[16,640]{1,0:T(8,128)(2,1)S(1)} %get-tuple-element.39), channel_id=1, source_target_pairs={{0,4},{4,8},{8,12},{12,16},{16,20},{20,24},{24,28},{28,32},{32,36}... | collective-permute-start | bytes 61448 | tf_op jit(solution)/shard_map/ppermute | solution.py:901
  59.3 1.3 collective-permute-start
  60.6 1.7 %collective-permute-start.3 = (bf16[272,640]{1,0:T(8,128)(2,1)S(1)}, bf16[272,640]{1,0:T(8,128)(2,1)S(1)}, u32[]{:S(2)}, u32[]{:S(2)}) collective-permute-start(bf16[272,640]{1,0:T(8,128)(2,1)S(1)} %constant_dynamic-update-slice_fusion.high_ref), channel_id=1, source_target_pairs={{0,3},{1,0},{2,1},{3,2},{4,7},{5,4},{6,5},{7,6},{8,11},{9,8},{10,9... | collective-permute-start | bytes 1044488 | tf_op jit(solution)/shard_map/ppermute | solution.py:898
  62.3 4.4 %decay_factors.1 = (bf16[5,512,256]{2,1,0:T(8,128)(2,1)}, f32[5,512,256]{2,1,0:T(8,128)}, f32[5,8,256]{2,1,0:T(8,128)S(1)}) custom-call(s32[512,1]{1,0:T(8,128)S(1)} %add_subtract_fusion.rel_ref, bf16[256,128]{1,0:T(8,128)(2,1)} %get-tuple-element.40.low_hbm, bf16[256,128]{1,0:T(8,128)(2,1)} %get-tuple-element.41.high_hbm), custom_call_target="tpu_custom_call" | custom-call | flops 671088640 | bytes 7000000 | tf_op jit(solution)/shard_map/decay_factors/pallas_call | solution.py:337
  66.8 2.7 %collective-permute-start.6 = (bf16[256,640]{1,0:T(8,128)(2,1)S(1)}, bf16[256,640]{1,0:T(8,128)(2,1)S(1)}, u32[]{:S(2)}, u32[]{:S(2)}) collective-permute-start(bf16[256,640]{1,0:T(8,128)(2,1)S(1)} %get-tuple-element.36.low_ref), channel_id=1, source_target_pairs={{0,3},{1,0},{2,1},{3,2},{4,7},{5,4},{6,5},{7,6},{8,11},{9,8},{10,9... | collective-permute-start | bytes 983048 | tf_op jit(solution)/shard_map/ppermute | solution.py:898
  69.5 1.1 collective-permute-done.3.high3
  70.6 3.0 %collective-permute-start.4 = (bf16[272,640]{1,0:T(8,128)(2,1)S(1)}, bf16[272,640]{1,0:T(8,128)(2,1)S(1)}, u32[]{:S(2)}, u32[]{:S(2)}) collective-permute-start(bf16[272,640]{1,0:T(8,128)(2,1)S(1)} %collective-permute-done.3.high3), channel_id=1, source_target_pairs={{0,3},{1,0},{2,1},{3,2},{4,7},{5,4},{6,5},{7,6},{8,11},{9,8},{10,9... | collective-permute-start | bytes 1044488 | tf_op jit(solution)/shard_map/ppermute | solution.py:898
  73.6 3.9 %project_own.1 = (f32[528,1536]{1,0:T(8,128)S(1)}, bf16[640,1536]{1,0:T(8,128)(2,1)S(1)}, bf16[640,1536]{1,0:T(8,128)(2,1)S(1)}, bf16[640,1536]{1,0:T(8,128)(2,1)S(1)}) custom-call(s32[1]{0:T(128)} %bitcast.6.me_ref, bf16[256,640]{1,0:T(8,128)(2,1)S(1)} %get-tuple-element.36.low_ref, bf16[272,640]{1,0:T(8,128)(2,1)S(1)} %constant_dynamic-update-slice_fusion.high_ref, ...), custom_call_target="tpu_custom_call" | custom-call | flops 1038090240 | bytes 8000000 | tf_op jit(solution)/shard_map/project_own/pallas_call | solution.py:400
  77.9 3.2 %project_near.1.total_ref = f32[528,1536]{1,0:T(8,128)S(1)} custom-call(bf16[256,640]{1,0:T(8,128)(2,1)S(1)} %collective-permute-done.low1, bf16[272,640]{1,0:T(8,128)(2,1)S(1)} %collective-permute-done.5.high1, bf16[256,640]{1,0:T(8,128)(2,1)S(1)} %collective-permute-done.6.low3, bf16[272,640]{1,0:T(8,128)(2,1)S(1)} %collective-permute-done.3.high3, ...), custom_call_target="tpu_custom_call" | custom-call | flops 2076180480 | bytes 8000000 | tf_op jit(solution)/shard_map/project_near/pallas_call | solution.py:434
  81.2 3.5 %collective-permute-done.1.low_ref = bf16[256,640]{1,0:T(8,128)(2,1)S(1)} collective-permute-done((bf16[256,640]{1,0:T(8,128)(2,1)S(1)}, bf16[256,640]{1,0:T(8,128)(2,1)S(1)}, u32[]{:S(2)}, u32[]{:S(2)}) %collective-permute-start.1) | collective-permute-done | bytes 327712 | tf_op jit(solution)/shard_map/ppermute | solution.py:898
  85.1 7.4 %front.1 = (bf16[512,1280]{1,0:T(8,128)(2,1)}, bf16[144,1280]{1,0:T(8,128)(2,1)S(1)}, bf16[512,128]{1,0:T(8,128)(2,1)}, bf16[512,128]{1,0:T(8,128)(2,1)S(1)}) custom-call(bf16[256,640]{1,0:T(8,128)(2,1)S(1)} %collective-permute-done.1.low_ref, bf16[272,640]{1,0:T(8,128)(2,1)S(1)} %collective-permute-done.4.high_ref, f32[528,1536]{1,0:T(8,128)S(1)} %project_near.1.total_ref, ...), custom_call_target="tpu_custom_call" | custom-call | flops 1006632960 | bytes 12000000 | tf_op jit(solution)/shard_map/front/pallas_call | solution.py:517
  93.2 1.3 collective-permute-done.7.theirs_ref
  95.4 4.9 %all-to-all-start.1 = ((bf16[32,24,128]{2,1,0:T(8,128)(2,1)}), bf16[32,24,128]{2,1,0:T(8,128)(2,1)S(1)}, u32[]{:S(2)}, u32[]{:S(2)}) async-start(bf16[32,24,128]{2,1,0:T(8,128)(2,1)} %get-tuple-element.54), calls=%async_computation.1 | async-start | bytes 393216 | tf_op jit(solution)/shard_map/all_to_all | solution.py:932
  100.4 8.5 %inner_part.1.part_hbm = f32[512,1280]{1,0:T(8,128)} custom-call(s32[512,1]{1,0:T(8,128)S(1)} %add_subtract_fusion.rel_ref, f32[1,1280]{1,0:T(1,128)S(1)} %broadcast_in_dim_reshape.3.skip_ref, bf16[512,128]{1,0:T(8,128)(2,1)S(1)} %get-tuple-element.55.outmap_ref, bf16[256,128]{1,0:T(8,128)(2,1)} %get-tuple-element.40.low_hbm, ...), custom_call_target="tpu_custom_call" | custom-call | flops 1342177280 | bytes 8000000 | tf_op jit(solution)/shard_map/inner_part/pallas_call | solution.py:743
  110.4 8.5 %all-to-all-start.2 = ((bf16[32,24,128]{2,1,0:T(8,128)(2,1)}), bf16[32,24,128]{2,1,0:T(8,128)(2,1)S(1)}, u32[]{:S(2)}, u32[]{:S(2)}) async-start(bf16[32,24,128]{2,1,0:T(8,128)(2,1)} %scan_shards.1), calls=%async_computation.2 | async-start | bytes 393216 | tf_op jit(solution)/shard_map/all_to_all | solution.py:932
  118.9 3.7 %prepare.1.gain_ref = f32[512,1280]{1,0:T(8,128)S(1)} custom-call(s32[512,1]{1,0:T(8,128)S(1)} %add_subtract_fusion.rel_ref, bf16[256,128]{1,0:T(8,128)(2,1)} %get-tuple-element.40.low_hbm, bf16[256,128]{1,0:T(8,128)(2,1)} %get-tuple-element.41.high_hbm), custom_call_target="tpu_custom_call" | custom-call | flops 671088640 | bytes 8000000 | tf_op jit(solution)/shard_map/prepare/pallas_call | solution.py:827
  122.6 5.7 %all-to-all-done.2.recv_ref = bf16[32,24,128]{2,1,0:T(8,128)(2,1)S(1)} async-done(((bf16[32,24,128]{2,1,0:T(8,128)(2,1)}), bf16[32,24,128]{2,1,0:T(8,128)(2,1)S(1)}, u32[]{:S(2)}, u32[]{:S(2)}) %all-to-all-start.2) | async-done | bytes 196640 | tf_op jit(solution)/shard_map/all_to_all | solution.py:932
  128.4 2.9 %collective-permute-start.8 = (bf16[64,1280]{1,0:T(8,128)(2,1)S(1)}, bf16[64,1280]{1,0:T(8,128)(2,1)S(1)}, u32[]{:S(2)}, u32[]{:S(2)}) collective-permute-start(bf16[64,1280]{1,0:T(8,128)(2,1)S(1)} %get-tuple-element.64), channel_id=1, source_target_pairs={{0,4},{4,0},{8,12},{12,8},{16,20},{20,16},{24,28},{28,24},{32,36},... | collective-permute-start | bytes 491528 | tf_op jit(solution)/shard_map/ppermute | solution.py:949
  132.4 3.0 %final.1 = bf16[512,1280]{1,0:T(8,128)(2,1)} custom-call(s32[1]{0:T(128)} %bitcast.core_ref, bf16[64,1280]{1,0:T(8,128)(2,1)S(1)} %get-tuple-element.63.keep_ref, bf16[64,1280]{1,0:T(8,128)(2,1)S(1)} %collective-permute-done.8.got_ref, f32[512,1280]{1,0:T(8,128)S(1)} %prepare.1.gain_ref, bf16[512,128]{1,0:T(8,128)(2,1)S(1)} %get-tuple-element.55.outmap_ref, ...), custom_call_target="tpu_custom_call" | custom-call | flops 167772160 | bytes 7000000 | tf_op jit(solution)/shard_map/final/pallas_call | solution.py:870
  (37 shorter events, 6.1 us)
Async XLA Ops:
  3.5 13.2 %copy-start.4 = (s32[128]{0:T(128)S(1)}, s32[128]{0:T(128)}, u32[]{:S(2)}) copy-start(s32[128]{0:T(128)} %param.14) | copy-start | bytes 1540
  3.5 50.2 %all-to-all-start = ((bf16[64,88,128]{2,1,0:T(8,128)(2,1)}), bf16[64,88,128]{2,1,0:T(8,128)(2,1)S(1)}, u32[]{:S(2)}, u32[]{:S(2)}) async-start(bf16[64,88,128]{2,1,0:T(8,128)(2,1)} %pack.1), calls=%async_computation | async-start | bytes 2883584 | tf_op jit(solution)/shard_map/all_to_all | solution.py:894
  55.9 17.7 %copy-start.3 = (f32[1280]{0:T(1024)S(1)}, f32[1280]{0:T(1024)}, u32[]{:S(2)}) copy-start(f32[1280]{0:T(1024)} %param.19) | copy-start | bytes 15364
  55.9 4.7 %collective-permute-start.2 = (bf16[16,640]{1,0:T(8,128)(2,1)S(1)}, bf16[16,640]{1,0:T(8,128)(2,1)S(1)}, u32[]{:S(2)}, u32[]{:S(2)}) collective-permute-start(bf16[16,640]{1,0:T(8,128)(2,1)S(1)} %get-tuple-element.39), channel_id=1, source_target_pairs={{0,4},{4,8},{8,12},{12,16},{16,20},{20,24},{24,28},{28,32},{32,36}... | collective-permute-start | bytes 61448 | tf_op jit(solution)/shard_map/ppermute | solution.py:901
  59.3 14.3 %collective-permute-start = (bf16[256,640]{1,0:T(8,128)(2,1)S(1)}, bf16[256,640]{1,0:T(8,128)(2,1)S(1)}, u32[]{:S(2)}, u32[]{:S(2)}) collective-permute-start(bf16[256,640]{1,0:T(8,128)(2,1)S(1)} %get-tuple-element.36.low_ref), channel_id=1, source_target_pairs={{0,1},{1,2},{2,3},{3,0},{4,5},{5,6},{6,7},{7,4},{8,9},{9,10},{10,1... | collective-permute-start | bytes 983048 | tf_op jit(solution)/shard_map/ppermute | solution.py:898
  60.6 10.0 %collective-permute-start.3 = (bf16[272,640]{1,0:T(8,128)(2,1)S(1)}, bf16[272,640]{1,0:T(8,128)(2,1)S(1)}, u32[]{:S(2)}, u32[]{:S(2)}) collective-permute-start(bf16[272,640]{1,0:T(8,128)(2,1)S(1)} %constant_dynamic-update-slice_fusion.high_ref), channel_id=1, source_target_pairs={{0,3},{1,0},{2,1},{3,2},{4,7},{5,4},{6,5},{7,6},{8,11},{9,8},{10,9... | collective-permute-start | bytes 1044488 | tf_op jit(solution)/shard_map/ppermute | solution.py:898
  66.7 11.2 %collective-permute-start.5 = (bf16[272,640]{1,0:T(8,128)(2,1)S(1)}, bf16[272,640]{1,0:T(8,128)(2,1)S(1)}, u32[]{:S(2)}, u32[]{:S(2)}) collective-permute-start(bf16[272,640]{1,0:T(8,128)(2,1)S(1)} %constant_dynamic-update-slice_fusion.high_ref), channel_id=1, source_target_pairs={{0,1},{1,2},{2,3},{3,0},{4,5},{5,6},{6,7},{7,4},{8,9},{9,10},{10,1... | collective-permute-start | bytes 1044488 | tf_op jit(solution)/shard_map/ppermute | solution.py:898
  66.8 10.8 %collective-permute-start.6 = (bf16[256,640]{1,0:T(8,128)(2,1)S(1)}, bf16[256,640]{1,0:T(8,128)(2,1)S(1)}, u32[]{:S(2)}, u32[]{:S(2)}) collective-permute-start(bf16[256,640]{1,0:T(8,128)(2,1)S(1)} %get-tuple-element.36.low_ref), channel_id=1, source_target_pairs={{0,3},{1,0},{2,1},{3,2},{4,7},{5,4},{6,5},{7,6},{8,11},{9,8},{10,9... | collective-permute-start | bytes 983048 | tf_op jit(solution)/shard_map/ppermute | solution.py:898
  70.6 14.5 %collective-permute-start.4 = (bf16[272,640]{1,0:T(8,128)(2,1)S(1)}, bf16[272,640]{1,0:T(8,128)(2,1)S(1)}, u32[]{:S(2)}, u32[]{:S(2)}) collective-permute-start(bf16[272,640]{1,0:T(8,128)(2,1)S(1)} %collective-permute-done.3.high3), channel_id=1, source_target_pairs={{0,3},{1,0},{2,1},{3,2},{4,7},{5,4},{6,5},{7,6},{8,11},{9,8},{10,9... | collective-permute-start | bytes 1044488 | tf_op jit(solution)/shard_map/ppermute | solution.py:898
  73.6 11.1 %collective-permute-start.1 = (bf16[256,640]{1,0:T(8,128)(2,1)S(1)}, bf16[256,640]{1,0:T(8,128)(2,1)S(1)}, u32[]{:S(2)}, u32[]{:S(2)}) collective-permute-start(bf16[256,640]{1,0:T(8,128)(2,1)S(1)} %collective-permute-done.low1), channel_id=1, source_target_pairs={{0,1},{1,2},{2,3},{3,0},{4,5},{5,6},{6,7},{7,4},{8,9},{9,10},{10,1... | collective-permute-start | bytes 983048 | tf_op jit(solution)/shard_map/ppermute | solution.py:898
  77.9 7.1 %copy-start = (f32[4,1280]{1,0:T(4,128)S(1)}, f32[4,1280]{1,0:T(4,128)}, u32[]{:S(2)}) copy-start(f32[4,1280]{1,0:T(4,128)} %cx_ref.1) | copy-start | bytes 61444
  77.9 7.1 %copy-start.1 = (f32[4,256]{1,0:T(4,128)S(1)}, f32[4,256]{1,0:T(4,128)}, u32[]{:S(2)}) copy-start(f32[4,256]{1,0:T(4,128)} %cb_ref.1) | copy-start | bytes 12292
  77.9 7.1 %copy-start.2 = (f32[256]{0:T(256)S(1)}, f32[256]{0:T(256)}, u32[]{:S(2)}) copy-start(f32[256]{0:T(256)} %param.20) | copy-start | bytes 3076
  85.1 15.2 %copy-start.5 = (f32[20]{0:T(128)S(1)}, f32[20]{0:T(128)}, u32[]{:S(2)}) copy-start(f32[20]{0:T(128)} %param.21) | copy-start | bytes 244
  92.5 2.0 %collective-permute-start.7 = (bf16[144,1280]{1,0:T(8,128)(2,1)S(1)}, bf16[144,1280]{1,0:T(8,128)(2,1)S(1)}, u32[]{:S(2)}, u32[]{:S(2)}) collective-permute-start(bf16[144,1280]{1,0:T(8,128)(2,1)S(1)} %get-tuple-element.51.mine_ref), channel_id=1, source_target_pairs={{0,4},{4,0},{8,12},{12,8},{16,20},{20,16},{24,28},{28,24},{32,36},... | collective-permute-start | bytes 1105928 | tf_op jit(solution)/shard_map/ppermute | solution.py:936
  95.4 14.3 %all-to-all-start.1 = ((bf16[32,24,128]{2,1,0:T(8,128)(2,1)}), bf16[32,24,128]{2,1,0:T(8,128)(2,1)S(1)}, u32[]{:S(2)}, u32[]{:S(2)}) async-start(bf16[32,24,128]{2,1,0:T(8,128)(2,1)} %get-tuple-element.54), calls=%async_computation.1 | async-start | bytes 393216 | tf_op jit(solution)/shard_map/all_to_all | solution.py:932
  110.4 17.9 %all-to-all-start.2 = ((bf16[32,24,128]{2,1,0:T(8,128)(2,1)}), bf16[32,24,128]{2,1,0:T(8,128)(2,1)S(1)}, u32[]{:S(2)}, u32[]{:S(2)}) async-start(bf16[32,24,128]{2,1,0:T(8,128)(2,1)} %scan_shards.1), calls=%async_computation.2 | async-start | bytes 393216 | tf_op jit(solution)/shard_map/all_to_all | solution.py:932
  128.4 4.0 %collective-permute-start.8 = (bf16[64,1280]{1,0:T(8,128)(2,1)S(1)}, bf16[64,1280]{1,0:T(8,128)(2,1)S(1)}, u32[]{:S(2)}, u32[]{:S(2)}) collective-permute-start(bf16[64,1280]{1,0:T(8,128)(2,1)S(1)} %get-tuple-element.64), channel_id=1, source_target_pairs={{0,4},{4,0},{8,12},{12,8},{16,20},{20,16},{24,28},{28,24},{32,36},... | collective-permute-start | bytes 491528 | tf_op jit(solution)/shard_map/ppermute | solution.py:949

commit v8 on v7

--- a/solution.py
+++ b/solution.py
@@ -451,8 +451,8 @@
 def front_kernel(
     low_ref, high_ref, total_ref, w_ref, rel_ref, carry_ref, cx_ref, bx_ref, cb_ref, bb_ref,
     steps_hbm, tail_hbm,
-    conv_hbm, mine_ref, in_hbm, outmap_ref,
-    steps_ref, tail_ref, conv_ref, in_ref, across_ref,
+    conv_hbm, mine_ref, in_ref, outmap_ref,
+    steps_ref, tail_ref, conv_ref, across_ref,
     xe_ref, ext_ref, gets, puts,
 ):
     half, width = low_ref.shape
@@ -476,7 +476,6 @@
     both = conv_silu(ext_ref.at[tiles], cb_ref[...], bb_ref[...], rel, rows)
     in_ref[...] = both[:, :states]
     outmap_ref[...] = both[:, states:]
-    put_map = fetch(in_ref, in_hbm, puts.at[0])
     across_ref[...] = both[:, :states].astype(F32).T.astype(BF)
     for tile in range(tiles):
         columns = slice(tile * TILE, (tile + 1) * TILE)
@@ -501,7 +500,6 @@
         line = iota((HALO, TILE), 0)
         codes = jnp.where(line == 0, high, jnp.where(line == 1, reach - high, 0.0))
         mine_ref[states:, columns] = codes.astype(BF)
-    put_map.wait()
     for tile in range(tiles):
         pltpu.make_async_copy(
             conv_ref.at[tile], conv_hbm.at[:, pl.ds(tile * TILE, TILE)], puts.at[2 + tile]
@@ -517,18 +515,17 @@
     return pl.pallas_call(
         front_kernel,
         in_specs=vmem(10) + hbm(2),
-        out_specs=hbm(1) + vmem(1) + hbm(1) + vmem(1),
+        out_specs=hbm(1) + vmem(3),
         out_shape=[
             pltpu.HBM((rows, inner), BF),
             jax.ShapeDtypeStruct((states + HALO, inner), BF),
-            pltpu.HBM((rows, states), BF),
+            pltpu.VMEM((rows, states), BF),
             pltpu.VMEM((rows, states), BF),
         ],
         scratch_shapes=[
             pltpu.VMEM(steps.shape, BF),
             pltpu.VMEM(tail.shape, F32),
             pltpu.VMEM((tiles, rows, TILE), BF),
-            pltpu.VMEM((rows, states), BF),
             pltpu.VMEM((states, rows), BF),
             pltpu.VMEM((rows + HALO, width), BF),
             pltpu.VMEM((tiles + 1, rows + HALO, TILE), F32),
@@ -646,8 +643,8 @@
 
 
 def inner_kernel(
-    rel_ref, skip_ref, outmap_ref, low_hbm, high_hbm, in_hbm, conv_hbm, part_hbm,
-    small_ref, in_ref, conv_ref, part_ref,
+    rel_ref, skip_ref, outmap_ref, in_ref, low_hbm, high_hbm, conv_hbm, part_hbm,
+    small_ref, conv_ref, part_ref,
     scores_ref, across_ref, turned_ref, gets, puts,
 ):
     half = low_hbm.shape[0]
@@ -660,7 +657,6 @@
             (
                 (low_hbm, small_ref.at[pl.ds(0, half)]),
                 (high_hbm, small_ref.at[pl.ds(half, half)]),
-                (in_hbm, in_ref),
             )
         )
     ]
@@ -742,12 +738,11 @@
     tiles = inner // TILE
     return pl.pallas_call(
         inner_kernel,
-        in_specs=vmem(3) + hbm(4),
+        in_specs=vmem(4) + hbm(3),
         out_specs=hbm(1)[0],
         out_shape=pltpu.HBM((rows, inner), F32),
         scratch_shapes=[
             pltpu.VMEM((rows, LANES), BF),
-            pltpu.VMEM(input_map.shape, BF),
             pltpu.VMEM(conv.shape, BF),
             pltpu.VMEM((rows, inner), F32),
             pltpu.VMEM((blocks, BLK, BLK), F32),
@@ -758,7 +753,7 @@
         ],
         name="inner_part",
         **params(24, 8 * rows * BLK * inner, 8_000_000),
-    )(rel, skip_wide, near(output_map), *[far(x) for x in (*small, input_map, conv)])
+    )(rel, skip_wide, near(output_map), near(input_map), *[far(x) for x in (*small, conv)])
 
 
 def scan_kernel(lines, me_ref, recv_ref, out_ref):

time: 136 us -> 136 us (level)
  no operation moved by 1% of the time
where the time goes in v8:
time: 136 us; the launch traced here: 135 us
  waiting for transfers between devices  50.9 us (37%)
  starting transfers between devices  41.7 us (31%)
  Pallas kernels  41.4 us (30%)
    all_to_all x1, waiting for transfers between devices, on_device(): lax.all_to_all(sent, 'ctx', split_axis=0, concat_axis=0, tiled=True)  36.6 us
    all_to_all x2, starting transfers between devices, exchange(): lax.all_to_all(x, 'ctx', split_axis=0, concat_axis=0, tiled=True, axis_in...  13.3 us
    all_to_all x1, starting transfers between devices, on_device(): lax.all_to_all(sent, 'ctx', split_axis=0, concat_axis=0, tiled=True)  13.2 us
    ppermute x6, starting transfers between devices, turned(): return lax.ppermute(x, 'head', [(i, (i + by) % ring) for i in range(ring)])  8.73 us
    pallas_call x1, Pallas kernels, inner_part(): pl.pallas_call(inner_kernel, in_specs=vmem(4) + hbm(3), out_specs=hbm(1)[...  8.38 us
    pallas_call x1, Pallas kernels, front(): pl.pallas_call(front_kernel, in_specs=vmem(10) + hbm(2), out_specs=hbm(1)...  7.35 us
    all_to_all x2, waiting for transfers between devices, exchange(): lax.all_to_all(x, 'ctx', split_axis=0, concat_axis=0, tiled=True, axis_in...  6.56 us
    ppermute x6, waiting for transfers between devices, turned(): return lax.ppermute(x, 'head', [(i, (i + by) % ring) for i in range(ring)])  5.42 us
  transfers between devices with their start and end apart: 12, of which 10 were waited for; matrix products, arithmetic and copies ran while one was open for 1% of the time, Pallas kernels for 17%

profile of v8, /device:TPU:1, one launch (start us, length us, event | category | flops | bytes accessed | tf_op | source)
XLA Modules:
  0.0 135.4 jit_solution(8746933458481142415)
XLA Ops:
  0.0 3.4 %pack.1 = bf16[64,88,128]{2,1,0:T(8,128)(2,1)} custom-call(s32[1,512]{1,0:T(1,128)} %bitcast.12, bf16[20,2,512]{2,1,0:T(2,128)(2,1)} %bitcast.11, bf16[512,640]{1,0:T(8,128)(2,1)} %tok_hbm.1), custom_call_target="tpu_custom_call" | custom-call | flops 805306368 | bytes 1310720 | tf_op jit(solution)/shard_map/pack/pallas_call | solution.py:139
  3.5 13.2 %all-to-all-start = ((bf16[64,88,128]{2,1,0:T(8,128)(2,1)}), bf16[64,88,128]{2,1,0:T(8,128)(2,1)S(1)}, u32[]{:S(2)}, u32[]{:S(2)}) async-start(bf16[64,88,128]{2,1,0:T(8,128)(2,1)} %pack.1), calls=%async_computation | async-start | bytes 2883584 | tf_op jit(solution)/shard_map/all_to_all | solution.py:889
  17.1 36.6 %all-to-all-done.recv_ref = bf16[64,88,128]{2,1,0:T(8,128)(2,1)S(1)} async-done(((bf16[64,88,128]{2,1,0:T(8,128)(2,1)}), bf16[64,88,128]{2,1,0:T(8,128)(2,1)S(1)}, u32[]{:S(2)}, u32[]{:S(2)}) %all-to-all-start) | async-done | bytes 1441824 | tf_op jit(solution)/shard_map/all_to_all | solution.py:889
  53.6 1.2 unpack_low.1
  54.8 1.1 unpack_high.1
  55.9 3.0 %collective-permute-start.2 = (bf16[16,640]{1,0:T(8,128)(2,1)S(1)}, bf16[16,640]{1,0:T(8,128)(2,1)S(1)}, u32[]{:S(2)}, u32[]{:S(2)}) collective-permute-start(bf16[16,640]{1,0:T(8,128)(2,1)S(1)} %get-tuple-element.39), channel_id=1, source_target_pairs={{0,4},{4,8},{8,12},{12,16},{16,20},{20,24},{24,28},{28,32},{32,36}... | collective-permute-start | bytes 61448 | tf_op jit(solution)/shard_map/ppermute | solution.py:896
  59.3 1.3 collective-permute-start
  60.6 1.7 %collective-permute-start.3 = (bf16[272,640]{1,0:T(8,128)(2,1)S(1)}, bf16[272,640]{1,0:T(8,128)(2,1)S(1)}, u32[]{:S(2)}, u32[]{:S(2)}) collective-permute-start(bf16[272,640]{1,0:T(8,128)(2,1)S(1)} %constant_dynamic-update-slice_fusion.high_ref), channel_id=1, source_target_pairs={{0,3},{1,0},{2,1},{3,2},{4,7},{5,4},{6,5},{7,6},{8,11},{9,8},{10,9... | collective-permute-start | bytes 1044488 | tf_op jit(solution)/shard_map/ppermute | solution.py:893
  62.3 4.4 %decay_factors.1 = (bf16[5,512,256]{2,1,0:T(8,128)(2,1)}, f32[5,512,256]{2,1,0:T(8,128)}, f32[5,8,256]{2,1,0:T(8,128)S(1)}) custom-call(s32[512,1]{1,0:T(8,128)S(1)} %add_subtract_fusion.rel_ref, bf16[256,128]{1,0:T(8,128)(2,1)} %get-tuple-element.40.low_hbm, bf16[256,128]{1,0:T(8,128)(2,1)} %get-tuple-element.41.high_hbm), custom_call_target="tpu_custom_call" | custom-call | flops 671088640 | bytes 7000000 | tf_op jit(solution)/shard_map/decay_factors/pallas_call | solution.py:337
  66.8 2.7 %collective-permute-start.6 = (bf16[256,640]{1,0:T(8,128)(2,1)S(1)}, bf16[256,640]{1,0:T(8,128)(2,1)S(1)}, u32[]{:S(2)}, u32[]{:S(2)}) collective-permute-start(bf16[256,640]{1,0:T(8,128)(2,1)S(1)} %get-tuple-element.36.low_ref), channel_id=1, source_target_pairs={{0,3},{1,0},{2,1},{3,2},{4,7},{5,4},{6,5},{7,6},{8,11},{9,8},{10,9... | collective-permute-start | bytes 983048 | tf_op jit(solution)/shard_map/ppermute | solution.py:893
  69.5 1.1 collective-permute-done.3.high3
  70.6 3.0 %collective-permute-start.4 = (bf16[272,640]{1,0:T(8,128)(2,1)S(1)}, bf16[272,640]{1,0:T(8,128)(2,1)S(1)}, u32[]{:S(2)}, u32[]{:S(2)}) collective-permute-start(bf16[272,640]{1,0:T(8,128)(2,1)S(1)} %collective-permute-done.3.high3), channel_id=1, source_target_pairs={{0,3},{1,0},{2,1},{3,2},{4,7},{5,4},{6,5},{7,6},{8,11},{9,8},{10,9... | collective-permute-start | bytes 1044488 | tf_op jit(solution)/shard_map/ppermute | solution.py:893
  73.6 3.9 %project_own.1 = (f32[528,1536]{1,0:T(8,128)S(1)}, bf16[640,1536]{1,0:T(8,128)(2,1)S(1)}, bf16[640,1536]{1,0:T(8,128)(2,1)S(1)}, bf16[640,1536]{1,0:T(8,128)(2,1)S(1)}) custom-call(s32[1]{0:T(128)} %bitcast.6.me_ref, bf16[256,640]{1,0:T(8,128)(2,1)S(1)} %get-tuple-element.36.low_ref, bf16[272,640]{1,0:T(8,128)(2,1)S(1)} %constant_dynamic-update-slice_fusion.high_ref, ...), custom_call_target="tpu_custom_call" | custom-call | flops 1038090240 | bytes 8000000 | tf_op jit(solution)/shard_map/project_own/pallas_call | solution.py:400
  77.9 3.2 %project_near.1.total_ref = f32[528,1536]{1,0:T(8,128)S(1)} custom-call(bf16[256,640]{1,0:T(8,128)(2,1)S(1)} %collective-permute-done.low1, bf16[272,640]{1,0:T(8,128)(2,1)S(1)} %collective-permute-done.5.high1, bf16[256,640]{1,0:T(8,128)(2,1)S(1)} %collective-permute-done.6.low3, bf16[272,640]{1,0:T(8,128)(2,1)S(1)} %collective-permute-done.3.high3, ...), custom_call_target="tpu_custom_call" | custom-call | flops 2076180480 | bytes 8000000 | tf_op jit(solution)/shard_map/project_near/pallas_call | solution.py:434
  81.2 3.5 %collective-permute-done.1.low_ref = bf16[256,640]{1,0:T(8,128)(2,1)S(1)} collective-permute-done((bf16[256,640]{1,0:T(8,128)(2,1)S(1)}, bf16[256,640]{1,0:T(8,128)(2,1)S(1)}, u32[]{:S(2)}, u32[]{:S(2)}) %collective-permute-start.1) | collective-permute-done | bytes 327712 | tf_op jit(solution)/shard_map/ppermute | solution.py:893
  85.1 7.3 %front.1 = (bf16[512,1280]{1,0:T(8,128)(2,1)}, bf16[144,1280]{1,0:T(8,128)(2,1)S(1)}, bf16[512,128]{1,0:T(8,128)(2,1)S(1)}, bf16[512,128]{1,0:T(8,128)(2,1)S(1)}) custom-call(bf16[256,640]{1,0:T(8,128)(2,1)S(1)} %collective-permute-done.1.low_ref, bf16[272,640]{1,0:T(8,128)(2,1)S(1)} %collective-permute-done.4.high_ref, ...), custom_call_target="tpu_custom_call" | custom-call | flops 1006632960 | bytes 12000000 | tf_op jit(solution)/shard_map/front/pallas_call | solution.py:515
  93.1 1.3 collective-permute-done.7.theirs_ref
  95.3 4.9 %all-to-all-start.1 = ((bf16[32,24,128]{2,1,0:T(8,128)(2,1)}), bf16[32,24,128]{2,1,0:T(8,128)(2,1)S(1)}, u32[]{:S(2)}, u32[]{:S(2)}) async-start(bf16[32,24,128]{2,1,0:T(8,128)(2,1)} %get-tuple-element.54), calls=%async_computation.1 | async-start | bytes 393216 | tf_op jit(solution)/shard_map/all_to_all | solution.py:927
  100.3 8.4 %inner_part.1.part_hbm = f32[512,1280]{1,0:T(8,128)} custom-call(s32[512,1]{1,0:T(8,128)S(1)} %add_subtract_fusion.rel_ref, f32[1,1280]{1,0:T(1,128)S(1)} %broadcast_in_dim_reshape.3.skip_ref, bf16[512,128]{1,0:T(8,128)(2,1)S(1)} %get-tuple-element.55.outmap_ref, bf16[512,128]{1,0:T(8,128)(2,1)S(1)} %get-tuple-element.56.in_ref, ...), custom_call_target="tpu_custom_call" | custom-call | flops 1342177280 | bytes 8000000 | tf_op jit(solution)/shard_map/inner_part/pallas_call | solution.py:739
  110.4 8.4 %all-to-all-start.2 = ((bf16[32,24,128]{2,1,0:T(8,128)(2,1)}), bf16[32,24,128]{2,1,0:T(8,128)(2,1)S(1)}, u32[]{:S(2)}, u32[]{:S(2)}) async-start(bf16[32,24,128]{2,1,0:T(8,128)(2,1)} %scan_shards.1), calls=%async_computation.2 | async-start | bytes 393216 | tf_op jit(solution)/shard_map/all_to_all | solution.py:927
  118.8 3.7 %prepare.1.gain_ref = f32[512,1280]{1,0:T(8,128)S(1)} custom-call(s32[512,1]{1,0:T(8,128)S(1)} %add_subtract_fusion.rel_ref, bf16[256,128]{1,0:T(8,128)(2,1)} %get-tuple-element.40.low_hbm, bf16[256,128]{1,0:T(8,128)(2,1)} %get-tuple-element.41.high_hbm), custom_call_target="tpu_custom_call" | custom-call | flops 671088640 | bytes 8000000 | tf_op jit(solution)/shard_map/prepare/pallas_call | solution.py:822
  122.5 5.7 %all-to-all-done.2.recv_ref = bf16[32,24,128]{2,1,0:T(8,128)(2,1)S(1)} async-done(((bf16[32,24,128]{2,1,0:T(8,128)(2,1)}), bf16[32,24,128]{2,1,0:T(8,128)(2,1)S(1)}, u32[]{:S(2)}, u32[]{:S(2)}) %all-to-all-start.2) | async-done | bytes 196640 | tf_op jit(solution)/shard_map/all_to_all | solution.py:927
  128.3 2.9 %collective-permute-start.8 = (bf16[64,1280]{1,0:T(8,128)(2,1)S(1)}, bf16[64,1280]{1,0:T(8,128)(2,1)S(1)}, u32[]{:S(2)}, u32[]{:S(2)}) collective-permute-start(bf16[64,1280]{1,0:T(8,128)(2,1)S(1)} %get-tuple-element.64), channel_id=1, source_target_pairs={{0,4},{4,0},{8,12},{12,8},{16,20},{20,16},{24,28},{28,24},{32,36},... | collective-permute-start | bytes 491528 | tf_op jit(solution)/shard_map/ppermute | solution.py:944
  132.2 3.0 %final.1 = bf16[512,1280]{1,0:T(8,128)(2,1)} custom-call(s32[1]{0:T(128)} %bitcast.core_ref, bf16[64,1280]{1,0:T(8,128)(2,1)S(1)} %get-tuple-element.63.keep_ref, bf16[64,1280]{1,0:T(8,128)(2,1)S(1)} %collective-permute-done.8.got_ref, f32[512,1280]{1,0:T(8,128)S(1)} %prepare.1.gain_ref, bf16[512,128]{1,0:T(8,128)(2,1)S(1)} %get-tuple-element.55.outmap_ref, ...), custom_call_target="tpu_custom_call" | custom-call | flops 167772160 | bytes 7000000 | tf_op jit(solution)/shard_map/final/pallas_call | solution.py:865
  (37 shorter events, 6.2 us)
Async XLA Ops:
  3.5 13.2 %copy-start.4 = (s32[128]{0:T(128)S(1)}, s32[128]{0:T(128)}, u32[]{:S(2)}) copy-start(s32[128]{0:T(128)} %param.14) | copy-start | bytes 1540
  3.5 50.2 %all-to-all-start = ((bf16[64,88,128]{2,1,0:T(8,128)(2,1)}), bf16[64,88,128]{2,1,0:T(8,128)(2,1)S(1)}, u32[]{:S(2)}, u32[]{:S(2)}) async-start(bf16[64,88,128]{2,1,0:T(8,128)(2,1)} %pack.1), calls=%async_computation | async-start | bytes 2883584 | tf_op jit(solution)/shard_map/all_to_all | solution.py:889
  55.9 17.7 %copy-start.3 = (f32[1280]{0:T(1024)S(1)}, f32[1280]{0:T(1024)}, u32[]{:S(2)}) copy-start(f32[1280]{0:T(1024)} %param.19) | copy-start | bytes 15364
  55.9 4.7 %collective-permute-start.2 = (bf16[16,640]{1,0:T(8,128)(2,1)S(1)}, bf16[16,640]{1,0:T(8,128)(2,1)S(1)}, u32[]{:S(2)}, u32[]{:S(2)}) collective-permute-start(bf16[16,640]{1,0:T(8,128)(2,1)S(1)} %get-tuple-element.39), channel_id=1, source_target_pairs={{0,4},{4,8},{8,12},{12,16},{16,20},{20,24},{24,28},{28,32},{32,36}... | collective-permute-start | bytes 61448 | tf_op jit(solution)/shard_map/ppermute | solution.py:896
  59.3 14.3 %collective-permute-start = (bf16[256,640]{1,0:T(8,128)(2,1)S(1)}, bf16[256,640]{1,0:T(8,128)(2,1)S(1)}, u32[]{:S(2)}, u32[]{:S(2)}) collective-permute-start(bf16[256,640]{1,0:T(8,128)(2,1)S(1)} %get-tuple-element.36.low_ref), channel_id=1, source_target_pairs={{0,1},{1,2},{2,3},{3,0},{4,5},{5,6},{6,7},{7,4},{8,9},{9,10},{10,1... | collective-permute-start | bytes 983048 | tf_op jit(solution)/shard_map/ppermute | solution.py:893
  60.6 10.0 %collective-permute-start.3 = (bf16[272,640]{1,0:T(8,128)(2,1)S(1)}, bf16[272,640]{1,0:T(8,128)(2,1)S(1)}, u32[]{:S(2)}, u32[]{:S(2)}) collective-permute-start(bf16[272,640]{1,0:T(8,128)(2,1)S(1)} %constant_dynamic-update-slice_fusion.high_ref), channel_id=1, source_target_pairs={{0,3},{1,0},{2,1},{3,2},{4,7},{5,4},{6,5},{7,6},{8,11},{9,8},{10,9... | collective-permute-start | bytes 1044488 | tf_op jit(solution)/shard_map/ppermute | solution.py:893
  66.7 11.2 %collective-permute-start.5 = (bf16[272,640]{1,0:T(8,128)(2,1)S(1)}, bf16[272,640]{1,0:T(8,128)(2,1)S(1)}, u32[]{:S(2)}, u32[]{:S(2)}) collective-permute-start(bf16[272,640]{1,0:T(8,128)(2,1)S(1)} %constant_dynamic-update-slice_fusion.high_ref), channel_id=1, source_target_pairs={{0,1},{1,2},{2,3},{3,0},{4,5},{5,6},{6,7},{7,4},{8,9},{9,10},{10,1... | collective-permute-start | bytes 1044488 | tf_op jit(solution)/shard_map/ppermute | solution.py:893
  66.8 10.8 %collective-permute-start.6 = (bf16[256,640]{1,0:T(8,128)(2,1)S(1)}, bf16[256,640]{1,0:T(8,128)(2,1)S(1)}, u32[]{:S(2)}, u32[]{:S(2)}) collective-permute-start(bf16[256,640]{1,0:T(8,128)(2,1)S(1)} %get-tuple-element.36.low_ref), channel_id=1, source_target_pairs={{0,3},{1,0},{2,1},{3,2},{4,7},{5,4},{6,5},{7,6},{8,11},{9,8},{10,9... | collective-permute-start | bytes 983048 | tf_op jit(solution)/shard_map/ppermute | solution.py:893
  70.6 14.5 %collective-permute-start.4 = (bf16[272,640]{1,0:T(8,128)(2,1)S(1)}, bf16[272,640]{1,0:T(8,128)(2,1)S(1)}, u32[]{:S(2)}, u32[]{:S(2)}) collective-permute-start(bf16[272,640]{1,0:T(8,128)(2,1)S(1)} %collective-permute-done.3.high3), channel_id=1, source_target_pairs={{0,3},{1,0},{2,1},{3,2},{4,7},{5,4},{6,5},{7,6},{8,11},{9,8},{10,9... | collective-permute-start | bytes 1044488 | tf_op jit(solution)/shard_map/ppermute | solution.py:893
  73.6 11.1 %collective-permute-start.1 = (bf16[256,640]{1,0:T(8,128)(2,1)S(1)}, bf16[256,640]{1,0:T(8,128)(2,1)S(1)}, u32[]{:S(2)}, u32[]{:S(2)}) collective-permute-start(bf16[256,640]{1,0:T(8,128)(2,1)S(1)} %collective-permute-done.low1), channel_id=1, source_target_pairs={{0,1},{1,2},{2,3},{3,0},{4,5},{5,6},{6,7},{7,4},{8,9},{9,10},{10,1... | collective-permute-start | bytes 983048 | tf_op jit(solution)/shard_map/ppermute | solution.py:893
  77.9 7.1 %copy-start = (f32[4,1280]{1,0:T(4,128)S(1)}, f32[4,1280]{1,0:T(4,128)}, u32[]{:S(2)}) copy-start(f32[4,1280]{1,0:T(4,128)} %cx_ref.1) | copy-start | bytes 61444
  77.9 7.1 %copy-start.1 = (f32[4,256]{1,0:T(4,128)S(1)}, f32[4,256]{1,0:T(4,128)}, u32[]{:S(2)}) copy-start(f32[4,256]{1,0:T(4,128)} %cb_ref.1) | copy-start | bytes 12292
  77.9 7.1 %copy-start.2 = (f32[256]{0:T(256)S(1)}, f32[256]{0:T(256)}, u32[]{:S(2)}) copy-start(f32[256]{0:T(256)} %param.20) | copy-start | bytes 3076
  85.1 15.1 %copy-start.5 = (f32[20]{0:T(128)S(1)}, f32[20]{0:T(128)}, u32[]{:S(2)}) copy-start(f32[20]{0:T(128)} %param.21) | copy-start | bytes 244
  92.4 2.0 %collective-permute-start.7 = (bf16[144,1280]{1,0:T(8,128)(2,1)S(1)}, bf16[144,1280]{1,0:T(8,128)(2,1)S(1)}, u32[]{:S(2)}, u32[]{:S(2)}) collective-permute-start(bf16[144,1280]{1,0:T(8,128)(2,1)S(1)} %get-tuple-element.51.mine_ref), channel_id=1, source_target_pairs={{0,4},{4,0},{8,12},{12,8},{16,20},{20,16},{24,28},{28,24},{32,36},... | collective-permute-start | bytes 1105928 | tf_op jit(solution)/shard_map/ppermute | solution.py:931
  95.3 14.3 %all-to-all-start.1 = ((bf16[32,24,128]{2,1,0:T(8,128)(2,1)}), bf16[32,24,128]{2,1,0:T(8,128)(2,1)S(1)}, u32[]{:S(2)}, u32[]{:S(2)}) async-start(bf16[32,24,128]{2,1,0:T(8,128)(2,1)} %get-tuple-element.54), calls=%async_computation.1 | async-start | bytes 393216 | tf_op jit(solution)/shard_map/all_to_all | solution.py:927
  110.4 17.8 %all-to-all-start.2 = ((bf16[32,24,128]{2,1,0:T(8,128)(2,1)}), bf16[32,24,128]{2,1,0:T(8,128)(2,1)S(1)}, u32[]{:S(2)}, u32[]{:S(2)}) async-start(bf16[32,24,128]{2,1,0:T(8,128)(2,1)} %scan_shards.1), calls=%async_computation.2 | async-start | bytes 393216 | tf_op jit(solution)/shard_map/all_to_all | solution.py:927
  128.3 4.0 %collective-permute-start.8 = (bf16[64,1280]{1,0:T(8,128)(2,1)S(1)}, bf16[64,1280]{1,0:T(8,128)(2,1)S(1)}, u32[]{:S(2)}, u32[]{:S(2)}) collective-permute-start(bf16[64,1280]{1,0:T(8,128)(2,1)S(1)} %get-tuple-element.64), channel_id=1, source_target_pairs={{0,4},{4,0},{8,12},{12,8},{16,20},{20,16},{24,28},{28,24},{32,36},... | collective-permute-start | bytes 491528 | tf_op jit(solution)/shard_map/ppermute | solution.py:944
